TPU v7x, 128 devices: a whole 4x4x4 slice. The times are simulated.
128 devices in a mesh: feat: 8 (over x, core), dom: 16 (over y, z).
Axes of the slice: x: 4, y: 4, z: 4, core: 2. Of those that a mesh axis runs over, the one named last changes fastest.
Arguments:
- features: bfloat16 [768, 98304], P('feat', 'dom'), may hold values from -6 to 6
- adj_one: bfloat16 [768, 4, 128, 128], P('dom'), may hold values from -0.25 to 0.25
- src_one: int32 [768, 4], P('dom'), may hold values from 0 to 47
- w_self_one: bfloat16 [768, 1024], P('feat'), may hold values from -0.21875 to 0.21875
- w_neigh_one: bfloat16 [768, 1024], P('feat'), may hold values from -0.21875 to 0.21875
- bias_one: float32 [1024], replicated, may hold values from -4 to 4
- w_self_two: bfloat16 [1024, 1024], replicated, may hold values from -0.1875 to 0.1875
- w_neigh_two: bfloat16 [1024, 1024], replicated, may hold values from -0.1875 to 0.1875
- bias_two: float32 [1024], replicated, may hold values from -4 to 4
- seed_rows: int32 [16, 8, 512], P('dom', 'feat'), may hold values from 0 to 767
- adj_two: bfloat16 [16, 8, 4, 16, 128, 128], P('dom', 'feat'), may hold values from -0.125 to 0.125
- src_two: int32 [16, 8, 4, 16], P('dom', 'feat'), may hold values from 0 to 21
- send_tiles: int32 [16, 8, 4, 4], P('dom', 'feat'), may hold values from 0 to 5
- send_count: int32 [16, 8, 4], P('dom', 'feat'), may hold values from 1 to 4, as said below
- cotangent: bfloat16 [16, 4096, 1024], P('dom', 'feat'), may hold values from -6 to 6
Outputs:
- layer_two: bfloat16 [16, 4096, 1024], P('dom', 'feat')
- grad_hidden: float32 [16, 6144, 1024], P('dom', 'feat')
Inputs may be any that keep to these rules, and one draw needn't show every extreme that they name: `seed_rows`: rows of the device's own block of 768 hidden rows; they may repeat. `src_one`: tiles of the same partition. `src_two`: slots of the device's source table: its 6 local tiles, then 4 slots from each of the partitions at offsets -2, -1, +1, +2; a slot beyond the sender's live count holds zeros. `send_tiles`: local tiles of the sending device; they may repeat. `send_count`: uneven over devices and directions; some device has 4 in every direction.
All inputs are finite; a program needn't handle non-finite values.
Results may differ from a plain program's by a relative error of at most 0.018.
Values may be sent and summed in bfloat16 or wider, within the bound.
No kernel may reach another device: no remote copies, remote signals or barrier semaphores. Data moves between devices by JAX's collectives and lax.ppermute only.
A program may use at most 192 MiB of HBM per device.

v0:
```python
import jax
import jax.numpy as jnp
from jax import lax
from jax.sharding import PartitionSpec as P

OFFSETS = (-2, -1, 1, 2)


def shifted(shard, axis, by):
    count = lax.axis_size(axis)
    pairs = [(i, i + by) for i in range(count) if 0 <= i + by < count]
    return lax.ppermute(shard, axis, pairs)


def shards(
    features,
    adj_one,
    src_one,
    w_self_one,
    w_neigh_one,
    bias_one,
    w_self_two,
    w_neigh_two,
    bias_two,
    seed_rows,
    adj_two,
    src_two,
    send_tiles,
    send_count,
    cotangent,
):
    slice_width = features.shape[0]
    part_tiles = adj_one.shape[0]
    tile_rows = adj_one.shape[2]
    hid_width = w_self_two.shape[0]
    feat_count = lax.axis_size("feat")
    row_dev = features.shape[1] // feat_count
    tile_dev = row_dev // tile_rows
    halo_slots = send_tiles.shape[3]
    table_width = tile_dev + 4 * halo_slots
    tiled = features.reshape(slice_width, part_tiles, tile_rows)
    picked = tiled[:, src_one]
    gathered_one = jnp.einsum("ftkj,tkij->fti", picked, adj_one, preferred_element_type=jnp.float32)
    gathered_one = gathered_one.astype(jnp.bfloat16).reshape(slice_width, part_tiles * tile_rows)
    own_term = lax.dot_general(
        features, w_self_one, (((0,), (0,)), ((), ())), preferred_element_type=jnp.float32
    )
    near_term = lax.dot_general(
        gathered_one, w_neigh_one, (((0,), (0,)), ((), ())), preferred_element_type=jnp.float32
    )
    pre_hidden = lax.psum_scatter(
        (own_term + near_term).astype(jnp.bfloat16), "feat", scatter_dimension=0, tiled=True
    ).astype(jnp.float32)
    hidden = jax.nn.relu(pre_hidden + bias_one).astype(jnp.bfloat16)
    local_tiles = hidden.reshape(tile_dev, tile_rows, hid_width)
    send_list = send_tiles[0, 0]
    live_slots = jnp.arange(halo_slots, dtype=jnp.int32)[None, :] < send_count[0, 0][:, None]
    outgoing = jnp.where(
        live_slots[:, :, None, None], local_tiles[send_list], jnp.zeros((), jnp.bfloat16)
    )
    blocks = adj_two[0, 0]
    sources = src_two[0, 0]
    chosen_rows = seed_rows[0, 0]
    seed_tiles = blocks.shape[0]
    onehot = (
        sources[:, :, None] == jnp.arange(table_width, dtype=jnp.int32)[None, None, :]
    ).astype(jnp.bfloat16)
    folded = jnp.einsum("sku,skij->siuj", onehot, blocks, preferred_element_type=jnp.float32)
    folded = folded.astype(jnp.bfloat16).reshape(seed_tiles * tile_rows, table_width * tile_rows)
    received = [None, None, None, None]
    for slot_index in range(4):
        received[slot_index] = shifted(outgoing[slot_index], "dom", OFFSETS[slot_index])
    source_table = jnp.concatenate([local_tiles] + received, axis=0)
    gathered_two = jnp.dot(
        folded,
        source_table.reshape(table_width * tile_rows, hid_width),
        preferred_element_type=jnp.float32,
    )
    gathered_two = gathered_two.astype(jnp.bfloat16)
    chosen = hidden[chosen_rows]
    output = jnp.dot(chosen, w_self_two, preferred_element_type=jnp.float32)
    output = (
        output + jnp.dot(gathered_two, w_neigh_two, preferred_element_type=jnp.float32) + bias_two
    )
    layer_out = output.astype(jnp.bfloat16)[None]
    upstream = cotangent[0]
    back_self = lax.dot_general(
        upstream, w_self_two, (((1,), (1,)), ((), ())), preferred_element_type=jnp.float32
    )
    back_neigh = lax.dot_general(
        upstream, w_neigh_two, (((1,), (1,)), ((), ())), preferred_element_type=jnp.float32
    )
    back_neigh = back_neigh.astype(jnp.bfloat16)
    table_grad = lax.dot_general(
        folded, back_neigh, (((0,), (0,)), ((), ())), preferred_element_type=jnp.float32
    )
    table_grad = table_grad.reshape(table_width, tile_rows, hid_width)
    local_grad = table_grad[:tile_dev].reshape(row_dev, hid_width)
    local_grad = local_grad + jnp.zeros((row_dev, hid_width), jnp.float32).at[chosen_rows].add(
        back_self
    )
    halo_grads = table_grad[tile_dev:].reshape(4, halo_slots, tile_rows, hid_width)
    returned = [None, None, None, None]
    for slot_index in range(4):
        returned[slot_index] = shifted(
            halo_grads[slot_index].astype(jnp.bfloat16), "dom", -OFFSETS[slot_index]
        ).astype(jnp.float32)
    returned_all = jnp.stack(returned)
    returned_all = jnp.where(live_slots[:, :, None, None], returned_all, jnp.zeros((), jnp.float32))
    grad_tiles = local_grad.reshape(tile_dev, tile_rows, hid_width)
    grad_tiles = grad_tiles.at[send_list.reshape(-1)].add(
        returned_all.reshape(-1, tile_rows, hid_width)
    )
    return (layer_out, grad_tiles.reshape(1, row_dev, hid_width))


def solution(mesh):
    return jax.shard_map(
        shards,
        mesh=mesh,
        in_specs=(
            P("feat", "dom"),
            P("dom", None, None, None),
            P("dom", None),
            P("feat", None),
            P("feat", None),
            P(),
            P(),
            P(),
            P(),
            P("dom", "feat", None),
            P("dom", "feat", None, None, None, None),
            P("dom", "feat", None, None),
            P("dom", "feat", None, None),
            P("dom", "feat", None),
            P("dom", "feat", None),
        ),
        out_specs=(P("dom", "feat", None), P("dom", "feat", None)),
        check_vma=False,
    )
```

profile of v0, /device:TPU:104, one launch (start us, length us, event | category | flops | bytes accessed | tf_op | source)
XLA Modules:
  0.0 291.3 jit_solution(18240173714589766021)
XLA Ops:
  7.2 0.0 copy-start
  7.2 0.0 reduce-scatter.2.cloned.1.call-start
  7.2 0.0 copy-start.2
  7.2 1.6 copy_bitcast_fusion
  8.9 0.1 copy-done.2
  9.0 11.0 %fusion.29 = f32[6144,1024]{1,0:T(8,128)} fusion(bf16[96,6144]{1,0:T(8,128)(2,1)S(1)} %copy-done.2, bf16[96,1024]{1,0:T(8,128)(2,1)} %param.18), kind=kOutput, calls=%fused_computation.53 | convolution fusion | flops 1207959552 | bytes 26542080 | tf_op jit(solution)/shard_map/dot_general | solution.py:45
  20.0 0.0 copy-done.8
  20.0 0.1 copy.23
  20.1 0.1 reshape.173
  20.2 3.5 %gather_fusion = bf16[192,96,128]{2,1,0:T(8,128)(2,1)} fusion(bf16[96,48,128]{2,0,1:T(8,128)(2,1)S(1)} %copy_bitcast_fusion, s32[1024]{0:T(1024)S(1)} %pad_clamp_fusion.2), kind=kCustom, calls=%fused_computation | custom fusion | bytes 9437952 | tf_op jit(solution)/shard_map/gather | solution.py:42
  23.8 6.4 %fusion.10 = bf16[48,12,8,128]{3,2,1,0:T(8,128)(2,1)S(1)} fusion(bf16[96,48,4,128]{3,0,2,1:T(8,128)(2,1)} %bitcast.102, bf16[48,4,128,128]{3,2,1,0:T(8,128)(2,1)} %param.16), kind=kOutput, calls=%fused_computation.22 | convolution fusion | flops 604569600 | bytes 12189696 | tf_op jit(solution)/shard_map/ftkj,tkij->fti/dot_general | solution.py:43
  30.1 0.0 copy-done.4
  30.1 14.6 %add_convert_fusion = bf16[6144,1024]{1,0:T(8,128)(2,1)} fusion(f32[6144,1024]{1,0:T(8,128)} %fusion.29, bf16[96,1024]{1,0:T(8,128)(2,1)S(1)} %copy-done.4, bf16[48,12,8,128]{3,2,1,0:T(8,128)(2,1)S(1)} %fusion.10), kind=kOutput, calls=%fused_computation.5 | convolution fusion | flops 1220542464 | bytes 39124992 | tf_op jit(solution)/shard_map/dot_general | solution.py:48
  44.7 0.0 reduce-scatter.2.cloned.1.call-update
  44.7 0.0 copy-start.3
  44.7 0.6 copy-done.7
  45.4 4.9 %convolution_convert_fusion = bf16[4,22,128,128]{3,1,2,0:T(8,128)(2,1)} fusion(bf16[4,16,128,128]{3,2,1,0:T(8,128)(2,1)} %bitcast.104, s32[4,16]{1,0:T(4,128)S(1)} %bitcast.107), kind=kOutput, calls=%fused_computation.17 | convolution fusion | flops 47580544 | bytes 4980992 | tf_op jit(solution)/shard_map/sku,skij->siuj/dot_general | solution.py:68
  50.3 0.0 copy-done
  50.3 0.0 copy-done.3
  50.3 10.3 %fusion.26 = (bf16[2816,1024]{1,0:T(8,128)(2,1)}, f32[2816,1024]{1,0:T(8,128)}) fusion(bf16[1024,1024]{1,0:T(8,128)(2,1)S(1)} %copy-done, bf16[1,512,1024]{2,1,0:T(8,128)(2,1)S(1)} %copy-done.3, bf16[64,8,22,128]{3,2,1,0:T(8,128)(2,1)} %bitcast.100), kind=kOutput, calls=%fused_computation.52 | convolution fusion | flops 4029939712 | bytes 23330816 | tf_op jit(solution)/shard_map/dot_general | solution.py:94
  60.5 4.4 %fusion.25 = (bf16[512,1024]{1,0:T(8,128)(2,1)}, bf16[512,1024]{1,0:T(8,128)(2,1)}, bf16[512,1024]{1,0:T(8,128)(2,1)}, bf16[512,1024]{1,0:T(8,128)(2,1)}) fusion(bf16[2816,1024]{1,0:T(8,128)(2,1)} %get-tuple-element.10), kind=kLoop, calls=%fused_computation.51 | loop fusion | bytes 8388608 | tf_op jit(solution)/shard_map/slice | solution.py:106
  64.9 4.0 %collective-permute-start.4 = (bf16[4,128,1024]{2,1,0:T(8,128)(2,1)}, bf16[4,128,1024]{2,1,0:T(8,128)(2,1)}, u32[]{:S(2)}, u32[]{:S(2)}) collective-permute-start(bf16[4,128,1024]{2,1,0:T(8,128)(2,1)} %bitcast.25), channel_id=1, source_target_pairs={{0,2},{1,3},{2,4},{3,5},{4,6},{5,7},{6,8},{7,9},{8,10},{9,11},{10,... | collective-permute-start | bytes 3145736 | tf_op jit(solution)/shard_map/ppermute | solution.py:12
  68.9 4.2 %collective-permute-start.5 = (bf16[4,128,1024]{2,1,0:T(8,128)(2,1)}, bf16[4,128,1024]{2,1,0:T(8,128)(2,1)}, u32[]{:S(2)}, u32[]{:S(2)}) collective-permute-start(bf16[4,128,1024]{2,1,0:T(8,128)(2,1)} %bitcast.27), channel_id=1, source_target_pairs={{0,1},{1,2},{2,3},{3,4},{4,5},{5,6},{6,7},{7,8},{8,9},{9,10},{10,1... | collective-permute-start | bytes 3145736 | tf_op jit(solution)/shard_map/ppermute | solution.py:12
  73.1 1.9 collective-permute-start.6
  75.0 3.3 %collective-permute-start.7 = (bf16[4,128,1024]{2,1,0:T(8,128)(2,1)}, bf16[4,128,1024]{2,1,0:T(8,128)(2,1)}, u32[]{:S(2)}, u32[]{:S(2)}) collective-permute-start(bf16[4,128,1024]{2,1,0:T(8,128)(2,1)} %bitcast.31), channel_id=1, source_target_pairs={{2,0},{3,1},{4,2},{5,3},{6,4},{7,5},{8,6},{9,7},{10,8},{11,9},{12,... | collective-permute-start | bytes 3145736 | tf_op jit(solution)/shard_map/ppermute | solution.py:12
  78.3 0.0 copy-done.5
  78.3 0.1 reshape_squeeze.3
  78.4 0.1 reshape.189
  78.5 0.0 copy-done.13
  78.5 0.1 iota_compare_fusion.1
  78.6 0.1 lt.69
  78.7 4.2 %slice.61 = f32[768,1024]{1,0:T(8,128)} slice(f32[2816,1024]{1,0:T(8,128)} %get-tuple-element.11), slice={[0:768], [0:1024]} | slice | bytes 6291456 | tf_op jit(solution)/shard_map/slice | solution.py:98
  82.9 2.7 fusion.14
  85.5 9.3 %scatter_fusion = f32[768,1024]{1,0:T(8,128)} fusion(f32[768,1024]{1,0:T(8,128)} %slice.61, s32[512]{0:T(512)S(1)} %bitcast.105, f32[512,1024]{1,0:T(8,128)} %fusion.14), kind=kCustom, calls=%fused_computation.3 | custom fusion | flops 524288 | bytes 6293504 | tf_op jit(solution)/shard_map/scatter-add | solution.py:99
  94.9 44.6 %collective-permute-done.4 = bf16[4,128,1024]{2,1,0:T(8,128)(2,1)} collective-permute-done((bf16[4,128,1024]{2,1,0:T(8,128)(2,1)}, bf16[4,128,1024]{2,1,0:T(8,128)(2,1)}, u32[]{:S(2)}, u32[]{:S(2)}) %collective-permute-start.4) | collective-permute-done | bytes 1048608 | tf_op jit(solution)/shard_map/ppermute | solution.py:12
  139.5 0.0 collective-permute-done.5
  139.5 0.0 collective-permute-done.6
  139.5 0.0 collective-permute-done.7
  139.5 0.0 copy-start.6
  139.5 3.7 %pad_maximum_fusion = bf16[4,4,128,1024]{3,2,1,0:T(8,128)(2,1)} fusion(bf16[1,4,128,1024]{3,2,1,0:T(8,128)(2,1)} %bitcast.32, bf16[1,4,128,1024]{3,2,1,0:T(8,128)(2,1)} %bitcast.30, bf16[1,4,128,1024]{3,2,1,0:T(8,128)(2,1)} %bitcast.28, bf16[1,4,128,1024]{3,2,1,0:T(8,128)(2,1)} %bitcast.26), kind=kLoop, calls=%fused_computation.7 | loop fusion | flops 6291456 | bytes 8388608 | tf_op jit(solution)/shard_map/stack | solution.py:108
  143.3 3.0 %maximum_convert_fusion = bf16[768,1024]{1,0:T(8,128)(2,1)} fusion(bf16[768,1024]{1,0:T(8,128)(2,1)} %reduce-scatter.2.cloned.1.call-done, f32[1024]{0:T(1024)S(1)} %copy-done.6), kind=kLoop, calls=%fused_computation.9 | loop fusion | flops 3145728 | bytes 3149824 | tf_op jit(solution)/shard_map/convert_element_type | solution.py:54
  146.3 4.2 %gather_fusion.2 = bf16[16,128,1024]{2,1,0:T(8,128)(2,1)} fusion(bf16[6,128,1024]{2,1,0:T(8,128)(2,1)} %bitcast.98, s32[1024]{0:T(1024)S(1)} %get-tuple-element.12), kind=kCustom, calls=%fused_computation.2 | custom fusion | bytes 8388672 | tf_op jit(solution)/shard_map/gather | solution.py:59
  150.5 2.5 broadcast_select_fusion
  153.0 2.2 slice_bitcast_fusion
  155.2 23.3 %collective-permute-start = (bf16[4,128,1024]{2,1,0:T(8,128)(2,1)}, bf16[4,128,1024]{2,1,0:T(8,128)(2,1)}, u32[]{:S(2)}, u32[]{:S(2)}) collective-permute-start(bf16[4,128,1024]{2,1,0:T(8,128)(2,1)} %get-tuple-element.9), channel_id=1, source_target_pairs={{2,0},{3,1},{4,2},{5,3},{6,4},{7,5},{8,6},{9,7},{10,8},{11,9},{12,... | collective-permute-start | bytes 3145736 | tf_op jit(solution)/shard_map/ppermute | solution.py:12
  178.5 3.8 %collective-permute-start.1 = (bf16[4,128,1024]{2,1,0:T(8,128)(2,1)}, bf16[4,128,1024]{2,1,0:T(8,128)(2,1)}, u32[]{:S(2)}, u32[]{:S(2)}) collective-permute-start(bf16[4,128,1024]{2,1,0:T(8,128)(2,1)} %get-tuple-element.8), channel_id=1, source_target_pairs={{1,0},{2,1},{3,2},{4,3},{5,4},{6,5},{7,6},{8,7},{9,8},{10,9},{11,1... | collective-permute-start | bytes 3145736 | tf_op jit(solution)/shard_map/ppermute | solution.py:12
  182.3 24.5 %collective-permute-start.2 = (bf16[4,128,1024]{2,1,0:T(8,128)(2,1)}, bf16[4,128,1024]{2,1,0:T(8,128)(2,1)}, u32[]{:S(2)}, u32[]{:S(2)}) collective-permute-start(bf16[4,128,1024]{2,1,0:T(8,128)(2,1)} %get-tuple-element.7), channel_id=1, source_target_pairs={{0,1},{1,2},{2,3},{3,4},{4,5},{5,6},{6,7},{7,8},{8,9},{9,10},{10,1... | collective-permute-start | bytes 3145736 | tf_op jit(solution)/shard_map/ppermute | solution.py:12
  206.8 5.0 %collective-permute-start.3 = (bf16[4,128,1024]{2,1,0:T(8,128)(2,1)}, bf16[4,128,1024]{2,1,0:T(8,128)(2,1)}, u32[]{:S(2)}, u32[]{:S(2)}) collective-permute-start(bf16[4,128,1024]{2,1,0:T(8,128)(2,1)} %get-tuple-element.6), channel_id=1, source_target_pairs={{0,2},{1,3},{2,4},{3,5},{4,6},{5,7},{6,8},{7,9},{8,10},{9,11},{10,... | collective-permute-start | bytes 3145736 | tf_op jit(solution)/shard_map/ppermute | solution.py:12
  211.9 4.7 %convert_select_fusion = f32[16,128,1024]{2,1,0:T(8,128)} fusion(bf16[4,4,128,1024]{3,2,1,0:T(8,128)(2,1)S(1)} %copy-done.1, pred[16]{0:T(512)(128)(4,1)S(1)} %lt.69), kind=kLoop, calls=%fused_computation.6 | loop fusion | flops 4194304 | bytes 12582928 | tf_op jit(solution)/shard_map/jit(_where)/select_n | solution.py:109
  216.6 17.5 %scatter_fusion.1 = f32[6,128,1024]{2,1,0:T(8,128)} fusion(f32[6,128,1024]{2,1,0:T(8,128)} %bitcast.96, s32[16]{0:T(128)S(1)} %fusion.24, f32[16,128,1024]{2,1,0:T(8,128)} %convert_select_fusion), kind=kCustom, calls=%fused_computation.4 | custom fusion | flops 2097152 | bytes 25165888 | tf_op jit(solution)/shard_map/scatter-add | solution.py:111
  234.1 4.3 %gather_fusion.1 = bf16[512,1024]{1,0:T(8,128)(2,1)S(1)} fusion(bf16[768,1024]{1,0:T(8,128)(2,1)} %maximum_convert_fusion, s32[1024]{0:T(1024)S(1)} %get-tuple-element.13), kind=kCustom, calls=%fused_computation.1 | custom fusion | bytes 2099200 | tf_op jit(solution)/shard_map/gather | solution.py:80
  238.4 0.0 copy-start.11
  238.5 2.9 %constant_dynamic-update-slice_fusion.4 = bf16[22,128,1024]{2,1,0:T(8,128)(2,1)} fusion(bf16[6,128,1024]{2,1,0:T(8,128)(2,1)} %bitcast.99), kind=kLoop, calls=%fused_computation.42 | loop fusion | bytes 3145728
  241.4 2.6 fusion.30
  244.0 0.0 collective-permute-done
  244.0 2.3 constant_dynamic-update-slice_fusion.3
  246.3 0.0 collective-permute-done.1
  246.3 2.3 constant_dynamic-update-slice_fusion.2
  248.5 21.9 %collective-permute-done.2 = bf16[4,128,1024]{2,1,0:T(8,128)(2,1)} collective-permute-done((bf16[4,128,1024]{2,1,0:T(8,128)(2,1)}, bf16[4,128,1024]{2,1,0:T(8,128)(2,1)}, u32[]{:S(2)}, u32[]{:S(2)}) %collective-permute-start.2) | collective-permute-done | bytes 1048608 | tf_op jit(solution)/shard_map/ppermute | solution.py:12
  270.5 2.3 constant_dynamic-update-slice_fusion.1
  272.7 0.0 collective-permute-done.3
  272.7 2.3 constant_dynamic-update-slice_fusion
  275.0 0.0 copy-done.12
  275.0 9.4 %fusion.11 = bf16[1,512,1024]{2,1,0:T(8,128)(2,1)} fusion(f32[512,1024]{1,0:T(8,128)} %fusion.30, bf16[1024,1024]{1,0:T(8,128)(2,1)S(1)} %copy-done, f32[1024]{0:T(1024)S(1)} %copy-done.12, bf16[2816,1024]{1,0:T(8,128)(2,1)} %bitcast.20, bf16[64,8,22,128]{3,2,1,0:T(8,128)(2,1)} %bitcast.101), kind=kOutput, calls=%fused_computation.23 | convolution fusion | flops 4028628992 | bytes 13897728 | tf_op jit(solution)/shard_map/dot_general | solution.py:83
  (21 shorter events, 0.1 us)
Async XLA Ops:
  7.2 43.1 %copy-start = (bf16[1024,1024]{1,0:T(8,128)(2,1)S(1)}, bf16[1024,1024]{1,0:T(8,128)(2,1)}, u32[]{:S(2)}) copy-start(bf16[1024,1024]{1,0:T(8,128)(2,1)} %param.22) | copy-start | bytes 6291460
  7.2 136.1 %reduce-scatter.2.cloned.1.call-start = ((), (), s32[]{:S(2)}) async-start(), calls=%async_computation.1 | async-start | bytes 14155776 | tf_op jit(solution)/shard_map/reduce_scatter | solution.py:51
  7.2 1.8 copy-start.2
  9.0 11.0 %copy-start.8 = (s32[48,4]{0,1:T(4,128)S(1)}, s32[48,4]{0,1:T(4,128)}, u32[]{:S(2)}) copy-start(s32[48,4]{0,1:T(4,128)} %param.17) | copy-start | bytes 2308
  23.8 6.4 %copy-start.4 = (bf16[96,1024]{1,0:T(8,128)(2,1)S(1)}, bf16[96,1024]{1,0:T(8,128)(2,1)}, u32[]{:S(2)}) copy-start(bf16[96,1024]{1,0:T(8,128)(2,1)} %param.19) | copy-start | bytes 589828
  44.7 0.7 copy-start.7
  44.7 5.5 %copy-start.3 = (bf16[1,512,1024]{2,1,0:T(8,128)(2,1)S(1)}, bf16[1,512,1024]{2,1,0:T(8,128)(2,1)}, u32[]{:S(2)}) copy-start(bf16[1,512,1024]{2,1,0:T(8,128)(2,1)} %param.29) | copy-start | bytes 3145732
  60.5 17.8 %copy-start.5 = (s32[1,1,4,4]{3,2,1,0:T(4,128)S(1)}, s32[1,1,4,4]{3,2,1,0:T(4,128)}, u32[]{:S(2)}) copy-start(s32[1,1,4,4]{3,2,1,0:T(4,128)} %param.27) | copy-start | bytes 196
  60.5 18.0 %copy-start.13 = (s32[1,1,4]{2,1,0:T(1,128)S(1)}, s32[1,1,4]{2,1,0:T(1,128)}, u32[]{:S(2)}) copy-start(s32[1,1,4]{2,1,0:T(1,128)} %param.28) | copy-start | bytes 52
  64.9 74.6 %collective-permute-start.4 = (bf16[4,128,1024]{2,1,0:T(8,128)(2,1)}, bf16[4,128,1024]{2,1,0:T(8,128)(2,1)}, u32[]{:S(2)}, u32[]{:S(2)}) collective-permute-start(bf16[4,128,1024]{2,1,0:T(8,128)(2,1)} %bitcast.25), channel_id=1, source_target_pairs={{0,2},{1,3},{2,4},{3,5},{4,6},{5,7},{6,8},{7,9},{8,10},{9,11},{10,... | collective-permute-start | bytes 3145736 | tf_op jit(solution)/shard_map/ppermute | solution.py:12
  68.9 70.6 %collective-permute-start.5 = (bf16[4,128,1024]{2,1,0:T(8,128)(2,1)}, bf16[4,128,1024]{2,1,0:T(8,128)(2,1)}, u32[]{:S(2)}, u32[]{:S(2)}) collective-permute-start(bf16[4,128,1024]{2,1,0:T(8,128)(2,1)} %bitcast.27), channel_id=1, source_target_pairs={{0,1},{1,2},{2,3},{3,4},{4,5},{5,6},{6,7},{7,8},{8,9},{9,10},{10,1... | collective-permute-start | bytes 3145736 | tf_op jit(solution)/shard_map/ppermute | solution.py:12
  73.1 66.4 %collective-permute-start.6 = (bf16[4,128,1024]{2,1,0:T(8,128)(2,1)}, bf16[4,128,1024]{2,1,0:T(8,128)(2,1)}, u32[]{:S(2)}, u32[]{:S(2)}) collective-permute-start(bf16[4,128,1024]{2,1,0:T(8,128)(2,1)} %bitcast.29), channel_id=1, source_target_pairs={{1,0},{2,1},{3,2},{4,3},{5,4},{6,5},{7,6},{8,7},{9,8},{10,9},{11,1... | collective-permute-start | bytes 3145736 | tf_op jit(solution)/shard_map/ppermute | solution.py:12
  75.0 64.5 %collective-permute-start.7 = (bf16[4,128,1024]{2,1,0:T(8,128)(2,1)}, bf16[4,128,1024]{2,1,0:T(8,128)(2,1)}, u32[]{:S(2)}, u32[]{:S(2)}) collective-permute-start(bf16[4,128,1024]{2,1,0:T(8,128)(2,1)} %bitcast.31), channel_id=1, source_target_pairs={{2,0},{3,1},{4,2},{5,3},{6,4},{7,5},{8,6},{9,7},{10,8},{11,9},{12,... | collective-permute-start | bytes 3145736 | tf_op jit(solution)/shard_map/ppermute | solution.py:12
  78.7 4.2 %copy-start.9 = (s32[1,1,512]{2,1,0:T(1,128)S(1)}, s32[1,1,512]{2,1,0:T(1,128)}, u32[]{:S(2)}) copy-start(s32[1,1,512]{2,1,0:T(1,128)} %param.24) | copy-start | bytes 6148
  78.7 4.2 %copy-start.10 = (bf16[1024,1024]{1,0:T(8,128)(2,1)S(1)}, bf16[1024,1024]{1,0:T(8,128)(2,1)}, u32[]{:S(2)}) copy-start(bf16[1024,1024]{1,0:T(8,128)(2,1)} %param.21) | copy-start | bytes 6291460
  139.5 3.7 %copy-start.6 = (f32[1024]{0:T(1024)S(1)}, f32[1024]{0:T(1024)}, u32[]{:S(2)}) copy-start(f32[1024]{0:T(1024)} %param.20) | copy-start | bytes 12292
  153.0 58.9 %copy-start.1 = (bf16[4,4,128,1024]{3,2,1,0:T(8,128)(2,1)S(1)}, bf16[4,4,128,1024]{3,2,1,0:T(8,128)(2,1)}, u32[]{:S(2)}) copy-start(bf16[4,4,128,1024]{3,2,1,0:T(8,128)(2,1)} %pad_maximum_fusion) | copy-start | bytes 12582916
  155.2 88.8 %collective-permute-start = (bf16[4,128,1024]{2,1,0:T(8,128)(2,1)}, bf16[4,128,1024]{2,1,0:T(8,128)(2,1)}, u32[]{:S(2)}, u32[]{:S(2)}) collective-permute-start(bf16[4,128,1024]{2,1,0:T(8,128)(2,1)} %get-tuple-element.9), channel_id=1, source_target_pairs={{2,0},{3,1},{4,2},{5,3},{6,4},{7,5},{8,6},{9,7},{10,8},{11,9},{12,... | collective-permute-start | bytes 3145736 | tf_op jit(solution)/shard_map/ppermute | solution.py:12
  178.5 67.7 %collective-permute-start.1 = (bf16[4,128,1024]{2,1,0:T(8,128)(2,1)}, bf16[4,128,1024]{2,1,0:T(8,128)(2,1)}, u32[]{:S(2)}, u32[]{:S(2)}) collective-permute-start(bf16[4,128,1024]{2,1,0:T(8,128)(2,1)} %get-tuple-element.8), channel_id=1, source_target_pairs={{1,0},{2,1},{3,2},{4,3},{5,4},{6,5},{7,6},{8,7},{9,8},{10,9},{11,1... | collective-permute-start | bytes 3145736 | tf_op jit(solution)/shard_map/ppermute | solution.py:12
  182.3 88.2 %collective-permute-start.2 = (bf16[4,128,1024]{2,1,0:T(8,128)(2,1)}, bf16[4,128,1024]{2,1,0:T(8,128)(2,1)}, u32[]{:S(2)}, u32[]{:S(2)}) collective-permute-start(bf16[4,128,1024]{2,1,0:T(8,128)(2,1)} %get-tuple-element.7), channel_id=1, source_target_pairs={{0,1},{1,2},{2,3},{3,4},{4,5},{5,6},{6,7},{7,8},{8,9},{9,10},{10,1... | collective-permute-start | bytes 3145736 | tf_op jit(solution)/shard_map/ppermute | solution.py:12
  206.8 66.0 %collective-permute-start.3 = (bf16[4,128,1024]{2,1,0:T(8,128)(2,1)}, bf16[4,128,1024]{2,1,0:T(8,128)(2,1)}, u32[]{:S(2)}, u32[]{:S(2)}) collective-permute-start(bf16[4,128,1024]{2,1,0:T(8,128)(2,1)} %get-tuple-element.6), channel_id=1, source_target_pairs={{0,2},{1,3},{2,4},{3,5},{4,6},{5,7},{6,8},{7,9},{8,10},{9,11},{10,... | collective-permute-start | bytes 3145736 | tf_op jit(solution)/shard_map/ppermute | solution.py:12
  238.4 3.0 %copy-start.11 = (bf16[1024,1024]{1,0:T(8,128)(2,1)S(1)}, bf16[1024,1024]{1,0:T(8,128)(2,1)}, u32[]{:S(2)}) copy-start(bf16[1024,1024]{1,0:T(8,128)(2,1)} %param.21) | copy-start | bytes 6291460
  246.3 28.8 %copy-start.12 = (f32[1024]{0:T(1024)S(1)}, f32[1024]{0:T(1024)}, u32[]{:S(2)}) copy-start(f32[1024]{0:T(1024)} %param.23) | copy-start | bytes 12292
Sparse Core Ops, SparseCore 0:
  44.8 73.5 reduce-scatter.1
where the time goes:
time: 292 us; the launch traced here: 291 us
  starting transfers between devices  70 us (24%)
  waiting for transfers between devices  66.6 us (23%)
  matrix products  61.7 us (21%)
  other arithmetic  40.9 us (14%)
  local copies, waits for them, and re-layouts  37.8 us (13%)
  between operations  14.2 us (5%)
    ppermute x8, starting transfers between devices, shifted(): return lax.ppermute(shard, axis, pairs)  70 us
    ppermute x8, waiting for transfers between devices, shifted(): return lax.ppermute(shard, axis, pairs)  66.6 us
    scatter-add x1, other arithmetic, shards(): grad_tiles.at[send_list.reshape(-1)]  17.5 us
    dot_general x1, matrix products, shards(): lax.dot_general(gathered_one, w_neigh_one, (((0,), (0,)), ((), ())), pref...  14.6 us
    dot_general x1, matrix products, shards(): lax.dot_general(features, w_self_one, (((0,), (0,)), ((), ())), preferred...  11 us
    unnamed x32, local copies, waits for them, and re-layouts  10.6 us
    dot_general x1, matrix products, shards(): lax.dot_general(folded, back_neigh, (((0,), (0,)), ((), ())), preferred_e...  10.3 us
    dot_general x1, matrix products, shards(): jnp.dot(gathered_two, w_neigh_two, preferred_element_type=jnp.float32)  9.38 us
  transfers between devices with their start and end apart: 9, of which 2 were waited for; matrix products, arithmetic and copies ran while one was open for 27% of the time, Pallas kernels for 0%

commit v1 on v0

v1 whole, which is shorter than its diff:
```python
import functools

import jax
import jax.numpy as jnp
from jax import lax
from jax.experimental import pallas as pl
from jax.experimental.pallas import tpu as pltpu
from jax.sharding import PartitionSpec as P

TILE = 128
TILE_DEV = 6
SLOTS = 4
NEAR = 4
MIB = 1 << 20

VMEM = pl.BlockSpec(memory_space=pltpu.VMEM)
SMEM = pl.BlockSpec(memory_space=pltpu.SMEM)


def shifted(shard, by):
    count = lax.axis_size("dom")
    pairs = [(i, i + by) for i in range(count) if 0 <= i + by < count]
    return lax.ppermute(shard, "dom", pairs)


def call(body, outs, in_specs, scratch=(), flops=0, moved=0, **extra):
    return pl.pallas_call(
        body,
        out_shape=outs,
        in_specs=in_specs,
        out_specs=jax.tree.map(lambda _: VMEM, outs),
        scratch_shapes=list(scratch),
        cost_estimate=pl.CostEstimate(flops=flops, bytes_accessed=moved, transcendentals=0),
        compiler_params=pltpu.CompilerParams(vmem_limit_bytes=52 * MIB),
        **extra,
    )


def tn_dot(left, right):
    return lax.dot_general(left, right, (((0,), (0,)), ((), ())), preferred_element_type=jnp.float32)


def nt_dot(left, right):
    return lax.dot_general(left, right, (((1,), (1,)), ((), ())), preferred_element_type=jnp.float32)


def nn_dot(left, right):
    return jnp.dot(left, right, preferred_element_type=jnp.float32)


def order_of(tiles, count):
    listed = []
    for tile in range(TILE_DEV):
        hit = jnp.int32(0)
        for slot in range(SLOTS):
            hit = jnp.where((tiles(slot) == tile) & (slot < count), 1, hit)
        listed.append(hit)
    total = functools.reduce(lambda a, b: a + b, listed)
    places = []
    ahead = jnp.int32(0)
    behind = total
    for tile in range(TILE_DEV):
        places.append(jnp.where(listed[tile] == 1, ahead, behind))
        ahead = ahead + listed[tile]
        behind = behind + (1 - listed[tile])
    return places


def place_of(places, tile):
    at = places[0]
    for other in range(1, TILE_DEV):
        at = jnp.where(tile == other, places[other], at)
    return at


def tile_rows(ref, index):
    return ref.at[pl.ds(pl.multiple_of(index * TILE, TILE), TILE)]


def far_kernel(adj_ref, src_ref, cot_ref, w_ref, back_ref, fold_ref, up_ref, down_ref, acc_ref):
    back = nt_dot(cot_ref[...], w_ref[...]).astype(jnp.bfloat16)
    back_ref[...] = back
    acc_ref[...] = jnp.zeros_like(acc_ref)
    for seed in range(adj_ref.shape[0]):
        rows = pl.ds(seed * TILE, TILE)

        def add(k, _):
            slot = src_ref[seed, k] - TILE_DEV
            low = (slot >= 0) & (slot < SLOTS)
            high = slot >= 3 * SLOTS

            @pl.when(low | high)
            def _():
                at = jnp.where(low, slot, slot - 2 * SLOTS)
                cols = pl.ds(pl.multiple_of(at * TILE, TILE), TILE)
                acc_ref[rows, cols] += adj_ref[seed, k].astype(jnp.float32)

            return 0

        lax.fori_loop(0, adj_ref.shape[1], add, 0, unroll=4)
    fold_ref[...] = acc_ref[...].astype(jnp.bfloat16)
    half = SLOTS * TILE
    up_ref[...] = tn_dot(fold_ref[:, :half], back).astype(jnp.bfloat16).reshape(up_ref.shape)
    down_ref[...] = tn_dot(fold_ref[:, half:], back).astype(jnp.bfloat16).reshape(down_ref.shape)


def near_kernel(
    adj_ref, src_ref, back_ref, meta_ref, fold_ref, own_up_ref, own_down_ref, b_up_ref, b_down_ref, acc_ref, place_ref
):
    acc_ref[...] = jnp.zeros_like(acc_ref)
    for seed in range(adj_ref.shape[0]):
        rows = pl.ds(seed * TILE, TILE)

        def add(k, _):
            slot = src_ref[seed, k]
            local = slot < TILE_DEV
            near = (slot >= TILE_DEV + SLOTS) & (slot < TILE_DEV + 3 * SLOTS)

            @pl.when(local | near)
            def _():
                at = jnp.where(local, slot, slot - SLOTS)
                cols = pl.ds(pl.multiple_of(at * TILE, TILE), TILE)
                acc_ref[rows, cols] += adj_ref[seed, k].astype(jnp.float32)

            return 0

        lax.fori_loop(0, adj_ref.shape[1], add, 0, unroll=4)
    fold_ref[...] = acc_ref[...].astype(jnp.bfloat16)
    back = back_ref[...]
    for far_q, near_q, row, own_ref, b_ref in ((0, 1, 3, own_up_ref, b_up_ref), (3, 2, 1, own_down_ref, b_down_ref)):
        places = order_of(lambda m: meta_ref[row, far_q * SLOTS + m], meta_ref[row, 16 + far_q])
        place_ref[...] = jnp.zeros_like(place_ref)
        for slot in range(SLOTS):
            at = place_of(places, meta_ref[row, near_q * SLOTS + slot])

            @pl.when(slot < meta_ref[row, 16 + near_q])
            def _():
                cols = pl.ds(pl.multiple_of(at * TILE, TILE), TILE)
                start = (TILE_DEV + (near_q - 1) * SLOTS + slot) * TILE
                place_ref[:, cols] += fold_ref[:, start : start + TILE].astype(jnp.float32)

        placed = place_ref[...].astype(jnp.bfloat16)
        own_ref[...] = tn_dot(placed[:, : NEAR * TILE], back).reshape(own_ref.shape)
        b_ref[...] = tn_dot(placed[:, NEAR * TILE :], back).astype(jnp.bfloat16).reshape(b_ref.shape)


def join_kernel(own_up_ref, own_down_ref, far_up_ref, far_down_ref, meta_ref, up_ref, down_ref, sum_ref):
    for far_q, row, own_ref, far_ref, out_ref in (
        (0, 3, own_up_ref, far_up_ref, up_ref),
        (3, 1, own_down_ref, far_down_ref, down_ref),
    ):
        count = meta_ref[row, 16 + far_q]
        places = order_of(lambda m: meta_ref[row, far_q * SLOTS + m], count)
        sum_ref[...] = own_ref[...]
        for slot in range(SLOTS):
            at = jnp.minimum(place_of(places, meta_ref[row, far_q * SLOTS + slot]), NEAR - 1)

            @pl.when(slot < count)
            def _():
                sum_ref[at] += far_ref[slot].astype(jnp.float32)

        out_ref[...] = sum_ref[...].astype(jnp.bfloat16)


def local_kernel(fold_ref, back_ref, cot_ref, w_ref, seeds_ref, out_ref):
    rows = out_ref.shape[0]
    back_self = nt_dot(cot_ref[...], w_ref[...]).astype(jnp.bfloat16)
    hot = lax.broadcasted_iota(jnp.int32, (rows, seeds_ref.shape[1]), 0) == seeds_ref[...]
    hot = hot.astype(jnp.float32).astype(jnp.bfloat16)
    out_ref[...] = nn_dot(hot, back_self) + tn_dot(fold_ref[:, :rows], back_ref[...])


def gather_kernel(src_ref, feat_ref, adj_ref, out_ref):
    step = pl.program_id(0)
    width = feat_ref.shape[0]
    span = out_ref.shape[2]
    out_ref[0, :width] = feat_ref[:, pl.ds(pl.multiple_of(step * span, span), span)]
    for tile in range(adj_ref.shape[0]):
        parts = []
        for k in range(adj_ref.shape[1]):
            source = src_ref[step * adj_ref.shape[0] + tile, k]
            parts.append(feat_ref[:, pl.ds(pl.multiple_of(source * TILE, TILE), TILE)])
        left = jnp.concatenate(parts, axis=1)
        right = jnp.concatenate([adj_ref[tile, k] for k in range(adj_ref.shape[1])], axis=1)
        out_ref[0, width:, tile * TILE : (tile + 1) * TILE] = nt_dot(left, right).astype(jnp.bfloat16)


def hidden_kernel(in_ref, w_ref, bias_ref, meta_ref, hid_ref, a_up_ref, a_down_ref, b_up_ref, b_down_ref):
    depth = in_ref.shape[0] * in_ref.shape[1]
    inputs = in_ref[...].reshape(depth, in_ref.shape[2])
    weights = w_ref[...].reshape(depth, w_ref.shape[2])
    total = tn_dot(inputs, weights) + bias_ref[...]
    hidden = jnp.maximum(total, 0.0).astype(jnp.bfloat16)
    hid_ref[...] = hidden.reshape(hid_ref.shape)
    for far_q, a_ref, b_ref in ((3, a_up_ref, b_up_ref), (0, a_down_ref, b_down_ref)):
        places = order_of(lambda m: meta_ref[2, far_q * SLOTS + m], meta_ref[2, 16 + far_q])
        for tile in range(TILE_DEV):

            @pl.when(places[tile] < NEAR)
            def _():
                a_ref[jnp.minimum(places[tile], NEAR - 1)] = hid_ref[tile]

            @pl.when(places[tile] >= NEAR)
            def _():
                b_ref[jnp.maximum(places[tile] - NEAR, 0)] = hid_ref[tile]


def mid_kernel(
    fold_ref, hid_ref, a_up_ref, b_up_ref, a_down_ref, b_down_ref, meta_ref, seeds_ref, w_ref, bias_ref,
    part_ref, self_ref, table_ref,
):
    rows = TILE_DEV * TILE
    table_ref[:rows] = hid_ref[...].reshape(rows, hid_ref.shape[2])
    start = TILE_DEV
    for near_q, far_q, row, a_ref, b_ref in ((1, 0, 3, a_down_ref, b_down_ref), (2, 3, 1, a_up_ref, b_up_ref)):
        places = order_of(lambda m: meta_ref[row, far_q * SLOTS + m], meta_ref[row, 16 + far_q])
        for slot in range(SLOTS):
            at = place_of(places, meta_ref[row, near_q * SLOTS + slot])
            live = slot < meta_ref[row, 16 + near_q]
            to = slice((start + slot) * TILE, (start + slot + 1) * TILE)

            @pl.when(live & (at < NEAR))
            def _():
                table_ref[to] = a_ref[jnp.minimum(at, NEAR - 1)]

            @pl.when(live & (at >= NEAR))
            def _():
                table_ref[to] = b_ref[jnp.maximum(at - NEAR, 0)]

            @pl.when(jnp.logical_not(live))
            def _():
                table_ref[to] = jnp.zeros((TILE, table_ref.shape[1]), table_ref.dtype)

        start += SLOTS
    part_ref[...] = nn_dot(fold_ref[...], table_ref[...])
    hot = lax.broadcasted_iota(jnp.int32, (rows, seeds_ref.shape[1]), 0) == seeds_ref[...]
    hot = hot.astype(jnp.float32).astype(jnp.bfloat16)
    chosen = tn_dot(hot, table_ref[:rows]).astype(jnp.bfloat16)
    self_ref[...] = nn_dot(chosen, w_ref[...]) + bias_ref[...]


def last_kernel(fold_ref, f_up_ref, f_down_ref, meta_ref, part_ref, self_ref, w_ref, out_ref, table_ref):
    start = 0
    for far_q, row, f_ref in ((0, 4, f_down_ref), (3, 0, f_up_ref)):
        count = meta_ref[row, 16 + far_q]
        places = order_of(lambda m: meta_ref[row, far_q * SLOTS + m], count)
        for slot in range(SLOTS):
            at = place_of(places, meta_ref[row, far_q * SLOTS + slot])
            to = slice((start + slot) * TILE, (start + slot + 1) * TILE)

            @pl.when(slot < count)
            def _():
                table_ref[to] = f_ref[jnp.minimum(at, NEAR - 1)]

            @pl.when(slot >= count)
            def _():
                table_ref[to] = jnp.zeros((TILE, table_ref.shape[1]), table_ref.dtype)

        start += SLOTS
    gathered = (part_ref[...] + nn_dot(fold_ref[...], table_ref[...])).astype(jnp.bfloat16)
    out_ref[...] = (self_ref[...] + nn_dot(gathered, w_ref[...])).astype(jnp.bfloat16)


def merge_kernel(local_ref, a_up_ref, b_up_ref, a_down_ref, b_down_ref, meta_ref, out_ref):
    up = order_of(lambda m: meta_ref[2, 3 * SLOTS + m], meta_ref[2, 16 + 3])
    down = order_of(lambda m: meta_ref[2, m], meta_ref[2, 16])
    for tile in range(TILE_DEV):
        to = slice(tile * TILE, (tile + 1) * TILE)
        out_ref[to] = local_ref[to]
        for places, a_ref, b_ref in ((up, a_up_ref, b_up_ref), (down, a_down_ref, b_down_ref)):

            @pl.when(places[tile] < NEAR)
            def _():
                out_ref[to] += a_ref[jnp.minimum(places[tile], NEAR - 1)].astype(jnp.float32)

            @pl.when(places[tile] >= NEAR)
            def _():
                out_ref[to] += b_ref[jnp.maximum(places[tile] - NEAR, 0)].astype(jnp.float32)


def shards(
    features,
    adj_one,
    src_one,
    w_self_one,
    w_neigh_one,
    bias_one,
    w_self_two,
    w_neigh_two,
    bias_two,
    seed_rows,
    adj_two,
    src_two,
    send_tiles,
    send_count,
    cotangent,
):
    bf16, f32 = jnp.bfloat16, jnp.float32
    width = features.shape[0]
    part_tiles = adj_one.shape[0]
    hid = w_self_two.shape[0]
    feat_count = lax.axis_size("feat")
    row_dev = features.shape[1] // feat_count
    seeds = cotangent.shape[1]
    blocks, sources = adj_two[0, 0], src_two[0, 0]
    upstream = cotangent[0]
    shape = jax.ShapeDtypeStruct

    own = jnp.concatenate([send_tiles.reshape(-1), send_count.reshape(-1), jnp.zeros((4,), jnp.int32)])
    lists = lax.all_gather(own, "dom")
    lists = jnp.pad(lists, ((2, 2), (0, 0)))
    meta = lax.dynamic_slice_in_dim(lists, lax.axis_index("dom"), 5, 0)
    weights = lax.all_gather(jnp.concatenate([w_self_one, w_neigh_one]), "feat")

    quad = shape((NEAR, TILE, hid), bf16)
    pair = shape((TILE_DEV - NEAR, TILE, hid), bf16)
    quad32 = shape((NEAR, TILE, hid), f32)
    far_cols, near_cols = 2 * SLOTS * TILE, (TILE_DEV + 2 * SLOTS) * TILE

    back, fold_far, far_up, far_down = call(
        far_kernel,
        (shape((seeds, hid), bf16), shape((seeds, far_cols), bf16), quad, quad),
        [VMEM, SMEM, VMEM, VMEM],
        [pltpu.VMEM((seeds, far_cols), f32)],
        flops=4 * seeds * hid * hid,
        moved=8 * MIB,
    )(blocks, sources, upstream, w_neigh_two)
    got_far_up = shifted(far_up, 1)
    got_far_down = shifted(far_down, -1)

    sent = pl.pallas_call(
        gather_kernel,
        grid=(feat_count,),
        in_specs=[
            SMEM,
            pl.BlockSpec((width, features.shape[1]), lambda i: (0, 0)),
            pl.BlockSpec((part_tiles // feat_count,) + adj_one.shape[1:], lambda i: (i, 0, 0, 0)),
        ],
        out_specs=pl.BlockSpec((1, 2 * width, row_dev), lambda i: (i, 0, 0)),
        out_shape=shape((feat_count, 2 * width, row_dev), bf16),
        cost_estimate=pl.CostEstimate(flops=1200 * MIB, bytes_accessed=10 * MIB, transcendentals=0),
        compiler_params=pltpu.CompilerParams(vmem_limit_bytes=32 * MIB),
    )(src_one, features, adj_one)

    fold_near, own_up, own_down, b_up, b_down = call(
        near_kernel,
        (shape((seeds, near_cols), bf16), quad32, quad32, pair, pair),
        [VMEM, SMEM, VMEM, SMEM],
        [pltpu.VMEM((seeds, near_cols), f32), pltpu.VMEM((seeds, TILE_DEV * TILE), f32)],
        flops=3 * seeds * hid * hid,
        moved=12 * MIB,
    )(blocks, sources, back, meta)
    got_b_up = shifted(b_up, 1)
    got_b_down = shifted(b_down, -1)

    taken = lax.all_to_all(sent, "feat", 0, 0)

    a_up, a_down = call(
        join_kernel,
        (quad, quad),
        [VMEM, VMEM, VMEM, VMEM, SMEM],
        [pltpu.VMEM(quad32.shape, f32)],
        moved=8 * MIB,
    )(own_up, own_down, got_far_up, got_far_down, meta)
    got_a_up = shifted(a_up, 1)
    got_a_down = shifted(a_down, -1)

    hidden, h_up, h_down, i_up, i_down = call(
        hidden_kernel,
        (shape((TILE_DEV, TILE, hid), bf16), quad, quad, pair, pair),
        [VMEM, VMEM, VMEM, SMEM],
        flops=2 * row_dev * 2 * width * feat_count * hid,
        moved=10 * MIB,
    )(taken, weights, bias_one[None], meta)
    got_h_up = shifted(h_up, 1)
    got_h_down = shifted(h_down, -1)
    got_i_up = shifted(i_up, 1)
    got_i_down = shifted(i_down, -1)
    next_up = shifted(got_h_up, 1)
    next_down = shifted(got_h_down, -1)

    local = call(
        local_kernel,
        shape((row_dev, hid), f32),
        [VMEM] * 5,
        flops=5 * seeds * hid * hid,
        moved=8 * MIB,
    )(fold_near, back, upstream, w_self_two, seed_rows[0])

    part, self_term = call(
        mid_kernel,
        (shape((seeds, hid), f32), shape((seeds, hid), f32)),
        [VMEM] * 6 + [SMEM] + [VMEM] * 3,
        [pltpu.VMEM((near_cols, hid), bf16)],
        flops=7 * seeds * hid * hid,
        moved=16 * MIB,
    )(fold_near, hidden, got_h_up, got_i_up, got_h_down, got_i_down, meta, seed_rows[0], w_self_two, bias_two[None])
    layer_out = call(
        last_kernel,
        shape((seeds, hid), bf16),
        [VMEM] * 3 + [SMEM] + [VMEM] * 3,
        [pltpu.VMEM((far_cols, hid), bf16)],
        flops=4 * seeds * hid * hid,
        moved=10 * MIB,
    )(fold_far, next_up, next_down, meta, part, self_term, w_neigh_two)
    grads = call(
        merge_kernel, shape((row_dev, hid), f32), [VMEM] * 5 + [SMEM], moved=9 * MIB
    )(local, got_a_down, got_b_down, got_a_up, got_b_up, meta)
    return (layer_out[None], grads[None])


def solution(mesh):
    return jax.shard_map(
        shards,
        mesh=mesh,
        in_specs=(
            P("feat", "dom"),
            P("dom", None, None, None),
            P("dom", None),
            P("feat", None),
            P("feat", None),
            P(),
            P(),
            P(),
            P(),
            P("dom", "feat", None),
            P("dom", "feat", None, None, None, None),
            P("dom", "feat", None, None),
            P("dom", "feat", None, None),
            P("dom", "feat", None),
            P("dom", "feat", None),
        ),
        out_specs=(P("dom", "feat", None), P("dom", "feat", None)),
        check_vma=False,
    )
```

time: 292 us -> 205 us (0.70)
  matrix products: 61.7 us -> 0 us
  Pallas kernels: 0 us -> 61.5 us
  other arithmetic: 40.9 us -> 2 us
  waiting for transfers between devices: 66.6 us -> 34.7 us
  blocking collectives: 0 us -> 29.1 us
  local copies, waits for them, and re-layouts: 37.8 us -> 11.3 us
  starting transfers between devices: 70 us -> 49.7 us
    dot_general x8 -> x0, matrix products: 61.7 us -> none  [the longest x1 14.6 us: shards(): lax.dot_general(gathered_one, w_neigh_one, (((0,), (0,)), ((), ())), pref...]
    pallas_call x0 -> x9, Pallas kernels: none -> 61.5 us  [the longest x1 9.06 us: shards(): call(mid_kernel, (shape((seeds, hid), f32), shape((seeds, hid), f32)), [V...]
    ppermute x8 -> x12, waiting for transfers between devices: 66.6 us -> 34.6 us  [shifted(): return lax.ppermute(shard, 'dom', pairs)]
    unnamed x0 -> x1, blocking collectives: none -> 29.1 us
    scatter-add x2 -> x0, other arithmetic: 26.8 us -> none  [the longest x1 17.5 us: shards(): grad_tiles.at[send_list.reshape(-1)]]
    ppermute x8 -> x12, starting transfers between devices: 70 us -> 45.2 us  [shifted(): return lax.ppermute(shard, 'dom', pairs)]
    gather x3 -> x0, local copies, waits for them, and re-layouts: 12.1 us -> none  [the longest x1 4.34 us: shards(): chosen = hidden[chosen_rows]]
    slice x2 -> x0, local copies, waits for them, and re-layouts: 8.56 us -> none  [the longest x1 4.38 us: shards(): halo_grads[slot_index].astype(jnp.bfloat16)]
  transfers between devices with their start and end apart: 9 -> 14, of which waited for: 2 -> 4; matrix products, arithmetic and copies ran while one was open for 27% -> 1% of each run, Pallas kernels for 0% -> 27%
where the time goes in v1:
time: 205 us; the launch traced here: 203 us
  Pallas kernels  61.5 us (30%)
  starting transfers between devices  49.7 us (24%)
  waiting for transfers between devices  34.7 us (17%)
  blocking collectives  29.1 us (14%)
  between operations  15 us (7%)
  local copies, waits for them, and re-layouts  11.3 us (6%)
    ppermute x12, starting transfers between devices, shifted(): return lax.ppermute(shard, 'dom', pairs)  45.2 us
    ppermute x12, waiting for transfers between devices, shifted(): return lax.ppermute(shard, 'dom', pairs)  34.6 us
    unnamed x1, blocking collectives  29.1 us
    unnamed x41, local copies, waits for them, and re-layouts  11.1 us
    pallas_call x1, Pallas kernels, shards(): call(mid_kernel, (shape((seeds, hid), f32), shape((seeds, hid), f32)), [V...  9.06 us
    pallas_call x1, Pallas kernels, shards(): call(far_kernel, (shape((seeds, hid), bf16), shape((seeds, far_cols), bf1...  7.63 us
    pallas_call x1, Pallas kernels, shards(): call(near_kernel, (shape((seeds, near_cols), bf16), quad32, quad32, pair,...  7.56 us
    pallas_call x1, Pallas kernels, shards(): call(hidden_kernel, (shape((TILE_DEV, TILE, hid), bf16), quad, quad, pair...  7.51 us
  transfers between devices with their start and end apart: 14, of which 4 were waited for; matrix products, arithmetic and copies ran while one was open for 1% of the time, Pallas kernels for 27%

profile of v1, /device:TPU:104, one launch (start us, length us, event | category | flops | bytes accessed | tf_op | source)
XLA Modules:
  0.0 203.2 jit_solution(8953792639007754210)
XLA Ops:
  7.2 0.0 all-gather.4.cloned.1.call-start
  7.2 1.8 pad_maximum_fusion
  9.0 0.0 all-gather.4.cloned.1.call-update
  9.1 0.8 copy.17.src_ref
  9.8 2.8 %copy-done = bf16[48,4,128,128]{3,2,1,0:T(8,128)(2,1)S(1)} copy-done((bf16[48,4,128,128]{3,2,1,0:T(8,128)(2,1)S(1)}, bf16[48,4,128,128]{3,2,1,0:T(8,128)(2,1)}, u32[]{:S(2)}) %copy-start) | copy-done | bytes 6291480
  12.6 1.3 copy-done.1
  13.9 5.8 %shard_map.159 = bf16[8,192,768]{2,1,0:T(8,128)(2,1)} custom-call(s32[48,4]{1,0:T(8,128)S(1)} %copy.17.src_ref, bf16[96,6144]{1,0:T(8,128)(2,1)S(1)} %copy-done.1, bf16[48,4,128,128]{3,2,1,0:T(8,128)(2,1)S(1)} %copy-done), custom_call_target="tpu_custom_call" | custom-call | flops 1258291200 | bytes 10485760 | tf_op jit(solution)/shard_map/pallas_call | solution.py:331
  19.7 4.4 %all-to-all-start = ((bf16[8,192,768]{2,1,0:T(8,128)(2,1)}), bf16[8,192,768]{2,1,0:T(8,128)(2,1)S(1)}, u32[]{:S(2)}, u32[]{:S(2)}) async-start(bf16[8,192,768]{2,1,0:T(8,128)(2,1)} %shard_map.159), calls=%async_computation | async-start | bytes 4718592 | tf_op jit(solution)/shard_map/all_to_all | solution.py:356
  24.2 0.0 copy-done.5
  24.2 0.0 copy-start.15
  24.2 0.0 copy-start.18
  24.2 0.0 copy-start.16
  24.2 0.0 copy-start.3
  24.2 7.6 %shard_map.158 = (bf16[512,1024]{1,0:T(8,128)(2,1)S(1)}, bf16[512,1024]{1,0:T(8,128)(2,1)}, bf16[4,128,1024]{2,1,0:T(8,128)(2,1)}, bf16[4,128,1024]{2,1,0:T(8,128)(2,1)}) custom-call(bf16[4,16,128,128]{3,2,1,0:T(8,128)(2,1)} %bitcast.21, s32[4,16]{1,0:T(4,128)S(1)} %bitcast.13, bf16[512,1024]{1,0:T(8,128)(2,1)} %bitcast.23, bf16[1024,1024]{1,0:T(8,128)(2,1)} %w_ref.6), custom_call_target="tpu_custom_call" | custom-call | flops 2147483648 | bytes 8388608 | tf_op jit(solution)/shard_map/pallas_call | solution.py:320
  31.9 1.0 copy-done.7
  32.8 2.1 %collective-permute-start.6 = (bf16[4,128,1024]{2,1,0:T(8,128)(2,1)}, bf16[4,128,1024]{2,1,0:T(8,128)(2,1)S(1)}, u32[]{:S(2)}, u32[]{:S(2)}) collective-permute-start(bf16[4,128,1024]{2,1,0:T(8,128)(2,1)} %get-tuple-element.32), channel_id=1, source_target_pairs={{0,1},{1,2},{2,3},{3,4},{4,5},{5,6},{6,7},{7,8},{8,9},{9,10},{10,1... | collective-permute-start | bytes 3145736 | tf_op jit(solution)/shard_map/ppermute | solution.py:23
  34.9 3.8 %collective-permute-start.7 = (bf16[4,128,1024]{2,1,0:T(8,128)(2,1)}, bf16[4,128,1024]{2,1,0:T(8,128)(2,1)}, u32[]{:S(2)}, u32[]{:S(2)}) collective-permute-start(bf16[4,128,1024]{2,1,0:T(8,128)(2,1)} %get-tuple-element.33), channel_id=1, source_target_pairs={{1,0},{2,1},{3,2},{4,3},{5,4},{6,5},{7,6},{8,7},{9,8},{10,9},{11,1... | collective-permute-start | bytes 3145736 | tf_op jit(solution)/shard_map/ppermute | solution.py:23
  38.7 0.0 copy-done.15
  38.7 0.1 reshape.10
  38.8 0.0 copy-done.18
  38.8 0.6 dynamic-slice
  40.1 0.0 copy-done.16
  40.1 0.2 add_dynamic-update-slice_fusion
  40.2 29.1 %all-reduce.1 = s32[384]{0:T(512)S(1)} all-reduce(s32[384]{0:T(512)S(1)} %add_dynamic-update-slice_fusion), channel_id=3, replica_groups=mesh['feat'=8,'dom'=16] {'dom'}, use_global_device_ids=true, to_apply=%add.1 | all-reduce | flops 384 | bytes 3072
  69.3 0.1 reshape.13
  69.4 0.0 all-to-all-done.in_ref
  69.4 0.0 copy-start.9
  69.4 0.0 all-gather.4.cloned.1.call-done
  69.5 1.4 copy-done.9
  70.8 0.0 copy-done.3
  70.8 7.5 %shard_map.160 = (bf16[6,128,1024]{2,1,0:T(8,128)(2,1)}, bf16[4,128,1024]{2,1,0:T(8,128)(2,1)}, bf16[4,128,1024]{2,1,0:T(8,128)(2,1)}, bf16[2,128,1024]{2,1,0:T(8,128)(2,1)S(1)}, bf16[2,128,1024]{2,1,0:T(8,128)(2,1)S(1)}) custom-call(bf16[8,192,768]{2,1,0:T(8,128)(2,1)} %copy-done.9, bf16[8,192,1024]{2,1,0:T(8,128)(2,1)} %bitcast.20, ...), custom_call_target="tpu_custom_call" | custom-call | flops 2415919104 | bytes 10485760 | tf_op jit(solution)/shard_map/pallas_call | solution.py:368
  78.4 7.3 %collective-permute-start = (bf16[4,128,1024]{2,1,0:T(8,128)(2,1)}, bf16[4,128,1024]{2,1,0:T(8,128)(2,1)S(1)}, u32[]{:S(2)}, u32[]{:S(2)}) collective-permute-start(bf16[4,128,1024]{2,1,0:T(8,128)(2,1)} %get-tuple-element.21), channel_id=1, source_target_pairs={{0,1},{1,2},{2,3},{3,4},{4,5},{5,6},{6,7},{7,8},{8,9},{9,10},{10,1... | collective-permute-start | bytes 3145736 | tf_op jit(solution)/shard_map/ppermute | solution.py:23
  85.7 1.9 collective-permute-start.2
  87.6 7.6 %shard_map.161 = (bf16[512,1792]{1,0:T(8,128)(2,1)}, f32[4,128,1024]{2,1,0:T(8,128)}, f32[4,128,1024]{2,1,0:T(8,128)}, bf16[2,128,1024]{2,1,0:T(8,128)(2,1)S(1)}, bf16[2,128,1024]{2,1,0:T(8,128)(2,1)S(1)}) custom-call(bf16[4,16,128,128]{3,2,1,0:T(8,128)(2,1)} %bitcast.22, s32[4,16]{1,0:T(4,128)S(1)} %bitcast.14, bf16[512,1024]{1,0:T(8,128)(2,1)} %copy-done.7, ...), custom_call_target="tpu_custom_call" | custom-call | flops 1610612736 | bytes 12582912 | tf_op jit(solution)/shard_map/pallas_call | solution.py:345
  95.2 5.9 %collective-permute-start.11 = (bf16[2,128,1024]{2,1,0:T(8,128)(2,1)S(1)}, bf16[2,128,1024]{2,1,0:T(8,128)(2,1)S(1)}, u32[]{:S(2)}, u32[]{:S(2)}) collective-permute-start(bf16[2,128,1024]{2,1,0:T(8,128)(2,1)S(1)} %get-tuple-element.37), channel_id=1, source_target_pairs={{0,1},{1,2},{2,3},{3,4},{4,5},{5,6},{6,7},{7,8},{8,9},{9,10},{10,1... | collective-permute-start | bytes 1572872 | tf_op jit(solution)/shard_map/ppermute | solution.py:23
  101.1 0.0 collective-permute-done.6.far_up_ref
  101.1 0.0 collective-permute-done.7.far_down_ref
  101.1 1.0 copy-done.14
  102.1 4.7 %shard_map.165 = (bf16[4,128,1024]{2,1,0:T(8,128)(2,1)S(1)}, bf16[4,128,1024]{2,1,0:T(8,128)(2,1)}) custom-call(f32[4,128,1024]{2,1,0:T(8,128)} %get-tuple-element.30.own_up_ref, f32[4,128,1024]{2,1,0:T(8,128)} %get-tuple-element.31.own_down_ref, bf16[4,128,1024]{2,1,0:T(8,128)(2,1)} %copy-done.14, ...), custom_call_target="tpu_custom_call" | custom-call | bytes 8388608 | tf_op jit(solution)/shard_map/pallas_call | solution.py:358
  106.8 1.9 collective-permute-start.10
  108.7 3.9 %collective-permute-start.9 = (bf16[2,128,1024]{2,1,0:T(8,128)(2,1)S(1)}, bf16[2,128,1024]{2,1,0:T(8,128)(2,1)S(1)}, u32[]{:S(2)}, u32[]{:S(2)}) collective-permute-start(bf16[2,128,1024]{2,1,0:T(8,128)(2,1)S(1)} %get-tuple-element.35), channel_id=1, source_target_pairs={{1,0},{2,1},{3,2},{4,3},{5,4},{6,5},{7,6},{8,7},{9,8},{10,9},{11,1... | collective-permute-start | bytes 1572872 | tf_op jit(solution)/shard_map/ppermute | solution.py:23
  112.6 8.1 %collective-permute-done.11.b_down_ref = bf16[2,128,1024]{2,1,0:T(8,128)(2,1)S(1)} collective-permute-done((bf16[2,128,1024]{2,1,0:T(8,128)(2,1)S(1)}, bf16[2,128,1024]{2,1,0:T(8,128)(2,1)S(1)}, u32[]{:S(2)}, u32[]{:S(2)}) %collective-permute-start.11) | collective-permute-done | bytes 524320 | tf_op jit(solution)/shard_map/ppermute | solution.py:23
  120.7 1.9 collective-permute-start.8
  122.6 0.0 collective-permute-done.a_up_ref
  122.6 0.0 copy-start.17
  122.6 6.5 %collective-permute-start.1 = (bf16[4,128,1024]{2,1,0:T(8,128)(2,1)S(1)}, bf16[4,128,1024]{2,1,0:T(8,128)(2,1)S(1)}, u32[]{:S(2)}, u32[]{:S(2)}) collective-permute-start(bf16[4,128,1024]{2,1,0:T(8,128)(2,1)S(1)} %collective-permute-done.a_up_ref), channel_id=1, source_target_pairs={{0,1},{1,2},{2,3},{3,4},{4,5},{5,6},{6,7},{7,8},{8,9},{9,10},{10,1... | collective-permute-start | bytes 3145736 | tf_op jit(solution)/shard_map/ppermute | solution.py:23
  129.1 0.0 collective-permute-done.2.a_down_ref
  129.2 1.9 collective-permute-start.3
  131.1 0.0 collective-permute-done.9.b_up_ref
  131.1 6.0 %collective-permute-start.4 = (bf16[2,128,1024]{2,1,0:T(8,128)(2,1)S(1)}, bf16[2,128,1024]{2,1,0:T(8,128)(2,1)S(1)}, u32[]{:S(2)}, u32[]{:S(2)}) collective-permute-start(bf16[2,128,1024]{2,1,0:T(8,128)(2,1)S(1)} %get-tuple-element.26), channel_id=1, source_target_pairs={{0,1},{1,2},{2,3},{3,4},{4,5},{5,6},{6,7},{7,8},{8,9},{9,10},{10,1... | collective-permute-start | bytes 1572872 | tf_op jit(solution)/shard_map/ppermute | solution.py:23
  137.1 6.0 %collective-permute-done.10.a_down_ref = bf16[4,128,1024]{2,1,0:T(8,128)(2,1)S(1)} collective-permute-done((bf16[4,128,1024]{2,1,0:T(8,128)(2,1)S(1)}, bf16[4,128,1024]{2,1,0:T(8,128)(2,1)S(1)}, u32[]{:S(2)}, u32[]{:S(2)}) %collective-permute-start.10) | collective-permute-done | bytes 1048608 | tf_op jit(solution)/shard_map/ppermute | solution.py:23
  143.2 2.1 %collective-permute-start.5 = (bf16[2,128,1024]{2,1,0:T(8,128)(2,1)S(1)}, bf16[2,128,1024]{2,1,0:T(8,128)(2,1)S(1)}, u32[]{:S(2)}, u32[]{:S(2)}) collective-permute-start(bf16[2,128,1024]{2,1,0:T(8,128)(2,1)S(1)} %get-tuple-element.27), channel_id=1, source_target_pairs={{1,0},{2,1},{3,2},{4,3},{5,4},{6,5},{7,6},{8,7},{9,8},{10,9},{11,1... | collective-permute-start | bytes 1572872 | tf_op jit(solution)/shard_map/ppermute | solution.py:23
  145.3 7.0 %shard_map.164.local_ref = f32[768,1024]{1,0:T(8,128)} custom-call(bf16[512,1792]{1,0:T(8,128)(2,1)} %get-tuple-element.24.fold_ref, bf16[512,1024]{1,0:T(8,128)(2,1)S(1)} %copy-done.8, bf16[512,1024]{1,0:T(8,128)(2,1)} %bitcast.24, bf16[1024,1024]{1,0:T(8,128)(2,1)} %w_ref.7, s32[1,512]{1,0:T(1,128)S(1)} %bitcast.15), custom_call_target="tpu_custom_call" | custom-call | flops 2684354560 | bytes 8388608 | tf_op jit(solution)/shard_map/pallas_call | solution.py:382
  152.3 0.0 collective-permute-done.8.a_up_ref
  152.4 1.0 copy-done.13
  153.3 5.0 %shard_map.166 = f32[768,1024]{1,0:T(8,128)} custom-call(f32[768,1024]{1,0:T(8,128)} %shard_map.164.local_ref, bf16[4,128,1024]{2,1,0:T(8,128)(2,1)} %copy-done.13, bf16[2,128,1024]{2,1,0:T(8,128)(2,1)S(1)} %collective-permute-done.9.b_up_ref, bf16[4,128,1024]{2,1,0:T(8,128)(2,1)} %copy-done.12, ...), custom_call_target="tpu_custom_call" | custom-call | bytes 9437184 | tf_op jit(solution)/shard_map/pallas_call | solution.py:406
  158.3 14.3 %collective-permute-done.4.b_up_ref = bf16[2,128,1024]{2,1,0:T(8,128)(2,1)S(1)} collective-permute-done((bf16[2,128,1024]{2,1,0:T(8,128)(2,1)S(1)}, bf16[2,128,1024]{2,1,0:T(8,128)(2,1)S(1)}, u32[]{:S(2)}, u32[]{:S(2)}) %collective-permute-start.4) | collective-permute-done | bytes 524320 | tf_op jit(solution)/shard_map/ppermute | solution.py:23
  172.6 6.2 %collective-permute-done.5.b_down_ref = bf16[2,128,1024]{2,1,0:T(8,128)(2,1)S(1)} collective-permute-done((bf16[2,128,1024]{2,1,0:T(8,128)(2,1)S(1)}, bf16[2,128,1024]{2,1,0:T(8,128)(2,1)S(1)}, u32[]{:S(2)}, u32[]{:S(2)}) %collective-permute-start.5) | collective-permute-done | bytes 524320 | tf_op jit(solution)/shard_map/ppermute | solution.py:23
  178.8 9.1 %shard_map.162 = (f32[512,1024]{1,0:T(8,128)}, f32[512,1024]{1,0:T(8,128)}) custom-call(bf16[512,1792]{1,0:T(8,128)(2,1)} %get-tuple-element.24.fold_ref, bf16[6,128,1024]{2,1,0:T(8,128)(2,1)} %get-tuple-element.25.hid_ref, bf16[4,128,1024]{2,1,0:T(8,128)(2,1)} %copy-done.17, bf16[2,128,1024]{2,1,0:T(8,128)(2,1)S(1)} %collective-permute-done.4.b_up_ref, ...), custom_call_target="tpu_custom_call" | custom-call | flops 3758096384 | bytes 16777216 | tf_op jit(solution)/shard_map/pallas_call | solution.py:390
  187.9 0.0 collective-permute-done.1.f_up_ref
  187.9 0.0 collective-permute-done.3.f_down_ref
  187.9 1.0 copy-done.10
  188.9 0.4 copy-done.11
  189.3 7.1 %shard_map.163 = bf16[512,1024]{1,0:T(8,128)(2,1)} custom-call(bf16[512,1024]{1,0:T(8,128)(2,1)S(1)} %copy-done.2, bf16[4,128,1024]{2,1,0:T(8,128)(2,1)} %copy-done.10, bf16[4,128,1024]{2,1,0:T(8,128)(2,1)} %copy-done.11, s32[5,24]{1,0:T(8,128)S(1)} %pad_dynamic-slice_fusion.meta_ref, f32[512,1024]{1,0:T(8,128)} %get-tuple-element.28.part_ref, ...), custom_call_target="tpu_custom_call" | custom-call | flops 2147483648 | bytes 10485760 | tf_op jit(solution)/shard_map/pallas_call | solution.py:398
  (22 shorter events, 0.1 us)
Async XLA Ops:
  7.2 62.3 %all-gather.4.cloned.1.call-start = ((), (), s32[]{:S(2)}) async-start(), calls=%async_computation.1 | async-start | bytes 3538944 | tf_op jit(solution)/shard_map/all_gather | solution.py:313
  9.8 2.8 %copy-start = (bf16[48,4,128,128]{3,2,1,0:T(8,128)(2,1)S(1)}, bf16[48,4,128,128]{3,2,1,0:T(8,128)(2,1)}, u32[]{:S(2)}) copy-start(bf16[48,4,128,128]{3,2,1,0:T(8,128)(2,1)} %adj_ref.1) | copy-start | bytes 18874372
  12.6 1.3 copy-start.1
  19.7 4.4 %copy-start.5 = (s32[1,1,4,16]{3,2,1,0:T(4,128)S(1)}, s32[1,1,4,16]{3,2,1,0:T(4,128)}, u32[]{:S(2)}) copy-start(s32[1,1,4,16]{3,2,1,0:T(4,128)} %param.26) | copy-start | bytes 772
  19.7 49.7 %all-to-all-start = ((bf16[8,192,768]{2,1,0:T(8,128)(2,1)}), bf16[8,192,768]{2,1,0:T(8,128)(2,1)S(1)}, u32[]{:S(2)}, u32[]{:S(2)}) async-start(bf16[8,192,768]{2,1,0:T(8,128)(2,1)} %shard_map.159), calls=%async_computation | async-start | bytes 4718592 | tf_op jit(solution)/shard_map/all_to_all | solution.py:356
  24.2 14.5 %copy-start.15 = (s32[1,1,4,4]{3,2,1,0:T(4,128)S(1)}, s32[1,1,4,4]{3,2,1,0:T(4,128)}, u32[]{:S(2)}) copy-start(s32[1,1,4,4]{3,2,1,0:T(4,128)} %param.27) | copy-start | bytes 196
  24.2 14.6 %copy-start.18 = (u32[128]{0:T(128)S(1)}, u32[128]{0:T(128)}, u32[]{:S(2)}) copy-start(u32[128]{0:T(128)} %constant.19) | copy-start | bytes 1540
  24.2 15.9 %copy-start.16 = (s32[1,1,4]{2,1,0:T(1,128)S(1)}, s32[1,1,4]{2,1,0:T(1,128)}, u32[]{:S(2)}) copy-start(s32[1,1,4]{2,1,0:T(1,128)} %param.28) | copy-start | bytes 52
  24.2 46.6 %copy-start.3 = (f32[1024]{0:T(1024)S(1)}, f32[1024]{0:T(1024)}, u32[]{:S(2)}) copy-start(f32[1024]{0:T(1024)} %param.20) | copy-start | bytes 12292
  31.9 1.0 copy-start.7
  32.8 68.2 %collective-permute-start.6 = (bf16[4,128,1024]{2,1,0:T(8,128)(2,1)}, bf16[4,128,1024]{2,1,0:T(8,128)(2,1)S(1)}, u32[]{:S(2)}, u32[]{:S(2)}) collective-permute-start(bf16[4,128,1024]{2,1,0:T(8,128)(2,1)} %get-tuple-element.32), channel_id=1, source_target_pairs={{0,1},{1,2},{2,3},{3,4},{4,5},{5,6},{6,7},{7,8},{8,9},{9,10},{10,1... | collective-permute-start | bytes 3145736 | tf_op jit(solution)/shard_map/ppermute | solution.py:23
  34.9 66.2 %collective-permute-start.7 = (bf16[4,128,1024]{2,1,0:T(8,128)(2,1)}, bf16[4,128,1024]{2,1,0:T(8,128)(2,1)}, u32[]{:S(2)}, u32[]{:S(2)}) collective-permute-start(bf16[4,128,1024]{2,1,0:T(8,128)(2,1)} %get-tuple-element.33), channel_id=1, source_target_pairs={{1,0},{2,1},{3,2},{4,3},{5,4},{6,5},{7,6},{8,7},{9,8},{10,9},{11,1... | collective-permute-start | bytes 3145736 | tf_op jit(solution)/shard_map/ppermute | solution.py:23
  69.4 1.4 copy-start.9
  78.4 44.3 %collective-permute-start = (bf16[4,128,1024]{2,1,0:T(8,128)(2,1)}, bf16[4,128,1024]{2,1,0:T(8,128)(2,1)S(1)}, u32[]{:S(2)}, u32[]{:S(2)}) collective-permute-start(bf16[4,128,1024]{2,1,0:T(8,128)(2,1)} %get-tuple-element.21), channel_id=1, source_target_pairs={{0,1},{1,2},{2,3},{3,4},{4,5},{5,6},{6,7},{7,8},{8,9},{9,10},{10,1... | collective-permute-start | bytes 3145736 | tf_op jit(solution)/shard_map/ppermute | solution.py:23
  85.7 43.5 %collective-permute-start.2 = (bf16[4,128,1024]{2,1,0:T(8,128)(2,1)}, bf16[4,128,1024]{2,1,0:T(8,128)(2,1)}, u32[]{:S(2)}, u32[]{:S(2)}) collective-permute-start(bf16[4,128,1024]{2,1,0:T(8,128)(2,1)} %get-tuple-element.22), channel_id=1, source_target_pairs={{1,0},{2,1},{3,2},{4,3},{5,4},{6,5},{7,6},{8,7},{9,8},{10,9},{11,1... | collective-permute-start | bytes 3145736 | tf_op jit(solution)/shard_map/ppermute | solution.py:23
  95.2 25.5 %collective-permute-start.11 = (bf16[2,128,1024]{2,1,0:T(8,128)(2,1)S(1)}, bf16[2,128,1024]{2,1,0:T(8,128)(2,1)S(1)}, u32[]{:S(2)}, u32[]{:S(2)}) collective-permute-start(bf16[2,128,1024]{2,1,0:T(8,128)(2,1)S(1)} %get-tuple-element.37), channel_id=1, source_target_pairs={{0,1},{1,2},{2,3},{3,4},{4,5},{5,6},{6,7},{7,8},{8,9},{9,10},{10,1... | collective-permute-start | bytes 1572872 | tf_op jit(solution)/shard_map/ppermute | solution.py:23
  101.1 1.0 copy-start.14
  102.1 43.2 %copy-start.6 = (s32[1,1,512]{2,1,0:T(1,128)S(1)}, s32[1,1,512]{2,1,0:T(1,128)}, u32[]{:S(2)}) copy-start(s32[1,1,512]{2,1,0:T(1,128)} %param.24) | copy-start | bytes 6148
  102.1 43.2 %copy-start.8 = (bf16[512,1024]{1,0:T(8,128)(2,1)S(1)}, bf16[512,1024]{1,0:T(8,128)(2,1)}, u32[]{:S(2)}) copy-start(bf16[512,1024]{1,0:T(8,128)(2,1)} %copy-done.7) | copy-start | bytes 3145732
  106.8 36.4 %collective-permute-start.10 = (bf16[4,128,1024]{2,1,0:T(8,128)(2,1)S(1)}, bf16[4,128,1024]{2,1,0:T(8,128)(2,1)S(1)}, u32[]{:S(2)}, u32[]{:S(2)}) collective-permute-start(bf16[4,128,1024]{2,1,0:T(8,128)(2,1)S(1)} %get-tuple-element.36), channel_id=1, source_target_pairs={{0,1},{1,2},{2,3},{3,4},{4,5},{5,6},{6,7},{7,8},{8,9},{9,10},{10,1... | collective-permute-start | bytes 3145736 | tf_op jit(solution)/shard_map/ppermute | solution.py:23
  108.7 22.4 %collective-permute-start.9 = (bf16[2,128,1024]{2,1,0:T(8,128)(2,1)S(1)}, bf16[2,128,1024]{2,1,0:T(8,128)(2,1)S(1)}, u32[]{:S(2)}, u32[]{:S(2)}) collective-permute-start(bf16[2,128,1024]{2,1,0:T(8,128)(2,1)S(1)} %get-tuple-element.35), channel_id=1, source_target_pairs={{1,0},{2,1},{3,2},{4,3},{5,4},{6,5},{7,6},{8,7},{9,8},{10,9},{11,1... | collective-permute-start | bytes 1572872 | tf_op jit(solution)/shard_map/ppermute | solution.py:23
  120.7 31.6 %collective-permute-start.8 = (bf16[4,128,1024]{2,1,0:T(8,128)(2,1)}, bf16[4,128,1024]{2,1,0:T(8,128)(2,1)S(1)}, u32[]{:S(2)}, u32[]{:S(2)}) collective-permute-start(bf16[4,128,1024]{2,1,0:T(8,128)(2,1)} %get-tuple-element.34), channel_id=1, source_target_pairs={{1,0},{2,1},{3,2},{4,3},{5,4},{6,5},{7,6},{8,7},{9,8},{10,9},{11,1... | collective-permute-start | bytes 3145736 | tf_op jit(solution)/shard_map/ppermute | solution.py:23
  122.6 29.7 %copy-start.17 = (bf16[4,128,1024]{2,1,0:T(8,128)(2,1)}, bf16[4,128,1024]{2,1,0:T(8,128)(2,1)S(1)}, u32[]{:S(2)}) copy-start(bf16[4,128,1024]{2,1,0:T(8,128)(2,1)S(1)} %collective-permute-done.a_up_ref) | copy-start | bytes 3145732
  122.6 65.3 %collective-permute-start.1 = (bf16[4,128,1024]{2,1,0:T(8,128)(2,1)S(1)}, bf16[4,128,1024]{2,1,0:T(8,128)(2,1)S(1)}, u32[]{:S(2)}, u32[]{:S(2)}) collective-permute-start(bf16[4,128,1024]{2,1,0:T(8,128)(2,1)S(1)} %collective-permute-done.a_up_ref), channel_id=1, source_target_pairs={{0,1},{1,2},{2,3},{3,4},{4,5},{5,6},{6,7},{7,8},{8,9},{9,10},{10,1... | collective-permute-start | bytes 3145736 | tf_op jit(solution)/shard_map/ppermute | solution.py:23
  129.2 58.7 %collective-permute-start.3 = (bf16[4,128,1024]{2,1,0:T(8,128)(2,1)}, bf16[4,128,1024]{2,1,0:T(8,128)(2,1)S(1)}, u32[]{:S(2)}, u32[]{:S(2)}) collective-permute-start(bf16[4,128,1024]{2,1,0:T(8,128)(2,1)} %collective-permute-done.2.a_down_ref), channel_id=1, source_target_pairs={{1,0},{2,1},{3,2},{4,3},{5,4},{6,5},{7,6},{8,7},{9,8},{10,9},{11,1... | collective-permute-start | bytes 3145736 | tf_op jit(solution)/shard_map/ppermute | solution.py:23
  131.1 41.5 %collective-permute-start.4 = (bf16[2,128,1024]{2,1,0:T(8,128)(2,1)S(1)}, bf16[2,128,1024]{2,1,0:T(8,128)(2,1)S(1)}, u32[]{:S(2)}, u32[]{:S(2)}) collective-permute-start(bf16[2,128,1024]{2,1,0:T(8,128)(2,1)S(1)} %get-tuple-element.26), channel_id=1, source_target_pairs={{0,1},{1,2},{2,3},{3,4},{4,5},{5,6},{6,7},{7,8},{8,9},{9,10},{10,1... | collective-permute-start | bytes 1572872 | tf_op jit(solution)/shard_map/ppermute | solution.py:23
  143.2 9.2 %copy-start.12 = (bf16[4,128,1024]{2,1,0:T(8,128)(2,1)}, bf16[4,128,1024]{2,1,0:T(8,128)(2,1)S(1)}, u32[]{:S(2)}) copy-start(bf16[4,128,1024]{2,1,0:T(8,128)(2,1)S(1)} %collective-permute-done.10.a_down_ref) | copy-start | bytes 3145732
  143.2 35.7 %collective-permute-start.5 = (bf16[2,128,1024]{2,1,0:T(8,128)(2,1)S(1)}, bf16[2,128,1024]{2,1,0:T(8,128)(2,1)S(1)}, u32[]{:S(2)}, u32[]{:S(2)}) collective-permute-start(bf16[2,128,1024]{2,1,0:T(8,128)(2,1)S(1)} %get-tuple-element.27), channel_id=1, source_target_pairs={{1,0},{2,1},{3,2},{4,3},{5,4},{6,5},{7,6},{8,7},{9,8},{10,9},{11,1... | collective-permute-start | bytes 1572872 | tf_op jit(solution)/shard_map/ppermute | solution.py:23
  152.3 26.5 %copy-start.4 = (f32[1024]{0:T(1024)S(1)}, f32[1024]{0:T(1024)}, u32[]{:S(2)}) copy-start(f32[1024]{0:T(1024)} %param.23) | copy-start | bytes 12292
  152.3 1.0 copy-start.13
  178.8 10.4 %copy-start.2 = (bf16[512,1024]{1,0:T(8,128)(2,1)S(1)}, bf16[512,1024]{1,0:T(8,128)(2,1)}, u32[]{:S(2)}) copy-start(bf16[512,1024]{1,0:T(8,128)(2,1)} %get-tuple-element.20.fold_ref) | copy-start | bytes 3145732
  187.9 1.0 copy-start.10
  187.9 1.4 copy-start.11
Sparse Core Ops, SparseCore 0:
  9.7 40.5 all-gather.3

commit v2 on v1

v2 whole, which is shorter than its diff:
```python
import functools

import jax
import jax.numpy as jnp
from jax import lax
from jax.experimental import pallas as pl
from jax.experimental.pallas import tpu as pltpu
from jax.sharding import PartitionSpec as P

TILE = 128
TILE_DEV = 6
SLOTS = 4
NEAR = 4
ROWS = 8
MIB = 1 << 20
OFFSETS = (-2, -1, 1, 2)
GIGA = 1 << 30

VMEM = pl.BlockSpec(memory_space=pltpu.VMEM)
SMEM = pl.BlockSpec(memory_space=pltpu.SMEM)
ANY = pl.BlockSpec(memory_space=pl.ANY)


def shifted(shard, by):
    count = lax.axis_size("dom")
    return lax.ppermute(shard, "dom", [(i, (i + by) % count) for i in range(count)])


def call(body, outs, in_specs, scratch=(), cost=1, vmem=32):
    return pl.pallas_call(
        body,
        out_shape=outs,
        in_specs=in_specs,
        out_specs=jax.tree.map(lambda _: VMEM, outs),
        scratch_shapes=list(scratch),
        cost_estimate=pl.CostEstimate(flops=cost * GIGA, bytes_accessed=1, transcendentals=0),
        compiler_params=pltpu.CompilerParams(vmem_limit_bytes=vmem * MIB),
    )


def tn_dot(left, right):
    return lax.dot_general(left, right, (((0,), (0,)), ((), ())), preferred_element_type=jnp.float32)


def nt_dot(left, right):
    return lax.dot_general(left, right, (((1,), (1,)), ((), ())), preferred_element_type=jnp.float32)


def nn_dot(left, right):
    return jnp.dot(left, right, preferred_element_type=jnp.float32)


def order_of(tiles, count):
    listed = []
    for tile in range(TILE_DEV):
        hit = jnp.int32(0)
        for slot in range(SLOTS):
            hit = jnp.where((tiles(slot) == tile) & (slot < count), 1, hit)
        listed.append(hit)
    total = functools.reduce(lambda a, b: a + b, listed)
    places = []
    ahead = jnp.int32(0)
    behind = total
    for tile in range(TILE_DEV):
        places.append(jnp.where(listed[tile] == 1, ahead, behind))
        ahead = ahead + listed[tile]
        behind = behind + (1 - listed[tile])
    return places


def place_of(places, tile):
    at = places[0]
    for other in range(1, TILE_DEV):
        at = jnp.where(tile == other, places[other], at)
    return at


def halves_kernel(self_ref, neigh_ref, out_ref, sems):
    copies = [
        pltpu.make_async_copy((self_ref, neigh_ref)[i % 2], out_ref.at[i], sems.at[i]) for i in range(out_ref.shape[0])
    ]
    for copy in copies:
        copy.start()
    for copy in copies:
        copy.wait()


def far_kernel(
    adj_ref, src_ref, cot_ref, w_ref, after_ref,
    back_ref, fold_ref, up_ref, down_ref, adj_buf, cot_buf, w_buf, acc_ref, sems,
):
    seeds = adj_ref.shape[0]
    loads = [pltpu.make_async_copy(adj_ref.at[s], adj_buf.at[s], sems.at[s]) for s in range(seeds)]
    load_w = pltpu.make_async_copy(w_ref, w_buf, sems.at[seeds])
    load_cot = pltpu.make_async_copy(cot_ref, cot_buf, sems.at[seeds + 1])
    for load in loads:
        load.start()
    load_cot.start()
    load_w.start()
    acc_ref[...] = jnp.zeros_like(acc_ref)
    for seed in range(seeds):
        loads[seed].wait()
        rows = pl.ds(seed * TILE, TILE)

        def add(k, _):
            slot = src_ref[seed, k] - TILE_DEV
            low = (slot >= 0) & (slot < SLOTS)
            high = slot >= 3 * SLOTS

            @pl.when(low | high)
            def _():
                at = jnp.where(low, slot, slot - 2 * SLOTS)
                cols = pl.ds(pl.multiple_of(at * TILE, TILE), TILE)
                acc_ref[rows, cols] += adj_buf[seed, k].astype(jnp.float32)

            return 0

        lax.fori_loop(0, adj_ref.shape[1], add, 0, unroll=4)
    fold_ref[...] = acc_ref[...].astype(jnp.bfloat16)
    load_cot.wait()
    load_w.wait()
    back = nt_dot(cot_buf[...], w_buf[...]).astype(jnp.bfloat16)
    back_ref[...] = back
    half = SLOTS * TILE
    up_ref[...] = tn_dot(fold_ref[:, :half], back).astype(jnp.bfloat16).reshape(up_ref.shape)
    down_ref[...] = tn_dot(fold_ref[:, half:], back).astype(jnp.bfloat16).reshape(down_ref.shape)


def near_kernel(adj_ref, src_ref, back_ref, after_ref, fold_ref, up_ref, down_ref, acc_ref):
    acc_ref[...] = jnp.zeros_like(acc_ref)
    for seed in range(adj_ref.shape[0]):
        rows = pl.ds(seed * TILE, TILE)

        def add(k, _):
            slot = src_ref[seed, k]
            local = slot < TILE_DEV
            near = (slot >= TILE_DEV + SLOTS) & (slot < TILE_DEV + 3 * SLOTS)

            @pl.when(local | near)
            def _():
                at = jnp.where(local, slot, slot - SLOTS)
                cols = pl.ds(pl.multiple_of(at * TILE, TILE), TILE)
                acc_ref[rows, cols] += adj_ref[seed, k].astype(jnp.float32)

            return 0

        lax.fori_loop(0, adj_ref.shape[1], add, 0, unroll=4)
    fold_ref[...] = acc_ref[...].astype(jnp.bfloat16)
    back = back_ref[...]
    start, half = TILE_DEV * TILE, SLOTS * TILE
    up_ref[...] = tn_dot(fold_ref[:, start : start + half], back).astype(jnp.bfloat16).reshape(up_ref.shape)
    down_ref[...] = tn_dot(fold_ref[:, start + half :], back).astype(jnp.bfloat16).reshape(down_ref.shape)


def local_kernel(fold_ref, back_ref, cot_ref, w_ref, seeds_ref, after_up_ref, after_down_ref, out_ref):
    rows = out_ref.shape[0]
    back_self = nt_dot(cot_ref[...], w_ref[...]).astype(jnp.bfloat16)
    hot = lax.broadcasted_iota(jnp.int32, (rows, seeds_ref.shape[1]), 0) == seeds_ref[...]
    hot = hot.astype(jnp.float32).astype(jnp.bfloat16)
    out_ref[...] = nn_dot(hot, back_self) + tn_dot(fold_ref[:, :rows], back_ref[...])


def gather_kernel(src_ref, feat_ref, adj_ref, after_ref, out_ref):
    step = pl.program_id(0)
    width = feat_ref.shape[0]
    span = out_ref.shape[2]
    out_ref[0, :width] = feat_ref[:, pl.ds(pl.multiple_of(step * span, span), span)]
    for tile in range(adj_ref.shape[0]):
        parts = []
        for k in range(adj_ref.shape[1]):
            source = src_ref[k, step * adj_ref.shape[0] + tile]
            parts.append(feat_ref[:, pl.ds(pl.multiple_of(source * TILE, TILE), TILE)])
        left = jnp.concatenate(parts, axis=1)
        right = jnp.concatenate([adj_ref[tile, k] for k in range(adj_ref.shape[1])], axis=1)
        out_ref[0, width:, tile * TILE : (tile + 1) * TILE] = nt_dot(left, right).astype(jnp.bfloat16)


def hidden_kernel(
    in_ref, mine_ref, other_ref, bias_ref, odd_ref, tiles_ref, count_ref, after_ref,
    hid_ref, up_ref, down_ref, turned_ref, w_ref,
):
    slices, width, span = in_ref.shape[0], in_ref.shape[1] // 2, in_ref.shape[2]
    depth = slices * width

    @pl.when(pl.program_id(0) == 0)
    def _():
        turned_ref[:, :depth] = in_ref[:, :width].reshape(depth, span).T
        turned_ref[:, depth:] = in_ref[:, width:].reshape(depth, span).T

    w_ref[pl.ds(pl.multiple_of(odd_ref[0] * depth, depth), depth)] = mine_ref[...]
    w_ref[pl.ds(pl.multiple_of((1 - odd_ref[0]) * depth, depth), depth)] = other_ref[...]
    total = nn_dot(turned_ref[...], w_ref[...])
    hidden = jnp.maximum(total + bias_ref[...], 0.0).astype(jnp.bfloat16)
    hid_ref[...] = hidden.reshape(hid_ref.shape)
    shape = (2 * ROWS, up_ref.shape[1])
    row = lax.broadcasted_iota(jnp.int32, shape, 0)
    block = (lax.broadcasted_iota(jnp.int32, shape, 1) + pl.program_id(0) * shape[1]) // TILE
    for near_q, far_q, out_ref in ((2, 3, up_ref), (1, 0, down_ref)):
        places = order_of(lambda m: tiles_ref[far_q, m], count_ref[far_q])
        for tile in range(TILE_DEV):

            @pl.when(places[tile] < NEAR)
            def _():
                at = jnp.minimum(places[tile], NEAR - 1) * TILE
                out_ref[pl.ds(pl.multiple_of(at, TILE), TILE)] = hid_ref[tile]

        marks = jnp.zeros(shape, jnp.float32)
        for first, q in ((0, near_q), (SLOTS, far_q)):
            for slot in range(SLOTS):
                at = jnp.where(slot < count_ref[q], place_of(places, tiles_ref[q, slot]), -1)
                marks = jnp.where((row == first + slot) & (block == at), 1.0, marks)
        out_ref[NEAR * TILE :] = marks.astype(jnp.bfloat16)


def merge_kernel(
    local_ref, from_0_ref, from_1_ref, from_2_ref, from_3_ref, hid_ref, tiles_ref, count_ref,
    out_ref, rest_up_ref, rest_down_ref,
):
    out_ref[...] = local_ref[...]
    for q, ref in enumerate((from_0_ref, from_1_ref, from_2_ref, from_3_ref)):
        for slot in range(SLOTS):

            @pl.when(slot < count_ref[q])
            def _():
                at = pl.multiple_of(tiles_ref[q, slot] * TILE, TILE)
                out_ref[pl.ds(at, TILE)] += ref[slot].astype(jnp.float32)

    for far_q, rest_ref in ((3, rest_up_ref), (0, rest_down_ref)):
        places = order_of(lambda m: tiles_ref[far_q, m], count_ref[far_q])
        for tile in range(TILE_DEV):

            @pl.when(places[tile] >= NEAR)
            def _():
                rest_ref[jnp.maximum(places[tile] - NEAR, 0)] = hid_ref[tile]


def placed(fold_ref, start, mark_ref, first, count, out_ref, to):
    marks = mark_ref[NEAR * TILE :].astype(jnp.float32)
    blocks = [
        fold_ref[:, (start + slot) * TILE : (start + slot + 1) * TILE].astype(jnp.float32) for slot in range(SLOTS)
    ]
    for place in range(count):
        cols = slice(place * TILE, (place + 1) * TILE)
        total = sum(blocks[slot] * marks[first + slot : first + slot + 1, cols] for slot in range(SLOTS))
        out_ref[:, (to + place) * TILE : (to + place + 1) * TILE] = total.astype(jnp.bfloat16)


def mid_kernel(
    fold_ref, hid_ref, a_up_ref, rest_up_ref, a_down_ref, rest_down_ref, seeds_ref, w_ref, bias_ref,
    part_ref, self_ref, placed_ref, table_ref,
):
    rows = TILE_DEV * TILE
    quad = NEAR * TILE
    pair = rows - quad
    hidden = hid_ref[...].reshape(rows, hid_ref.shape[2])
    start = 0
    for first, a_ref, rest_ref in ((TILE_DEV, a_down_ref, rest_down_ref), (TILE_DEV + SLOTS, a_up_ref, rest_up_ref)):
        placed(fold_ref, first, a_ref, 0, TILE_DEV, placed_ref, start // TILE)
        table_ref[start : start + quad] = a_ref[:quad]
        table_ref[start + quad : start + rows] = rest_ref[...].reshape(pair, rest_ref.shape[2])
        start += rows
    part_ref[...] = nn_dot(fold_ref[:, :rows], hidden) + nn_dot(placed_ref[...], table_ref[...])
    hot = lax.broadcasted_iota(jnp.int32, (rows, seeds_ref.shape[1]), 0) == seeds_ref[...]
    hot = hot.astype(jnp.float32).astype(jnp.bfloat16)
    chosen = tn_dot(hot, hidden).astype(jnp.bfloat16)
    self_ref[...] = nn_dot(chosen, w_ref[...]) + bias_ref[...]


def last_kernel(fold_ref, f_up_ref, f_down_ref, part_ref, self_ref, w_ref, out_ref, placed_ref):
    quad = NEAR * TILE
    placed(fold_ref, 0, f_down_ref, SLOTS, NEAR, placed_ref, 0)
    placed(fold_ref, SLOTS, f_up_ref, SLOTS, NEAR, placed_ref, NEAR)
    gathered = part_ref[...] + nn_dot(placed_ref[:, :quad], f_down_ref[:quad])
    gathered = (gathered + nn_dot(placed_ref[:, quad:], f_up_ref[:quad])).astype(jnp.bfloat16)
    out_ref[...] = (self_ref[...] + nn_dot(gathered, w_ref[...])).astype(jnp.bfloat16)


def shards(
    features,
    adj_one,
    src_one,
    w_self_one,
    w_neigh_one,
    bias_one,
    w_self_two,
    w_neigh_two,
    bias_two,
    seed_rows,
    adj_two,
    src_two,
    send_tiles,
    send_count,
    cotangent,
):
    bf16, f32 = jnp.bfloat16, jnp.float32
    width = features.shape[0]
    part_tiles = adj_one.shape[0]
    hid = w_self_two.shape[0]
    feat_count = lax.axis_size("feat")
    row_dev = features.shape[1] // feat_count
    seeds = cotangent.shape[1]
    blocks, sources = adj_two[0, 0], src_two[0, 0]
    upstream = cotangent[0]
    shape = jax.ShapeDtypeStruct

    lists = send_tiles[0, 0]
    partner = lax.axis_index("dom") + jnp.array(OFFSETS, jnp.int32)
    inside = (partner >= 0) & (partner < lax.axis_size("dom"))
    counts = jnp.where(inside, send_count[0, 0], 0)
    quad = shape((NEAR, TILE, hid), bf16)
    pair = shape((TILE_DEV - NEAR, TILE, hid), bf16)
    quad_marked = shape((NEAR * TILE + 2 * ROWS, hid), bf16)
    far_cols, near_cols = 2 * SLOTS * TILE, (TILE_DEV + 2 * SLOTS) * TILE

    halves = call(
        halves_kernel,
        shape((feat_count, width, hid), bf16),
        [ANY, ANY],
        [pltpu.SemaphoreType.DMA((feat_count,))],
        vmem=56,
    )(w_self_one, w_neigh_one)
    back, fold_far, far_up, far_down = call(
        far_kernel,
        (shape((seeds, hid), bf16), shape((seeds, far_cols), bf16), quad, quad),
        [ANY, SMEM, ANY, ANY, ANY],
        [
            pltpu.VMEM(blocks.shape, bf16),
            pltpu.VMEM((seeds, hid), bf16),
            pltpu.VMEM((hid, hid), bf16),
            pltpu.VMEM((seeds, far_cols), f32),
            pltpu.SemaphoreType.DMA((blocks.shape[0] + 2,)),
        ],
        vmem=56,
            )(blocks, sources, upstream, w_neigh_two, halves)
    got_far_up = shifted(far_up, 1)
    got_far_down = shifted(far_down, -1)

    sent = pl.pallas_call(
        gather_kernel,
        grid=(feat_count,),
        in_specs=[
            SMEM,
            pl.BlockSpec((width, features.shape[1]), lambda i: (0, 0)),
            pl.BlockSpec((part_tiles // feat_count,) + adj_one.shape[1:], lambda i: (i, 0, 0, 0)),
            ANY,
        ],
        out_specs=pl.BlockSpec((1, 2 * width, row_dev), lambda i: (i, 0, 0)),
        out_shape=shape((feat_count, 2 * width, row_dev), bf16),
        cost_estimate=pl.CostEstimate(flops=100 * GIGA, bytes_accessed=1, transcendentals=0),
        compiler_params=pltpu.CompilerParams(vmem_limit_bytes=56 * MIB),
    )(src_one.T, features, adj_one, back)
    taken = lax.all_to_all(sent, "feat", 0, 0)
    halves = lax.all_to_all(halves, "feat", 0, 0)
    halves = halves.reshape(feat_count * width, hid)
    swapped = lax.ppermute(halves, "feat", [(i, i ^ 1) for i in range(feat_count)])
    odd = (lax.axis_index("feat") % 2).astype(jnp.int32)[None]

    fold_near, near_up, near_down = call(
        near_kernel,
        (shape((seeds, near_cols), bf16), quad, quad),
        [VMEM, SMEM, VMEM, ANY],
        [pltpu.VMEM((seeds, near_cols), f32)],
        vmem=24,
    )(blocks, sources, back, sent)
    grad_1 = shifted(near_up, 1)
    grad_2 = shifted(near_down, -1)
    grad_0 = shifted(got_far_up, 1)
    grad_3 = shifted(got_far_down, -1)

    local = call(
        local_kernel,
        shape((row_dev, hid), f32),
        [VMEM] * 5 + [ANY] * 2,
        cost=20,
        vmem=28,
    )(fold_near, back, upstream, w_self_two, seed_rows[0], got_far_up, got_far_down)

    chunk = hid // 4
    hidden, h_up, h_down = pl.pallas_call(
        hidden_kernel,
        grid=(hid // chunk,),
        in_specs=[
            pl.BlockSpec(taken.shape, lambda j: (0, 0, 0)),
            pl.BlockSpec((feat_count * width, chunk), lambda j: (0, j)),
            pl.BlockSpec((feat_count * width, chunk), lambda j: (0, j)),
            pl.BlockSpec((1, chunk), lambda j: (0, j)),
            SMEM,
            SMEM,
            SMEM,
            ANY,
        ],
        out_specs=[
            pl.BlockSpec((TILE_DEV, TILE, chunk), lambda j: (0, 0, j)),
            pl.BlockSpec((quad_marked.shape[0], chunk), lambda j: (0, j)),
            pl.BlockSpec((quad_marked.shape[0], chunk), lambda j: (0, j)),
        ],
        out_shape=(shape((TILE_DEV, TILE, hid), bf16), quad_marked, quad_marked),
        scratch_shapes=[
            pltpu.VMEM((row_dev, 2 * width * feat_count), bf16),
            pltpu.VMEM((2 * width * feat_count, chunk), bf16),
        ],
        cost_estimate=pl.CostEstimate(flops=GIGA, bytes_accessed=1, transcendentals=0),
        compiler_params=pltpu.CompilerParams(vmem_limit_bytes=24 * MIB),
    )(taken, halves, swapped, bias_one[None], odd, lists, counts, local)
    got_h_up = shifted(h_up, 1)
    got_h_down = shifted(h_down, -1)
    next_up = shifted(got_h_up, 1)
    next_down = shifted(got_h_down, -1)
    grads, rest_up, rest_down = call(
        merge_kernel, (shape((row_dev, hid), f32), pair, pair), [VMEM] * 6 + [SMEM] * 2, vmem=24
    )(local, grad_0, grad_1, grad_2, grad_3, hidden, lists, counts)
    got_rest_up = shifted(rest_up, 1)
    got_rest_down = shifted(rest_down, -1)

    part, self_term = call(
        mid_kernel,
        (shape((seeds, hid), f32), shape((seeds, hid), f32)),
        [VMEM] * 9,
        [pltpu.VMEM((seeds, 2 * row_dev), bf16), pltpu.VMEM((2 * row_dev, hid), bf16)],
        cost=100,
        vmem=32,
    )(
        fold_near, hidden, got_h_up, got_rest_up, got_h_down, got_rest_down,
        seed_rows[0], w_self_two, bias_two[None],
    )
    layer_out = call(
        last_kernel,
        shape((seeds, hid), bf16),
        [VMEM] * 6,
        [pltpu.VMEM((seeds, far_cols), bf16)],
        vmem=20,
    )(fold_far, next_up, next_down, part, self_term, w_neigh_two)
    return (layer_out[None], grads[None])


def solution(mesh):
    return jax.shard_map(
        shards,
        mesh=mesh,
        in_specs=(
            P("feat", "dom"),
            P("dom", None, None, None),
            P("dom", None),
            P("feat", None),
            P("feat", None),
            P(),
            P(),
            P(),
            P(),
            P("dom", "feat", None),
            P("dom", "feat", None, None, None, None),
            P("dom", "feat", None, None),
            P("dom", "feat", None, None),
            P("dom", "feat", None),
            P("dom", "feat", None),
        ),
        out_specs=(P("dom", "feat", None), P("dom", "feat", None)),
        check_vma=False,
    )
```

time: 205 us -> 153 us (0.75)
  the two profiles are of different devices: /device:TPU:104 before, /device:TPU:1 now
where the time goes in v2:
time: 153 us; the launch traced here: 152 us
  waiting for transfers between devices  55.2 us (36%)
  Pallas kernels  46.5 us (30%)
  starting transfers between devices  42.8 us (28%)
  local copies, waits for them, and re-layouts  6.84 us (4%)
    ppermute x12, waiting for transfers between devices, shifted(): lax.ppermute(shard, 'dom', [(i, (i + by) % count) for i in range(count)])  39.9 us
    ppermute x12, starting transfers between devices, shifted(): lax.ppermute(shard, 'dom', [(i, (i + by) % count) for i in range(count)])  30.6 us
    all_to_all x1, waiting for transfers between devices, shards(): taken = lax.all_to_all(sent, 'feat', 0, 0)  15.3 us
    pallas_call x1, Pallas kernels, shards(): pl.pallas_call(gather_kernel, grid=(feat_count,), in_specs=[SMEM, pl.Bloc...  8.54 us
    pallas_call x1, Pallas kernels, shards(): pl.pallas_call(hidden_kernel, grid=(hid // chunk,), in_specs=[pl.BlockSpe...  7.47 us
    unnamed x36, local copies, waits for them, and re-layouts  6.84 us
    pallas_call x1, Pallas kernels, shards(): call(far_kernel, (shape((seeds, hid), bf16), shape((seeds, far_cols), bf1...  6.67 us
    all_to_all x1, starting transfers between devices, shards(): taken = lax.all_to_all(sent, 'feat', 0, 0)  5.83 us
  transfers between devices with their start and end apart: 15, of which 5 were waited for; matrix products, arithmetic and copies ran while one was open for 0% of the time, Pallas kernels for 26%

profile of v2, /device:TPU:1, one launch (start us, length us, event | category | flops | bytes accessed | tf_op | source)
XLA Modules:
  0.0 152.1 jit_solution(2736045411901136309)
XLA Ops:
  0.6 3.0 %shard_map.167.after_ref = bf16[8,96,1024]{2,1,0:T(8,128)(2,1)} custom-call(bf16[96,1024]{1,0:T(8,128)(2,1)} %self_ref.1, bf16[96,1024]{1,0:T(8,128)(2,1)} %neigh_ref.1), custom_call_target="tpu_custom_call" | custom-call | flops 1073741824 | bytes 1 | tf_op jit(solution)/shard_map/pallas_call | solution.py:315
  3.6 5.8 %all-to-all-start.1 = ((bf16[8,96,1024]{2,1,0:T(8,128)(2,1)}), bf16[8,96,1024]{2,1,0:T(8,128)(2,1)}, u32[]{:S(2)}, u32[]{:S(2)}) async-start(bf16[8,96,1024]{2,1,0:T(8,128)(2,1)} %shard_map.167.after_ref), calls=%async_computation.1 | async-start | bytes 3145728 | tf_op jit(solution)/shard_map/all_to_all | solution.py:353
  9.4 6.7 %shard_map.168 = (bf16[512,1024]{1,0:T(8,128)(2,1)}, bf16[512,1024]{1,0:T(8,128)(2,1)}, bf16[4,128,1024]{2,1,0:T(8,128)(2,1)}, bf16[4,128,1024]{2,1,0:T(8,128)(2,1)}) custom-call(bf16[4,16,128,128]{3,2,1,0:T(8,128)(2,1)} %bitcast.14, s32[4,16]{1,0:T(4,128)} %bitcast.18, bf16[512,1024]{1,0:T(8,128)(2,1)} %bitcast.16, bf16[1024,1024]{1,0:T(8,128)(2,1)} %w_ref.7, ...), custom_call_target="tpu_custom_call" | custom-call | flops 1073741824 | bytes 1 | tf_op jit(solution)/shard_map/pallas_call | solution.py:322
  16.1 1.7 %collective-permute-start.1 = (bf16[4,128,1024]{2,1,0:T(8,128)(2,1)}, bf16[4,128,1024]{2,1,0:T(8,128)(2,1)}, u32[]{:S(2)}, u32[]{:S(2)}) collective-permute-start(bf16[4,128,1024]{2,1,0:T(8,128)(2,1)} %get-tuple-element.20), channel_id=1, source_target_pairs={{0,1},{1,2},{2,3},{3,4},{4,5},{5,6},{6,7},{7,8},{8,9},{9,10},{10,1... | collective-permute-start | bytes 3145736 | tf_op jit(solution)/shard_map/ppermute | solution.py:26
  17.8 4.6 %collective-permute-start.2 = (bf16[4,128,1024]{2,1,0:T(8,128)(2,1)}, bf16[4,128,1024]{2,1,0:T(8,128)(2,1)}, u32[]{:S(2)}, u32[]{:S(2)}) collective-permute-start(bf16[4,128,1024]{2,1,0:T(8,128)(2,1)} %get-tuple-element.21), channel_id=1, source_target_pairs={{0,15},{1,0},{2,1},{3,2},{4,3},{5,4},{6,5},{7,6},{8,7},{9,8},{10,9... | collective-permute-start | bytes 3145736 | tf_op jit(solution)/shard_map/ppermute | solution.py:26
  22.4 0.0 copy-start
  22.4 0.0 copy-start.4
  22.5 0.0 copy-start.6
  22.5 8.5 %shard_map.169.after_ref = bf16[8,192,768]{2,1,0:T(8,128)(2,1)} custom-call(s32[4,48]{1,0:T(4,128)} %bitcast.28, bf16[96,6144]{1,0:T(8,128)(2,1)} %feat_ref.1, bf16[48,4,128,128]{3,2,1,0:T(8,128)(2,1)} %adj_ref.1, bf16[512,1024]{1,0:T(8,128)(2,1)} %get-tuple-element.18.after_ref.back_ref), custom_call_target="tpu_custom_call" | custom-call | flops 107374182400 | bytes 1 | tf_op jit(solution)/shard_map/pallas_call | solution.py:338
  31.0 0.0 copy-done
  31.0 0.0 copy-done.4
  31.0 0.0 copy-done.6
  31.0 4.4 %shard_map.170 = (bf16[512,1792]{1,0:T(8,128)(2,1)S(1)}, bf16[4,128,1024]{2,1,0:T(8,128)(2,1)}, bf16[4,128,1024]{2,1,0:T(8,128)(2,1)}) custom-call(bf16[4,16,128,128]{3,2,1,0:T(8,128)(2,1)S(1)} %bitcast.15, s32[4,16]{1,0:T(4,128)S(1)} %bitcast.19, bf16[512,1024]{1,0:T(8,128)(2,1)S(1)} %copy-done.4, bf16[8,192,768]{2,1,0:T(8,128)(2,1)} %shard_map.169.after_ref), custom_call_target="tpu_custom_call" | custom-call | flops 1073741824 | bytes 1 | tf_op jit(solution)/shard_map/pallas_call | solution.py:358
  35.4 0.0 copy-start.11
  35.4 1.2 copy-done.11
  36.6 0.0 collective-permute-start.8
  36.6 4.8 %collective-permute-start.9 = (bf16[4,128,1024]{2,1,0:T(8,128)(2,1)}, bf16[4,128,1024]{2,1,0:T(8,128)(2,1)}, u32[]{:S(2)}, u32[]{:S(2)}) collective-permute-start(bf16[4,128,1024]{2,1,0:T(8,128)(2,1)} %get-tuple-element.26), channel_id=1, source_target_pairs={{0,15},{1,0},{2,1},{3,2},{4,3},{5,4},{6,5},{7,6},{8,7},{9,8},{10,9... | collective-permute-start | bytes 3145736 | tf_op jit(solution)/shard_map/ppermute | solution.py:26
  41.4 0.0 copy-start.16
  41.4 0.0 all-to-all-done.1
  41.4 5.8 %all-to-all-start = ((bf16[8,192,768]{2,1,0:T(8,128)(2,1)}), bf16[8,192,768]{2,1,0:T(8,128)(2,1)}, u32[]{:S(2)}, u32[]{:S(2)}) async-start(bf16[8,192,768]{2,1,0:T(8,128)(2,1)} %shard_map.169.after_ref), calls=%async_computation | async-start | bytes 4718592 | tf_op jit(solution)/shard_map/all_to_all | solution.py:352
  47.3 0.0 copy-done.16
  47.3 0.0 copy-done.17
  47.3 0.0 collective-permute-done.1.after_up_ref
  47.3 0.1 collective-permute-start.7
  47.4 0.0 collective-permute-done.2.after_down_ref
  47.4 4.8 %collective-permute-start.10 = (bf16[4,128,1024]{2,1,0:T(8,128)(2,1)}, bf16[4,128,1024]{2,1,0:T(8,128)(2,1)}, u32[]{:S(2)}, u32[]{:S(2)}) collective-permute-start(bf16[4,128,1024]{2,1,0:T(8,128)(2,1)} %collective-permute-done.2.after_down_ref), channel_id=1, source_target_pairs={{0,15},{1,0},{2,1},{3,2},{4,3},{5,4},{6,5},{7,6},{8,7},{9,8},{10,9... | collective-permute-start | bytes 3145736 | tf_op jit(solution)/shard_map/ppermute | solution.py:26
  52.2 0.6 collective-permute-start
  52.7 0.0 copy-done.15
  52.7 1.2 copy-done.2
  54.0 1.2 copy-done.5
  55.2 1.6 %copy-done.9 = bf16[1024,1024]{1,0:T(8,128)(2,1)S(1)} copy-done((bf16[1024,1024]{1,0:T(8,128)(2,1)S(1)}, bf16[1024,1024]{1,0:T(8,128)(2,1)}, u32[]{:S(2)}) %copy-start.9) | copy-done | bytes 2097176
  56.8 1.5 copy-done.12
  58.3 2.9 %shard_map.171.after_ref.local_ref = f32[768,1024]{1,0:T(8,128)S(1)} custom-call(bf16[512,1792]{1,0:T(8,128)(2,1)S(1)} %copy-done.12, bf16[512,1024]{1,0:T(8,128)(2,1)S(1)} %copy-done.5, bf16[512,1024]{1,0:T(8,128)(2,1)S(1)} %bitcast.17, bf16[1024,1024]{1,0:T(8,128)(2,1)S(1)} %copy-done.9, s32[1,512]{1,0:T(1,128)S(1)} %bitcast.24, ...), custom_call_target="tpu_custom_call" | custom-call | flops 21474836480 | bytes 1 | tf_op jit(solution)/shard_map/pallas_call | solution.py:370
  61.2 15.3 %all-to-all-done.in_ref = bf16[8,192,768]{2,1,0:T(8,128)(2,1)} async-done(((bf16[8,192,768]{2,1,0:T(8,128)(2,1)}), bf16[8,192,768]{2,1,0:T(8,128)(2,1)}, u32[]{:S(2)}, u32[]{:S(2)}) %all-to-all-start) | async-done | bytes 2359328 | tf_op jit(solution)/shard_map/all_to_all | solution.py:352
  76.5 0.0 collective-permute-done.other_ref
  76.5 0.0 copy-done.7
  76.5 0.0 copy-done.8
  76.5 7.5 %shard_map.172 = (bf16[6,128,1024]{2,1,0:T(8,128)(2,1)S(1)}, bf16[528,1024]{1,0:T(8,128)(2,1)S(1)}, bf16[528,1024]{1,0:T(8,128)(2,1)S(1)}) custom-call(bf16[8,192,768]{2,1,0:T(8,128)(2,1)} %all-to-all-done.in_ref, bf16[768,1024]{1,0:T(8,128)(2,1)} %bitcast.4.mine_ref, bf16[768,1024]{1,0:T(8,128)(2,1)} %collective-permute-done.other_ref, ...), custom_call_target="tpu_custom_call" | custom-call | flops 1073741824 | bytes 1 | tf_op jit(solution)/shard_map/pallas_call | solution.py:379
  84.0 0.3 collective-permute-start.3
  84.3 0.0 collective-permute-done.8.from_1_ref
  84.3 4.8 %collective-permute-start.5 = (bf16[528,1024]{1,0:T(8,128)(2,1)S(1)}, bf16[528,1024]{1,0:T(8,128)(2,1)S(1)}, u32[]{:S(2)}, u32[]{:S(2)}) collective-permute-start(bf16[528,1024]{1,0:T(8,128)(2,1)S(1)} %get-tuple-element.23), channel_id=1, source_target_pairs={{0,15},{1,0},{2,1},{3,2},{4,3},{5,4},{6,5},{7,6},{8,7},{9,8},{10,9... | collective-permute-start | bytes 3244040 | tf_op jit(solution)/shard_map/ppermute | solution.py:26
  89.0 0.0 collective-permute-done.9.from_2_ref
  89.0 2.1 %collective-permute-done.7.from_0_ref = bf16[4,128,1024]{2,1,0:T(8,128)(2,1)} collective-permute-done((bf16[4,128,1024]{2,1,0:T(8,128)(2,1)}, bf16[4,128,1024]{2,1,0:T(8,128)(2,1)}, u32[]{:S(2)}, u32[]{:S(2)}) %collective-permute-start.7) | collective-permute-done | bytes 1048608 | tf_op jit(solution)/shard_map/ppermute | solution.py:26
  91.1 0.0 collective-permute-done.10.from_3_ref
  91.1 4.7 %shard_map.173 = (f32[768,1024]{1,0:T(8,128)}, bf16[2,128,1024]{2,1,0:T(8,128)(2,1)S(1)}, bf16[2,128,1024]{2,1,0:T(8,128)(2,1)S(1)}) custom-call(f32[768,1024]{1,0:T(8,128)S(1)} %shard_map.171.after_ref.local_ref, bf16[4,128,1024]{2,1,0:T(8,128)(2,1)} %collective-permute-done.7.from_0_ref, bf16[4,128,1024]{2,1,0:T(8,128)(2,1)} %collective-permute-done.8.from_1_ref, ...), custom_call_target="tpu_custom_call" | custom-call | flops 1073741824 | bytes 1 | tf_op jit(solution)/shard_map/pallas_call | solution.py:409
  95.9 0.0 collective-permute-start.11
  95.9 4.8 %collective-permute-start.12 = (bf16[2,128,1024]{2,1,0:T(8,128)(2,1)S(1)}, bf16[2,128,1024]{2,1,0:T(8,128)(2,1)S(1)}, u32[]{:S(2)}, u32[]{:S(2)}) collective-permute-start(bf16[2,128,1024]{2,1,0:T(8,128)(2,1)S(1)} %get-tuple-element.28), channel_id=1, source_target_pairs={{0,15},{1,0},{2,1},{3,2},{4,3},{5,4},{6,5},{7,6},{8,7},{9,8},{10,9... | collective-permute-start | bytes 1572872 | tf_op jit(solution)/shard_map/ppermute | solution.py:26
  100.7 13.3 %collective-permute-done.3.a_up_ref = bf16[528,1024]{1,0:T(8,128)(2,1)S(1)} collective-permute-done((bf16[528,1024]{1,0:T(8,128)(2,1)S(1)}, bf16[528,1024]{1,0:T(8,128)(2,1)S(1)}, u32[]{:S(2)}, u32[]{:S(2)}) %collective-permute-start.3) | collective-permute-done | bytes 1081376 | tf_op jit(solution)/shard_map/ppermute | solution.py:26
  114.0 0.0 collective-permute-start.4
  114.0 0.0 collective-permute-done.5.a_down_ref
  114.0 4.8 %collective-permute-start.6 = (bf16[528,1024]{1,0:T(8,128)(2,1)S(1)}, bf16[528,1024]{1,0:T(8,128)(2,1)S(1)}, u32[]{:S(2)}, u32[]{:S(2)}) collective-permute-start(bf16[528,1024]{1,0:T(8,128)(2,1)S(1)} %collective-permute-done.5.a_down_ref), channel_id=1, source_target_pairs={{0,15},{1,0},{2,1},{3,2},{4,3},{5,4},{6,5},{7,6},{8,7},{9,8},{10,9... | collective-permute-start | bytes 3244040 | tf_op jit(solution)/shard_map/ppermute | solution.py:26
  118.8 6.4 %collective-permute-done.11.rest_up_ref = bf16[2,128,1024]{2,1,0:T(8,128)(2,1)S(1)} collective-permute-done((bf16[2,128,1024]{2,1,0:T(8,128)(2,1)S(1)}, bf16[2,128,1024]{2,1,0:T(8,128)(2,1)S(1)}, u32[]{:S(2)}, u32[]{:S(2)}) %collective-permute-start.11) | collective-permute-done | bytes 524320 | tf_op jit(solution)/shard_map/ppermute | solution.py:26
  125.2 0.0 collective-permute-done.12.rest_down_ref
  125.2 0.0 copy-done.10
  125.2 0.0 copy-done.13
  125.2 0.0 copy-done.14
  125.2 0.0 copy-start.1
  125.2 0.0 copy-start.3
  125.3 5.1 %shard_map.174 = (f32[512,1024]{1,0:T(8,128)S(1)}, f32[512,1024]{1,0:T(8,128)S(1)}) custom-call(bf16[512,1792]{1,0:T(8,128)(2,1)S(1)} %copy-done.13, bf16[6,128,1024]{2,1,0:T(8,128)(2,1)S(1)} %get-tuple-element.24.hid_ref, bf16[528,1024]{1,0:T(8,128)(2,1)S(1)} %collective-permute-done.3.a_up_ref, ...), custom_call_target="tpu_custom_call" | custom-call | flops 107374182400 | bytes 1 | tf_op jit(solution)/shard_map/pallas_call | solution.py:415
  130.3 18.1 %collective-permute-done.4.f_up_ref = bf16[528,1024]{1,0:T(8,128)(2,1)S(1)} collective-permute-done((bf16[528,1024]{1,0:T(8,128)(2,1)S(1)}, bf16[528,1024]{1,0:T(8,128)(2,1)S(1)}, u32[]{:S(2)}, u32[]{:S(2)}) %collective-permute-start.4) | collective-permute-done | bytes 1081376 | tf_op jit(solution)/shard_map/ppermute | solution.py:26
  148.4 0.0 collective-permute-done.6.f_down_ref
  148.4 0.0 copy-done.1
  148.4 0.0 copy-done.3
  148.4 3.7 %shard_map.175 = bf16[512,1024]{1,0:T(8,128)(2,1)} custom-call(bf16[512,1024]{1,0:T(8,128)(2,1)S(1)} %copy-done.3, bf16[528,1024]{1,0:T(8,128)(2,1)S(1)} %collective-permute-done.4.f_up_ref, bf16[528,1024]{1,0:T(8,128)(2,1)S(1)} %collective-permute-done.6.f_down_ref, f32[512,1024]{1,0:T(8,128)S(1)} %get-tuple-element.29.part_ref, ...), custom_call_target="tpu_custom_call" | custom-call | flops 1073741824 | bytes 1 | tf_op jit(solution)/shard_map/pallas_call | solution.py:426
  (12 shorter events, 0.0 us)
Async XLA Ops:
  3.6 37.8 %all-to-all-start.1 = ((bf16[8,96,1024]{2,1,0:T(8,128)(2,1)}), bf16[8,96,1024]{2,1,0:T(8,128)(2,1)}, u32[]{:S(2)}, u32[]{:S(2)}) async-start(bf16[8,96,1024]{2,1,0:T(8,128)(2,1)} %shard_map.167.after_ref), calls=%async_computation.1 | async-start | bytes 3145728 | tf_op jit(solution)/shard_map/all_to_all | solution.py:353
  16.1 31.2 %collective-permute-start.1 = (bf16[4,128,1024]{2,1,0:T(8,128)(2,1)}, bf16[4,128,1024]{2,1,0:T(8,128)(2,1)}, u32[]{:S(2)}, u32[]{:S(2)}) collective-permute-start(bf16[4,128,1024]{2,1,0:T(8,128)(2,1)} %get-tuple-element.20), channel_id=1, source_target_pairs={{0,1},{1,2},{2,3},{3,4},{4,5},{5,6},{6,7},{7,8},{8,9},{9,10},{10,1... | collective-permute-start | bytes 3145736 | tf_op jit(solution)/shard_map/ppermute | solution.py:26
  17.8 29.6 %collective-permute-start.2 = (bf16[4,128,1024]{2,1,0:T(8,128)(2,1)}, bf16[4,128,1024]{2,1,0:T(8,128)(2,1)}, u32[]{:S(2)}, u32[]{:S(2)}) collective-permute-start(bf16[4,128,1024]{2,1,0:T(8,128)(2,1)} %get-tuple-element.21), channel_id=1, source_target_pairs={{0,15},{1,0},{2,1},{3,2},{4,3},{5,4},{6,5},{7,6},{8,7},{9,8},{10,9... | collective-permute-start | bytes 3145736 | tf_op jit(solution)/shard_map/ppermute | solution.py:26
  22.4 8.5 %copy-start = (bf16[1,1,4,16,128,128]{5,4,3,2,1,0:T(8,128)(2,1)S(1)}, bf16[1,1,4,16,128,128]{5,4,3,2,1,0:T(8,128)(2,1)}, u32[]{:S(2)}) copy-start(bf16[1,1,4,16,128,128]{5,4,3,2,1,0:T(8,128)(2,1)} %param.26) | copy-start | bytes 6291460
  22.4 8.5 %copy-start.4 = (bf16[512,1024]{1,0:T(8,128)(2,1)S(1)}, bf16[512,1024]{1,0:T(8,128)(2,1)}, u32[]{:S(2)}) copy-start(bf16[512,1024]{1,0:T(8,128)(2,1)} %get-tuple-element.18.after_ref.back_ref) | copy-start | bytes 3145732
  22.5 8.5 %copy-start.6 = (s32[1,1,4,16]{3,2,1,0:T(4,128)S(1)}, s32[1,1,4,16]{3,2,1,0:T(4,128)}, u32[]{:S(2)}) copy-start(s32[1,1,4,16]{3,2,1,0:T(4,128)} %param.27) | copy-start | bytes 772
  35.4 1.2 copy-start.11
  36.6 47.6 %collective-permute-start.8 = (bf16[4,128,1024]{2,1,0:T(8,128)(2,1)}, bf16[4,128,1024]{2,1,0:T(8,128)(2,1)}, u32[]{:S(2)}, u32[]{:S(2)}) collective-permute-start(bf16[4,128,1024]{2,1,0:T(8,128)(2,1)} %get-tuple-element.25), channel_id=1, source_target_pairs={{0,1},{1,2},{2,3},{3,4},{4,5},{5,6},{6,7},{7,8},{8,9},{9,10},{10,1... | collective-permute-start | bytes 3145736 | tf_op jit(solution)/shard_map/ppermute | solution.py:26
  36.6 52.4 %collective-permute-start.9 = (bf16[4,128,1024]{2,1,0:T(8,128)(2,1)}, bf16[4,128,1024]{2,1,0:T(8,128)(2,1)}, u32[]{:S(2)}, u32[]{:S(2)}) collective-permute-start(bf16[4,128,1024]{2,1,0:T(8,128)(2,1)} %get-tuple-element.26), channel_id=1, source_target_pairs={{0,15},{1,0},{2,1},{3,2},{4,3},{5,4},{6,5},{7,6},{8,7},{9,8},{10,9... | collective-permute-start | bytes 3145736 | tf_op jit(solution)/shard_map/ppermute | solution.py:26
  41.4 5.8 %copy-start.16 = (s32[1,1,4]{2,1,0:T(1,128)S(1)}, s32[1,1,4]{2,1,0:T(1,128)}, u32[]{:S(2)}) copy-start(s32[1,1,4]{2,1,0:T(1,128)} %param.29) | copy-start | bytes 52
  41.4 5.8 %copy-start.17 = (s32[4]{0:T(128)S(1)}, s32[4]{0:T(128)}, u32[]{:S(2)}) copy-start(s32[4]{0:T(128)} %constant.28.clone) | copy-start | bytes 52
  41.4 11.3 %copy-start.15 = (s32[1,1,512]{2,1,0:T(1,128)S(1)}, s32[1,1,512]{2,1,0:T(1,128)}, u32[]{:S(2)}) copy-start(s32[1,1,512]{2,1,0:T(1,128)} %param.25) | copy-start | bytes 6148
  41.4 35.1 %all-to-all-start = ((bf16[8,192,768]{2,1,0:T(8,128)(2,1)}), bf16[8,192,768]{2,1,0:T(8,128)(2,1)}, u32[]{:S(2)}, u32[]{:S(2)}) async-start(bf16[8,192,768]{2,1,0:T(8,128)(2,1)} %shard_map.169.after_ref), calls=%async_computation | async-start | bytes 4718592 | tf_op jit(solution)/shard_map/all_to_all | solution.py:352
  47.3 43.8 %collective-permute-start.7 = (bf16[4,128,1024]{2,1,0:T(8,128)(2,1)}, bf16[4,128,1024]{2,1,0:T(8,128)(2,1)}, u32[]{:S(2)}, u32[]{:S(2)}) collective-permute-start(bf16[4,128,1024]{2,1,0:T(8,128)(2,1)} %collective-permute-done.1.after_up_ref), channel_id=1, source_target_pairs={{0,1},{1,2},{2,3},{3,4},{4,5},{5,6},{6,7},{7,8},{8,9},{9,10},{10,1... | collective-permute-start | bytes 3145736 | tf_op jit(solution)/shard_map/ppermute | solution.py:26
  47.4 43.7 %collective-permute-start.10 = (bf16[4,128,1024]{2,1,0:T(8,128)(2,1)}, bf16[4,128,1024]{2,1,0:T(8,128)(2,1)}, u32[]{:S(2)}, u32[]{:S(2)}) collective-permute-start(bf16[4,128,1024]{2,1,0:T(8,128)(2,1)} %collective-permute-done.2.after_down_ref), channel_id=1, source_target_pairs={{0,15},{1,0},{2,1},{3,2},{4,3},{5,4},{6,5},{7,6},{8,7},{9,8},{10,9... | collective-permute-start | bytes 3145736 | tf_op jit(solution)/shard_map/ppermute | solution.py:26
  52.2 24.3 %collective-permute-start = (bf16[768,1024]{1,0:T(8,128)(2,1)}, bf16[768,1024]{1,0:T(8,128)(2,1)}, u32[]{:S(2)}, u32[]{:S(2)}) collective-permute-start(bf16[768,1024]{1,0:T(8,128)(2,1)} %bitcast.4.mine_ref), channel_id=1, source_target_pairs={{0,16},{16,0},{32,48},{48,32},{64,80},{80,64},{96,112},{112,96},{1... | collective-permute-start | bytes 4718600 | tf_op jit(solution)/shard_map/ppermute | solution.py:355
  52.7 1.2 copy-start.2
  54.0 1.2 copy-start.5
  55.2 1.6 %copy-start.9 = (bf16[1024,1024]{1,0:T(8,128)(2,1)S(1)}, bf16[1024,1024]{1,0:T(8,128)(2,1)}, u32[]{:S(2)}) copy-start(bf16[1024,1024]{1,0:T(8,128)(2,1)} %w_ref.6) | copy-start | bytes 6291460
  56.8 1.5 copy-start.12
  58.3 18.2 %copy-start.7 = (s32[1,1,4,4]{3,2,1,0:T(4,128)S(1)}, s32[1,1,4,4]{3,2,1,0:T(4,128)}, u32[]{:S(2)}) copy-start(s32[1,1,4,4]{3,2,1,0:T(4,128)} %param.28) | copy-start | bytes 196
  58.3 18.2 %copy-start.8 = (f32[1024]{0:T(1024)S(1)}, f32[1024]{0:T(1024)}, u32[]{:S(2)}) copy-start(f32[1024]{0:T(1024)} %param.21) | copy-start | bytes 12292
  84.0 30.0 %collective-permute-start.3 = (bf16[528,1024]{1,0:T(8,128)(2,1)S(1)}, bf16[528,1024]{1,0:T(8,128)(2,1)S(1)}, u32[]{:S(2)}, u32[]{:S(2)}) collective-permute-start(bf16[528,1024]{1,0:T(8,128)(2,1)S(1)} %get-tuple-element.22), channel_id=1, source_target_pairs={{0,1},{1,2},{2,3},{3,4},{4,5},{5,6},{6,7},{7,8},{8,9},{9,10},{10,1... | collective-permute-start | bytes 3244040 | tf_op jit(solution)/shard_map/ppermute | solution.py:26
  84.3 29.7 %collective-permute-start.5 = (bf16[528,1024]{1,0:T(8,128)(2,1)S(1)}, bf16[528,1024]{1,0:T(8,128)(2,1)S(1)}, u32[]{:S(2)}, u32[]{:S(2)}) collective-permute-start(bf16[528,1024]{1,0:T(8,128)(2,1)S(1)} %get-tuple-element.23), channel_id=1, source_target_pairs={{0,15},{1,0},{2,1},{3,2},{4,3},{5,4},{6,5},{7,6},{8,7},{9,8},{10,9... | collective-permute-start | bytes 3244040 | tf_op jit(solution)/shard_map/ppermute | solution.py:26
  91.1 34.1 %copy-start.10 = (bf16[1024,1024]{1,0:T(8,128)(2,1)S(1)}, bf16[1024,1024]{1,0:T(8,128)(2,1)}, u32[]{:S(2)}) copy-start(bf16[1024,1024]{1,0:T(8,128)(2,1)} %w_ref.6) | copy-start | bytes 6291460
  91.1 34.1 %copy-start.13 = (bf16[512,1792]{1,0:T(8,128)(2,1)S(1)}, bf16[512,1792]{1,0:T(8,128)(2,1)}, u32[]{:S(2)}) copy-start(bf16[512,1792]{1,0:T(8,128)(2,1)} %copy-done.11) | copy-start | bytes 5505028
  91.1 34.1 %copy-start.14 = (f32[1024]{0:T(1024)S(1)}, f32[1024]{0:T(1024)}, u32[]{:S(2)}) copy-start(f32[1024]{0:T(1024)} %param.24) | copy-start | bytes 12292
  95.9 29.3 %collective-permute-start.11 = (bf16[2,128,1024]{2,1,0:T(8,128)(2,1)S(1)}, bf16[2,128,1024]{2,1,0:T(8,128)(2,1)S(1)}, u32[]{:S(2)}, u32[]{:S(2)}) collective-permute-start(bf16[2,128,1024]{2,1,0:T(8,128)(2,1)S(1)} %get-tuple-element.27), channel_id=1, source_target_pairs={{0,1},{1,2},{2,3},{3,4},{4,5},{5,6},{6,7},{7,8},{8,9},{9,10},{10,1... | collective-permute-start | bytes 1572872 | tf_op jit(solution)/shard_map/ppermute | solution.py:26
  95.9 29.3 %collective-permute-start.12 = (bf16[2,128,1024]{2,1,0:T(8,128)(2,1)S(1)}, bf16[2,128,1024]{2,1,0:T(8,128)(2,1)S(1)}, u32[]{:S(2)}, u32[]{:S(2)}) collective-permute-start(bf16[2,128,1024]{2,1,0:T(8,128)(2,1)S(1)} %get-tuple-element.28), channel_id=1, source_target_pairs={{0,15},{1,0},{2,1},{3,2},{4,3},{5,4},{6,5},{7,6},{8,7},{9,8},{10,9... | collective-permute-start | bytes 1572872 | tf_op jit(solution)/shard_map/ppermute | solution.py:26
  114.0 34.4 %collective-permute-start.4 = (bf16[528,1024]{1,0:T(8,128)(2,1)S(1)}, bf16[528,1024]{1,0:T(8,128)(2,1)S(1)}, u32[]{:S(2)}, u32[]{:S(2)}) collective-permute-start(bf16[528,1024]{1,0:T(8,128)(2,1)S(1)} %collective-permute-done.3.a_up_ref), channel_id=1, source_target_pairs={{0,1},{1,2},{2,3},{3,4},{4,5},{5,6},{6,7},{7,8},{8,9},{9,10},{10,1... | collective-permute-start | bytes 3244040 | tf_op jit(solution)/shard_map/ppermute | solution.py:26
  114.0 34.4 %collective-permute-start.6 = (bf16[528,1024]{1,0:T(8,128)(2,1)S(1)}, bf16[528,1024]{1,0:T(8,128)(2,1)S(1)}, u32[]{:S(2)}, u32[]{:S(2)}) collective-permute-start(bf16[528,1024]{1,0:T(8,128)(2,1)S(1)} %collective-permute-done.5.a_down_ref), channel_id=1, source_target_pairs={{0,15},{1,0},{2,1},{3,2},{4,3},{5,4},{6,5},{7,6},{8,7},{9,8},{10,9... | collective-permute-start | bytes 3244040 | tf_op jit(solution)/shard_map/ppermute | solution.py:26
  125.2 23.2 %copy-start.1 = (bf16[1024,1024]{1,0:T(8,128)(2,1)S(1)}, bf16[1024,1024]{1,0:T(8,128)(2,1)}, u32[]{:S(2)}) copy-start(bf16[1024,1024]{1,0:T(8,128)(2,1)} %w_ref.7) | copy-start | bytes 6291460
  125.2 23.1 %copy-start.3 = (bf16[512,1024]{1,0:T(8,128)(2,1)S(1)}, bf16[512,1024]{1,0:T(8,128)(2,1)}, u32[]{:S(2)}) copy-start(bf16[512,1024]{1,0:T(8,128)(2,1)} %get-tuple-element.17.fold_ref) | copy-start | bytes 3145732

commit v3 on v2

--- a/solution.py
+++ b/solution.py
@@ -21,17 +21,22 @@
 ANY = pl.BlockSpec(memory_space=pl.ANY)
 
 
+def open_shift(shard, by):
+    count = lax.axis_size("dom")
+    return lax.ppermute(shard, "dom", [(i, i + by) for i in range(count) if 0 <= i + by < count])
+
+
 def shifted(shard, by):
     count = lax.axis_size("dom")
     return lax.ppermute(shard, "dom", [(i, (i + by) % count) for i in range(count)])
 
 
-def call(body, outs, in_specs, scratch=(), cost=1, vmem=32):
+def call(body, outs, in_specs, scratch=(), cost=1, vmem=32, out_specs=None):
     return pl.pallas_call(
         body,
         out_shape=outs,
         in_specs=in_specs,
-        out_specs=jax.tree.map(lambda _: VMEM, outs),
+        out_specs=out_specs or jax.tree.map(lambda _: VMEM, outs),
         scratch_shapes=list(scratch),
         cost_estimate=pl.CostEstimate(flops=cost * GIGA, bytes_accessed=1, transcendentals=0),
         compiler_params=pltpu.CompilerParams(vmem_limit_bytes=vmem * MIB),
@@ -75,18 +80,21 @@
     return at
 
 
-def halves_kernel(self_ref, neigh_ref, out_ref, sems):
-    copies = [
-        pltpu.make_async_copy((self_ref, neigh_ref)[i % 2], out_ref.at[i], sems.at[i]) for i in range(out_ref.shape[0])
-    ]
-    for copy in copies:
-        copy.start()
-    for copy in copies:
-        copy.wait()
+def halves_kernel(self_ref, neigh_ref, after_ref, out_ref, buf, sems):
+    loads = [pltpu.make_async_copy(ref, buf.at[i], sems.at[i]) for i, ref in enumerate((self_ref, neigh_ref))]
+    stores = [pltpu.make_async_copy(buf.at[i % 2], out_ref.at[i], sems.at[2 + i]) for i in range(out_ref.shape[0])]
+    for load in loads:
+        load.start()
+    for kind, load in enumerate(loads):
+        load.wait()
+        for store in stores[kind::2]:
+            store.start()
+    for store in stores:
+        store.wait()
 
 
 def far_kernel(
-    adj_ref, src_ref, cot_ref, w_ref, after_ref,
+    adj_ref, src_ref, cot_ref, w_ref,
     back_ref, fold_ref, up_ref, down_ref, adj_buf, cot_buf, w_buf, acc_ref, sems,
 ):
     seeds = adj_ref.shape[0]
@@ -177,19 +185,18 @@
 
 def hidden_kernel(
     in_ref, mine_ref, other_ref, bias_ref, odd_ref, tiles_ref, count_ref, after_ref,
-    hid_ref, up_ref, down_ref, turned_ref, w_ref,
+    hid_ref, up_ref, down_ref, turned_ref,
 ):
     slices, width, span = in_ref.shape[0], in_ref.shape[1] // 2, in_ref.shape[2]
     depth = slices * width
 
     @pl.when(pl.program_id(0) == 0)
     def _():
-        turned_ref[:, :depth] = in_ref[:, :width].reshape(depth, span).T
-        turned_ref[:, depth:] = in_ref[:, width:].reshape(depth, span).T
-
-    w_ref[pl.ds(pl.multiple_of(odd_ref[0] * depth, depth), depth)] = mine_ref[...]
-    w_ref[pl.ds(pl.multiple_of((1 - odd_ref[0]) * depth, depth), depth)] = other_ref[...]
-    total = nn_dot(turned_ref[...], w_ref[...])
+        for half, odd in enumerate((odd_ref[0], 1 - odd_ref[0])):
+            kind = in_ref[:, pl.ds(pl.multiple_of(odd * width, width), width)]
+            turned_ref[:, half * depth : (half + 1) * depth] = kind.reshape(depth, span).T
+
+    total = nn_dot(turned_ref[:, :depth], mine_ref[...]) + nn_dot(turned_ref[:, depth:], other_ref[...])
     hidden = jnp.maximum(total + bias_ref[...], 0.0).astype(jnp.bfloat16)
     hid_ref[...] = hidden.reshape(hid_ref.shape)
     shape = (2 * ROWS, up_ref.shape[1])
@@ -312,17 +319,10 @@
     quad_marked = shape((NEAR * TILE + 2 * ROWS, hid), bf16)
     far_cols, near_cols = 2 * SLOTS * TILE, (TILE_DEV + 2 * SLOTS) * TILE
 
-    halves = call(
-        halves_kernel,
-        shape((feat_count, width, hid), bf16),
-        [ANY, ANY],
-        [pltpu.SemaphoreType.DMA((feat_count,))],
-        vmem=56,
-    )(w_self_one, w_neigh_one)
     back, fold_far, far_up, far_down = call(
         far_kernel,
         (shape((seeds, hid), bf16), shape((seeds, far_cols), bf16), quad, quad),
-        [ANY, SMEM, ANY, ANY, ANY],
+        [ANY, SMEM, ANY, ANY],
         [
             pltpu.VMEM(blocks.shape, bf16),
             pltpu.VMEM((seeds, hid), bf16),
@@ -331,7 +331,17 @@
             pltpu.SemaphoreType.DMA((blocks.shape[0] + 2,)),
         ],
         vmem=56,
-            )(blocks, sources, upstream, w_neigh_two, halves)
+            )(blocks, sources, upstream, w_neigh_two)
+    halves = call(
+        halves_kernel,
+        shape((feat_count, width, hid), bf16),
+        [ANY, ANY, ANY],
+        [pltpu.VMEM((2, width, hid), bf16), pltpu.SemaphoreType.DMA((2 + feat_count,))],
+        vmem=56,
+        out_specs=ANY,
+    )(w_self_one, w_neigh_one, far_up)
+    halves = lax.all_to_all(halves, "feat", 0, 0)
+    halves = halves.reshape(feat_count * width, hid)
     got_far_up = shifted(far_up, 1)
     got_far_down = shifted(far_down, -1)
 
@@ -350,8 +360,6 @@
         compiler_params=pltpu.CompilerParams(vmem_limit_bytes=56 * MIB),
     )(src_one.T, features, adj_one, back)
     taken = lax.all_to_all(sent, "feat", 0, 0)
-    halves = lax.all_to_all(halves, "feat", 0, 0)
-    halves = halves.reshape(feat_count * width, hid)
     swapped = lax.ppermute(halves, "feat", [(i, i ^ 1) for i in range(feat_count)])
     odd = (lax.axis_index("feat") % 2).astype(jnp.int32)[None]
 
@@ -375,7 +383,7 @@
         vmem=28,
     )(fold_near, back, upstream, w_self_two, seed_rows[0], got_far_up, got_far_down)
 
-    chunk = hid // 4
+    chunk = hid // 2
     hidden, h_up, h_down = pl.pallas_call(
         hidden_kernel,
         grid=(hid // chunk,),
@@ -397,15 +405,14 @@
         out_shape=(shape((TILE_DEV, TILE, hid), bf16), quad_marked, quad_marked),
         scratch_shapes=[
             pltpu.VMEM((row_dev, 2 * width * feat_count), bf16),
-            pltpu.VMEM((2 * width * feat_count, chunk), bf16),
         ],
         cost_estimate=pl.CostEstimate(flops=GIGA, bytes_accessed=1, transcendentals=0),
         compiler_params=pltpu.CompilerParams(vmem_limit_bytes=24 * MIB),
     )(taken, halves, swapped, bias_one[None], odd, lists, counts, local)
     got_h_up = shifted(h_up, 1)
     got_h_down = shifted(h_down, -1)
-    next_up = shifted(got_h_up, 1)
-    next_down = shifted(got_h_down, -1)
+    next_up = open_shift(got_h_up, 1)
+    next_down = open_shift(got_h_down, -1)
     grads, rest_up, rest_down = call(
         merge_kernel, (shape((row_dev, hid), f32), pair, pair), [VMEM] * 6 + [SMEM] * 2, vmem=24
     )(local, grad_0, grad_1, grad_2, grad_3, hidden, lists, counts)

time: 153 us -> 148 us (0.967)
  the two profiles are of different devices: /device:TPU:1 before, /device:TPU:104 now
where the time goes in v3:
time: 148 us; the launch traced here: 147 us
  waiting for transfers between devices  64.3 us (43%)
  Pallas kernels  45 us (30%)
  starting transfers between devices  29.6 us (20%)
  local copies, waits for them, and re-layouts  6.85 us (5%)
    ppermute x10, waiting for transfers between devices, shifted(): lax.ppermute(shard, 'dom', [(i, (i + by) % count) for i in range(count)])  25 us
    all_to_all x1, waiting for transfers between devices, shards(): taken = lax.all_to_all(sent, 'feat', 0, 0)  17.3 us
    ppermute x2, waiting for transfers between devices, open_shift(): lax.ppermute(shard, 'dom', [(i, i + by) for i in range(count) if 0 <= i +...  16.7 us
    ppermute x10, starting transfers between devices, shifted(): lax.ppermute(shard, 'dom', [(i, (i + by) % count) for i in range(count)])  15 us
    pallas_call x1, Pallas kernels, shards(): pl.pallas_call(gather_kernel, grid=(feat_count,), in_specs=[SMEM, pl.Bloc...  8.54 us
    unnamed x36, local copies, waits for them, and re-layouts  6.85 us
    pallas_call x1, Pallas kernels, shards(): call(far_kernel, (shape((seeds, hid), bf16), shape((seeds, far_cols), bf1...  6.65 us
    pallas_call x1, Pallas kernels, shards(): pl.pallas_call(hidden_kernel, grid=(hid // chunk,), in_specs=[pl.BlockSpe...  6.51 us
  transfers between devices with their start and end apart: 15, of which 7 were waited for; matrix products, arithmetic and copies ran while one was open for 0% of the time, Pallas kernels for 24%

profile of v3, /device:TPU:104, one launch (start us, length us, event | category | flops | bytes accessed | tf_op | source)
XLA Modules:
  0.0 146.6 jit_solution(14878463647295613295)
XLA Ops:
  0.6 6.7 %shard_map.167 = (bf16[512,1024]{1,0:T(8,128)(2,1)}, bf16[512,1024]{1,0:T(8,128)(2,1)}, bf16[4,128,1024]{2,1,0:T(8,128)(2,1)}, bf16[4,128,1024]{2,1,0:T(8,128)(2,1)}) custom-call(bf16[4,16,128,128]{3,2,1,0:T(8,128)(2,1)} %bitcast.14, s32[4,16]{1,0:T(4,128)} %bitcast.18, bf16[512,1024]{1,0:T(8,128)(2,1)} %bitcast.16, bf16[1024,1024]{1,0:T(8,128)(2,1)} %w_ref.7), custom_call_target="tpu_custom_call" | custom-call | flops 1073741824 | bytes 1 | tf_op jit(solution)/shard_map/pallas_call | solution.py:322
  7.3 0.5 collective-permute-start.2
  7.8 3.7 %collective-permute-start.1 = (bf16[4,128,1024]{2,1,0:T(8,128)(2,1)}, bf16[4,128,1024]{2,1,0:T(8,128)(2,1)}, u32[]{:S(2)}, u32[]{:S(2)}) collective-permute-start(bf16[4,128,1024]{2,1,0:T(8,128)(2,1)} %get-tuple-element.19.after_ref), channel_id=1, source_target_pairs={{0,1},{1,2},{2,3},{3,4},{4,5},{5,6},{6,7},{7,8},{8,9},{9,10},{10,1... | collective-permute-start | bytes 3145736 | tf_op jit(solution)/shard_map/ppermute | solution.py:31
  11.5 2.2 %shard_map.169 = bf16[8,96,1024]{2,1,0:T(8,128)(2,1)} custom-call(bf16[96,1024]{1,0:T(8,128)(2,1)} %self_ref.1, bf16[96,1024]{1,0:T(8,128)(2,1)} %neigh_ref.1, bf16[4,128,1024]{2,1,0:T(8,128)(2,1)} %get-tuple-element.19.after_ref), custom_call_target="tpu_custom_call" | custom-call | flops 1073741824 | bytes 1 | tf_op jit(solution)/shard_map/pallas_call | solution.py:335
  13.7 4.3 %all-to-all-start.1 = ((bf16[8,96,1024]{2,1,0:T(8,128)(2,1)}), bf16[8,96,1024]{2,1,0:T(8,128)(2,1)}, u32[]{:S(2)}, u32[]{:S(2)}) async-start(bf16[8,96,1024]{2,1,0:T(8,128)(2,1)} %shard_map.169), calls=%async_computation.1 | async-start | bytes 3145728 | tf_op jit(solution)/shard_map/all_to_all | solution.py:343
  18.0 0.0 copy-start
  18.0 0.0 copy-start.4
  18.0 0.0 copy-start.6
  18.1 8.5 %shard_map.168.after_ref = bf16[8,192,768]{2,1,0:T(8,128)(2,1)} custom-call(s32[4,48]{1,0:T(4,128)} %bitcast.28, bf16[96,6144]{1,0:T(8,128)(2,1)} %feat_ref.1, bf16[48,4,128,128]{3,2,1,0:T(8,128)(2,1)} %adj_ref.1, bf16[512,1024]{1,0:T(8,128)(2,1)} %get-tuple-element.18.after_ref.back_ref), custom_call_target="tpu_custom_call" | custom-call | flops 107374182400 | bytes 1 | tf_op jit(solution)/shard_map/pallas_call | solution.py:348
  26.6 0.0 copy-done
  26.6 0.0 copy-done.4
  26.6 0.0 copy-done.6
  26.6 4.5 %shard_map.170 = (bf16[512,1792]{1,0:T(8,128)(2,1)S(1)}, bf16[4,128,1024]{2,1,0:T(8,128)(2,1)}, bf16[4,128,1024]{2,1,0:T(8,128)(2,1)}) custom-call(bf16[4,16,128,128]{3,2,1,0:T(8,128)(2,1)S(1)} %bitcast.15, s32[4,16]{1,0:T(4,128)S(1)} %bitcast.19, bf16[512,1024]{1,0:T(8,128)(2,1)S(1)} %copy-done.4, bf16[8,192,768]{2,1,0:T(8,128)(2,1)} %shard_map.168.after_ref), custom_call_target="tpu_custom_call" | custom-call | flops 1073741824 | bytes 1 | tf_op jit(solution)/shard_map/pallas_call | solution.py:366
  31.1 1.2 copy-done.11
  32.3 0.0 collective-permute-start.8
  32.3 2.0 %collective-permute-start.9 = (bf16[4,128,1024]{2,1,0:T(8,128)(2,1)}, bf16[4,128,1024]{2,1,0:T(8,128)(2,1)}, u32[]{:S(2)}, u32[]{:S(2)}) collective-permute-start(bf16[4,128,1024]{2,1,0:T(8,128)(2,1)} %get-tuple-element.26), channel_id=1, source_target_pairs={{0,15},{1,0},{2,1},{3,2},{4,3},{5,4},{6,5},{7,6},{8,7},{9,8},{10,9... | collective-permute-start | bytes 3145736 | tf_op jit(solution)/shard_map/ppermute | solution.py:31
  34.4 5.3 %all-to-all-done.1 = bf16[8,96,1024]{2,1,0:T(8,128)(2,1)} async-done(((bf16[8,96,1024]{2,1,0:T(8,128)(2,1)}), bf16[8,96,1024]{2,1,0:T(8,128)(2,1)}, u32[]{:S(2)}, u32[]{:S(2)}) %all-to-all-start.1) | async-done | bytes 1572896 | tf_op jit(solution)/shard_map/all_to_all | solution.py:343
  39.7 4.4 %all-to-all-start = ((bf16[8,192,768]{2,1,0:T(8,128)(2,1)}), bf16[8,192,768]{2,1,0:T(8,128)(2,1)}, u32[]{:S(2)}, u32[]{:S(2)}) async-start(bf16[8,192,768]{2,1,0:T(8,128)(2,1)} %shard_map.168.after_ref), calls=%async_computation | async-start | bytes 4718592 | tf_op jit(solution)/shard_map/all_to_all | solution.py:362
  44.1 0.0 copy-done.16
  44.1 0.0 copy-done.17
  44.1 0.0 collective-permute-done.2.after_down_ref
  44.1 0.1 collective-permute-start.10
  44.2 0.0 collective-permute-done.1.after_up_ref
  44.2 4.1 %collective-permute-start.7 = (bf16[4,128,1024]{2,1,0:T(8,128)(2,1)}, bf16[4,128,1024]{2,1,0:T(8,128)(2,1)}, u32[]{:S(2)}, u32[]{:S(2)}) collective-permute-start(bf16[4,128,1024]{2,1,0:T(8,128)(2,1)} %collective-permute-done.1.after_up_ref), channel_id=1, source_target_pairs={{0,1},{1,2},{2,3},{3,4},{4,5},{5,6},{6,7},{7,8},{8,9},{9,10},{10,1... | collective-permute-start | bytes 3145736 | tf_op jit(solution)/shard_map/ppermute | solution.py:31
  48.4 0.0 collective-permute-start
  48.4 0.0 copy-done.15
  48.4 1.2 copy-done.2
  49.6 1.2 copy-done.5
  50.8 1.6 %copy-done.9 = bf16[1024,1024]{1,0:T(8,128)(2,1)S(1)} copy-done((bf16[1024,1024]{1,0:T(8,128)(2,1)S(1)}, bf16[1024,1024]{1,0:T(8,128)(2,1)}, u32[]{:S(2)}) %copy-start.9) | copy-done | bytes 2097176
  52.4 1.5 %copy-done.12 = bf16[512,1792]{1,0:T(8,128)(2,1)S(1)} copy-done((bf16[512,1792]{1,0:T(8,128)(2,1)S(1)}, bf16[512,1792]{1,0:T(8,128)(2,1)}, u32[]{:S(2)}) %copy-start.12) | copy-done | bytes 1835032
  53.9 2.9 %shard_map.171.after_ref.local_ref = f32[768,1024]{1,0:T(8,128)S(1)} custom-call(bf16[512,1792]{1,0:T(8,128)(2,1)S(1)} %copy-done.12, bf16[512,1024]{1,0:T(8,128)(2,1)S(1)} %copy-done.5, bf16[512,1024]{1,0:T(8,128)(2,1)S(1)} %bitcast.17, bf16[1024,1024]{1,0:T(8,128)(2,1)S(1)} %copy-done.9, s32[1,512]{1,0:T(1,128)S(1)} %bitcast.24, ...), custom_call_target="tpu_custom_call" | custom-call | flops 21474836480 | bytes 1 | tf_op jit(solution)/shard_map/pallas_call | solution.py:378
  56.8 17.3 %all-to-all-done.in_ref = bf16[8,192,768]{2,1,0:T(8,128)(2,1)} async-done(((bf16[8,192,768]{2,1,0:T(8,128)(2,1)}), bf16[8,192,768]{2,1,0:T(8,128)(2,1)}, u32[]{:S(2)}, u32[]{:S(2)}) %all-to-all-start) | async-done | bytes 2359328 | tf_op jit(solution)/shard_map/all_to_all | solution.py:362
  74.1 0.0 collective-permute-done.other_ref
  74.1 0.0 copy-done.7
  74.1 0.0 copy-done.8
  74.1 6.5 %shard_map.172 = (bf16[6,128,1024]{2,1,0:T(8,128)(2,1)S(1)}, bf16[528,1024]{1,0:T(8,128)(2,1)S(1)}, bf16[528,1024]{1,0:T(8,128)(2,1)S(1)}) custom-call(bf16[8,192,768]{2,1,0:T(8,128)(2,1)} %all-to-all-done.in_ref, bf16[768,1024]{1,0:T(8,128)(2,1)} %bitcast.4.mine_ref, bf16[768,1024]{1,0:T(8,128)(2,1)} %collective-permute-done.other_ref, ...), custom_call_target="tpu_custom_call" | custom-call | flops 1073741824 | bytes 1 | tf_op jit(solution)/shard_map/pallas_call | solution.py:387
  80.6 0.3 collective-permute-start.3
  80.9 0.0 collective-permute-done.8.from_1_ref
  80.9 2.0 %collective-permute-start.5 = (bf16[528,1024]{1,0:T(8,128)(2,1)S(1)}, bf16[528,1024]{1,0:T(8,128)(2,1)S(1)}, u32[]{:S(2)}, u32[]{:S(2)}) collective-permute-start(bf16[528,1024]{1,0:T(8,128)(2,1)S(1)} %get-tuple-element.23), channel_id=1, source_target_pairs={{0,15},{1,0},{2,1},{3,2},{4,3},{5,4},{6,5},{7,6},{8,7},{9,8},{10,9... | collective-permute-start | bytes 3244040 | tf_op jit(solution)/shard_map/ppermute | solution.py:31
  82.9 0.0 collective-permute-done.9.from_2_ref
  82.9 0.0 collective-permute-done.10.from_3_ref
  82.9 0.0 collective-permute-done.7.from_0_ref
  82.9 0.0 copy-start.10
  82.9 0.0 copy-start.13
  82.9 0.0 copy-start.14
  82.9 4.9 %shard_map.173 = (f32[768,1024]{1,0:T(8,128)}, bf16[2,128,1024]{2,1,0:T(8,128)(2,1)S(1)}, bf16[2,128,1024]{2,1,0:T(8,128)(2,1)S(1)}) custom-call(f32[768,1024]{1,0:T(8,128)S(1)} %shard_map.171.after_ref.local_ref, bf16[4,128,1024]{2,1,0:T(8,128)(2,1)} %collective-permute-done.7.from_0_ref, bf16[4,128,1024]{2,1,0:T(8,128)(2,1)} %collective-permute-done.8.from_1_ref, ...), custom_call_target="tpu_custom_call" | custom-call | flops 1073741824 | bytes 1 | tf_op jit(solution)/shard_map/pallas_call | solution.py:416
  87.9 2.3 %collective-permute-start.11 = (bf16[2,128,1024]{2,1,0:T(8,128)(2,1)S(1)}, bf16[2,128,1024]{2,1,0:T(8,128)(2,1)S(1)}, u32[]{:S(2)}, u32[]{:S(2)}) collective-permute-start(bf16[2,128,1024]{2,1,0:T(8,128)(2,1)S(1)} %get-tuple-element.27), channel_id=1, source_target_pairs={{0,1},{1,2},{2,3},{3,4},{4,5},{5,6},{6,7},{7,8},{8,9},{9,10},{10,1... | collective-permute-start | bytes 1572872 | tf_op jit(solution)/shard_map/ppermute | solution.py:31
  90.2 0.0 collective-permute-start.12
  90.2 17.5 %collective-permute-done.3.a_up_ref = bf16[528,1024]{1,0:T(8,128)(2,1)S(1)} collective-permute-done((bf16[528,1024]{1,0:T(8,128)(2,1)S(1)}, bf16[528,1024]{1,0:T(8,128)(2,1)S(1)}, u32[]{:S(2)}, u32[]{:S(2)}) %collective-permute-start.3) | collective-permute-done | bytes 1081376 | tf_op jit(solution)/shard_map/ppermute | solution.py:31
  107.6 4.0 %collective-permute-start.4 = (bf16[528,1024]{1,0:T(8,128)(2,1)S(1)}, bf16[528,1024]{1,0:T(8,128)(2,1)S(1)}, u32[]{:S(2)}, u32[]{:S(2)}) collective-permute-start(bf16[528,1024]{1,0:T(8,128)(2,1)S(1)} %collective-permute-done.3.a_up_ref), channel_id=1, source_target_pairs={{0,1},{1,2},{2,3},{3,4},{4,5},{5,6},{6,7},{7,8},{8,9},{9,10},{10,1... | collective-permute-start | bytes 3244040 | tf_op jit(solution)/shard_map/ppermute | solution.py:26
  111.6 0.0 collective-permute-done.5.a_down_ref
  111.6 1.9 %collective-permute-start.6 = (bf16[528,1024]{1,0:T(8,128)(2,1)S(1)}, bf16[528,1024]{1,0:T(8,128)(2,1)S(1)}, u32[]{:S(2)}, u32[]{:S(2)}) collective-permute-start(bf16[528,1024]{1,0:T(8,128)(2,1)S(1)} %collective-permute-done.5.a_down_ref), channel_id=1, source_target_pairs={{1,0},{2,1},{3,2},{4,3},{5,4},{6,5},{7,6},{8,7},{9,8},{10,9},{11,1... | collective-permute-start | bytes 3244040 | tf_op jit(solution)/shard_map/ppermute | solution.py:26
  113.6 5.3 %collective-permute-done.11.rest_up_ref = bf16[2,128,1024]{2,1,0:T(8,128)(2,1)S(1)} collective-permute-done((bf16[2,128,1024]{2,1,0:T(8,128)(2,1)S(1)}, bf16[2,128,1024]{2,1,0:T(8,128)(2,1)S(1)}, u32[]{:S(2)}, u32[]{:S(2)}) %collective-permute-start.11) | collective-permute-done | bytes 524320 | tf_op jit(solution)/shard_map/ppermute | solution.py:31
  118.9 2.2 %collective-permute-done.12.rest_down_ref = bf16[2,128,1024]{2,1,0:T(8,128)(2,1)S(1)} collective-permute-done((bf16[2,128,1024]{2,1,0:T(8,128)(2,1)S(1)}, bf16[2,128,1024]{2,1,0:T(8,128)(2,1)S(1)}, u32[]{:S(2)}, u32[]{:S(2)}) %collective-permute-start.12) | collective-permute-done | bytes 524320 | tf_op jit(solution)/shard_map/ppermute | solution.py:31
  121.1 0.0 copy-done.10
  121.1 0.0 copy-done.13
  121.1 0.0 copy-done.14
  121.1 0.0 copy-start.1
  121.1 0.0 copy-start.3
  121.1 5.1 %shard_map.174 = (f32[512,1024]{1,0:T(8,128)S(1)}, f32[512,1024]{1,0:T(8,128)S(1)}) custom-call(bf16[512,1792]{1,0:T(8,128)(2,1)S(1)} %copy-done.13, bf16[6,128,1024]{2,1,0:T(8,128)(2,1)S(1)} %get-tuple-element.24.hid_ref, bf16[528,1024]{1,0:T(8,128)(2,1)S(1)} %collective-permute-done.3.a_up_ref, ...), custom_call_target="tpu_custom_call" | custom-call | flops 107374182400 | bytes 1 | tf_op jit(solution)/shard_map/pallas_call | solution.py:422
  126.2 14.5 %collective-permute-done.4.f_up_ref = bf16[528,1024]{1,0:T(8,128)(2,1)S(1)} collective-permute-done((bf16[528,1024]{1,0:T(8,128)(2,1)S(1)}, bf16[528,1024]{1,0:T(8,128)(2,1)S(1)}, u32[]{:S(2)}, u32[]{:S(2)}) %collective-permute-start.4) | collective-permute-done | bytes 1081376 | tf_op jit(solution)/shard_map/ppermute | solution.py:26
  140.7 2.2 %collective-permute-done.6.f_down_ref = bf16[528,1024]{1,0:T(8,128)(2,1)S(1)} collective-permute-done((bf16[528,1024]{1,0:T(8,128)(2,1)S(1)}, bf16[528,1024]{1,0:T(8,128)(2,1)S(1)}, u32[]{:S(2)}, u32[]{:S(2)}) %collective-permute-start.6) | collective-permute-done | bytes 1081376 | tf_op jit(solution)/shard_map/ppermute | solution.py:26
  142.9 0.0 copy-done.1
  142.9 3.7 %shard_map.175 = bf16[512,1024]{1,0:T(8,128)(2,1)} custom-call(bf16[512,1024]{1,0:T(8,128)(2,1)S(1)} %copy-done.3, bf16[528,1024]{1,0:T(8,128)(2,1)S(1)} %collective-permute-done.4.f_up_ref, bf16[528,1024]{1,0:T(8,128)(2,1)S(1)} %collective-permute-done.6.f_down_ref, f32[512,1024]{1,0:T(8,128)S(1)} %get-tuple-element.29.part_ref, ...), custom_call_target="tpu_custom_call" | custom-call | flops 1073741824 | bytes 1 | tf_op jit(solution)/shard_map/pallas_call | solution.py:433
  (12 shorter events, 0.0 us)
Async XLA Ops:
  7.3 36.8 %collective-permute-start.2 = (bf16[4,128,1024]{2,1,0:T(8,128)(2,1)}, bf16[4,128,1024]{2,1,0:T(8,128)(2,1)}, u32[]{:S(2)}, u32[]{:S(2)}) collective-permute-start(bf16[4,128,1024]{2,1,0:T(8,128)(2,1)} %get-tuple-element.21), channel_id=1, source_target_pairs={{0,15},{1,0},{2,1},{3,2},{4,3},{5,4},{6,5},{7,6},{8,7},{9,8},{10,9... | collective-permute-start | bytes 3145736 | tf_op jit(solution)/shard_map/ppermute | solution.py:31
  7.8 36.5 %collective-permute-start.1 = (bf16[4,128,1024]{2,1,0:T(8,128)(2,1)}, bf16[4,128,1024]{2,1,0:T(8,128)(2,1)}, u32[]{:S(2)}, u32[]{:S(2)}) collective-permute-start(bf16[4,128,1024]{2,1,0:T(8,128)(2,1)} %get-tuple-element.19.after_ref), channel_id=1, source_target_pairs={{0,1},{1,2},{2,3},{3,4},{4,5},{5,6},{6,7},{7,8},{8,9},{9,10},{10,1... | collective-permute-start | bytes 3145736 | tf_op jit(solution)/shard_map/ppermute | solution.py:31
  13.7 26.0 %all-to-all-start.1 = ((bf16[8,96,1024]{2,1,0:T(8,128)(2,1)}), bf16[8,96,1024]{2,1,0:T(8,128)(2,1)}, u32[]{:S(2)}, u32[]{:S(2)}) async-start(bf16[8,96,1024]{2,1,0:T(8,128)(2,1)} %shard_map.169), calls=%async_computation.1 | async-start | bytes 3145728 | tf_op jit(solution)/shard_map/all_to_all | solution.py:343
  18.0 8.6 %copy-start = (bf16[1,1,4,16,128,128]{5,4,3,2,1,0:T(8,128)(2,1)S(1)}, bf16[1,1,4,16,128,128]{5,4,3,2,1,0:T(8,128)(2,1)}, u32[]{:S(2)}) copy-start(bf16[1,1,4,16,128,128]{5,4,3,2,1,0:T(8,128)(2,1)} %param.26) | copy-start | bytes 6291460
  18.0 8.6 %copy-start.4 = (bf16[512,1024]{1,0:T(8,128)(2,1)S(1)}, bf16[512,1024]{1,0:T(8,128)(2,1)}, u32[]{:S(2)}) copy-start(bf16[512,1024]{1,0:T(8,128)(2,1)} %get-tuple-element.18.after_ref.back_ref) | copy-start | bytes 3145732
  18.0 8.6 %copy-start.6 = (s32[1,1,4,16]{3,2,1,0:T(4,128)S(1)}, s32[1,1,4,16]{3,2,1,0:T(4,128)}, u32[]{:S(2)}) copy-start(s32[1,1,4,16]{3,2,1,0:T(4,128)} %param.27) | copy-start | bytes 772
  31.1 1.2 copy-start.11
  32.3 48.6 %collective-permute-start.8 = (bf16[4,128,1024]{2,1,0:T(8,128)(2,1)}, bf16[4,128,1024]{2,1,0:T(8,128)(2,1)}, u32[]{:S(2)}, u32[]{:S(2)}) collective-permute-start(bf16[4,128,1024]{2,1,0:T(8,128)(2,1)} %get-tuple-element.25), channel_id=1, source_target_pairs={{0,1},{1,2},{2,3},{3,4},{4,5},{5,6},{6,7},{7,8},{8,9},{9,10},{10,1... | collective-permute-start | bytes 3145736 | tf_op jit(solution)/shard_map/ppermute | solution.py:31
  32.3 50.6 %collective-permute-start.9 = (bf16[4,128,1024]{2,1,0:T(8,128)(2,1)}, bf16[4,128,1024]{2,1,0:T(8,128)(2,1)}, u32[]{:S(2)}, u32[]{:S(2)}) collective-permute-start(bf16[4,128,1024]{2,1,0:T(8,128)(2,1)} %get-tuple-element.26), channel_id=1, source_target_pairs={{0,15},{1,0},{2,1},{3,2},{4,3},{5,4},{6,5},{7,6},{8,7},{9,8},{10,9... | collective-permute-start | bytes 3145736 | tf_op jit(solution)/shard_map/ppermute | solution.py:31
  34.4 9.7 %copy-start.16 = (s32[1,1,4]{2,1,0:T(1,128)S(1)}, s32[1,1,4]{2,1,0:T(1,128)}, u32[]{:S(2)}) copy-start(s32[1,1,4]{2,1,0:T(1,128)} %param.29) | copy-start | bytes 52
  34.4 9.7 %copy-start.17 = (s32[4]{0:T(128)S(1)}, s32[4]{0:T(128)}, u32[]{:S(2)}) copy-start(s32[4]{0:T(128)} %constant.28.clone) | copy-start | bytes 52
  34.4 14.0 %copy-start.15 = (s32[1,1,512]{2,1,0:T(1,128)S(1)}, s32[1,1,512]{2,1,0:T(1,128)}, u32[]{:S(2)}) copy-start(s32[1,1,512]{2,1,0:T(1,128)} %param.25) | copy-start | bytes 6148
  39.7 34.4 %all-to-all-start = ((bf16[8,192,768]{2,1,0:T(8,128)(2,1)}), bf16[8,192,768]{2,1,0:T(8,128)(2,1)}, u32[]{:S(2)}, u32[]{:S(2)}) async-start(bf16[8,192,768]{2,1,0:T(8,128)(2,1)} %shard_map.168.after_ref), calls=%async_computation | async-start | bytes 4718592 | tf_op jit(solution)/shard_map/all_to_all | solution.py:362
  44.1 38.8 %collective-permute-start.10 = (bf16[4,128,1024]{2,1,0:T(8,128)(2,1)}, bf16[4,128,1024]{2,1,0:T(8,128)(2,1)}, u32[]{:S(2)}, u32[]{:S(2)}) collective-permute-start(bf16[4,128,1024]{2,1,0:T(8,128)(2,1)} %collective-permute-done.2.after_down_ref), channel_id=1, source_target_pairs={{0,15},{1,0},{2,1},{3,2},{4,3},{5,4},{6,5},{7,6},{8,7},{9,8},{10,9... | collective-permute-start | bytes 3145736 | tf_op jit(solution)/shard_map/ppermute | solution.py:31
  44.2 38.7 %collective-permute-start.7 = (bf16[4,128,1024]{2,1,0:T(8,128)(2,1)}, bf16[4,128,1024]{2,1,0:T(8,128)(2,1)}, u32[]{:S(2)}, u32[]{:S(2)}) collective-permute-start(bf16[4,128,1024]{2,1,0:T(8,128)(2,1)} %collective-permute-done.1.after_up_ref), channel_id=1, source_target_pairs={{0,1},{1,2},{2,3},{3,4},{4,5},{5,6},{6,7},{7,8},{8,9},{9,10},{10,1... | collective-permute-start | bytes 3145736 | tf_op jit(solution)/shard_map/ppermute | solution.py:31
  48.4 25.7 %collective-permute-start = (bf16[768,1024]{1,0:T(8,128)(2,1)}, bf16[768,1024]{1,0:T(8,128)(2,1)}, u32[]{:S(2)}, u32[]{:S(2)}) collective-permute-start(bf16[768,1024]{1,0:T(8,128)(2,1)} %bitcast.4.mine_ref), channel_id=1, source_target_pairs={{0,16},{16,0},{32,48},{48,32},{64,80},{80,64},{96,112},{112,96},{1... | collective-permute-start | bytes 4718600 | tf_op jit(solution)/shard_map/ppermute | solution.py:363
  48.4 1.2 copy-start.2
  49.6 1.2 copy-start.5
  50.8 1.6 %copy-start.9 = (bf16[1024,1024]{1,0:T(8,128)(2,1)S(1)}, bf16[1024,1024]{1,0:T(8,128)(2,1)}, u32[]{:S(2)}) copy-start(bf16[1024,1024]{1,0:T(8,128)(2,1)} %w_ref.6) | copy-start | bytes 6291460
  52.4 1.5 %copy-start.12 = (bf16[512,1792]{1,0:T(8,128)(2,1)S(1)}, bf16[512,1792]{1,0:T(8,128)(2,1)}, u32[]{:S(2)}) copy-start(bf16[512,1792]{1,0:T(8,128)(2,1)} %copy-done.11) | copy-start | bytes 5505028
  53.9 20.2 %copy-start.7 = (s32[1,1,4,4]{3,2,1,0:T(4,128)S(1)}, s32[1,1,4,4]{3,2,1,0:T(4,128)}, u32[]{:S(2)}) copy-start(s32[1,1,4,4]{3,2,1,0:T(4,128)} %param.28) | copy-start | bytes 196
  53.9 20.2 %copy-start.8 = (f32[1024]{0:T(1024)S(1)}, f32[1024]{0:T(1024)}, u32[]{:S(2)}) copy-start(f32[1024]{0:T(1024)} %param.21) | copy-start | bytes 12292
  80.6 27.0 %collective-permute-start.3 = (bf16[528,1024]{1,0:T(8,128)(2,1)S(1)}, bf16[528,1024]{1,0:T(8,128)(2,1)S(1)}, u32[]{:S(2)}, u32[]{:S(2)}) collective-permute-start(bf16[528,1024]{1,0:T(8,128)(2,1)S(1)} %get-tuple-element.22), channel_id=1, source_target_pairs={{0,1},{1,2},{2,3},{3,4},{4,5},{5,6},{6,7},{7,8},{8,9},{9,10},{10,1... | collective-permute-start | bytes 3244040 | tf_op jit(solution)/shard_map/ppermute | solution.py:31
  80.9 30.7 %collective-permute-start.5 = (bf16[528,1024]{1,0:T(8,128)(2,1)S(1)}, bf16[528,1024]{1,0:T(8,128)(2,1)S(1)}, u32[]{:S(2)}, u32[]{:S(2)}) collective-permute-start(bf16[528,1024]{1,0:T(8,128)(2,1)S(1)} %get-tuple-element.23), channel_id=1, source_target_pairs={{0,15},{1,0},{2,1},{3,2},{4,3},{5,4},{6,5},{7,6},{8,7},{9,8},{10,9... | collective-permute-start | bytes 3244040 | tf_op jit(solution)/shard_map/ppermute | solution.py:31
  82.9 38.2 %copy-start.10 = (bf16[1024,1024]{1,0:T(8,128)(2,1)S(1)}, bf16[1024,1024]{1,0:T(8,128)(2,1)}, u32[]{:S(2)}) copy-start(bf16[1024,1024]{1,0:T(8,128)(2,1)} %w_ref.6) | copy-start | bytes 6291460
  82.9 38.2 %copy-start.13 = (bf16[512,1792]{1,0:T(8,128)(2,1)S(1)}, bf16[512,1792]{1,0:T(8,128)(2,1)}, u32[]{:S(2)}) copy-start(bf16[512,1792]{1,0:T(8,128)(2,1)} %copy-done.11) | copy-start | bytes 5505028
  82.9 38.2 %copy-start.14 = (f32[1024]{0:T(1024)S(1)}, f32[1024]{0:T(1024)}, u32[]{:S(2)}) copy-start(f32[1024]{0:T(1024)} %param.24) | copy-start | bytes 12292
  87.9 31.0 %collective-permute-start.11 = (bf16[2,128,1024]{2,1,0:T(8,128)(2,1)S(1)}, bf16[2,128,1024]{2,1,0:T(8,128)(2,1)S(1)}, u32[]{:S(2)}, u32[]{:S(2)}) collective-permute-start(bf16[2,128,1024]{2,1,0:T(8,128)(2,1)S(1)} %get-tuple-element.27), channel_id=1, source_target_pairs={{0,1},{1,2},{2,3},{3,4},{4,5},{5,6},{6,7},{7,8},{8,9},{9,10},{10,1... | collective-permute-start | bytes 1572872 | tf_op jit(solution)/shard_map/ppermute | solution.py:31
  90.2 30.9 %collective-permute-start.12 = (bf16[2,128,1024]{2,1,0:T(8,128)(2,1)S(1)}, bf16[2,128,1024]{2,1,0:T(8,128)(2,1)S(1)}, u32[]{:S(2)}, u32[]{:S(2)}) collective-permute-start(bf16[2,128,1024]{2,1,0:T(8,128)(2,1)S(1)} %get-tuple-element.28), channel_id=1, source_target_pairs={{0,15},{1,0},{2,1},{3,2},{4,3},{5,4},{6,5},{7,6},{8,7},{9,8},{10,9... | collective-permute-start | bytes 1572872 | tf_op jit(solution)/shard_map/ppermute | solution.py:31
  107.6 33.0 %collective-permute-start.4 = (bf16[528,1024]{1,0:T(8,128)(2,1)S(1)}, bf16[528,1024]{1,0:T(8,128)(2,1)S(1)}, u32[]{:S(2)}, u32[]{:S(2)}) collective-permute-start(bf16[528,1024]{1,0:T(8,128)(2,1)S(1)} %collective-permute-done.3.a_up_ref), channel_id=1, source_target_pairs={{0,1},{1,2},{2,3},{3,4},{4,5},{5,6},{6,7},{7,8},{8,9},{9,10},{10,1... | collective-permute-start | bytes 3244040 | tf_op jit(solution)/shard_map/ppermute | solution.py:26
  111.6 31.2 %collective-permute-start.6 = (bf16[528,1024]{1,0:T(8,128)(2,1)S(1)}, bf16[528,1024]{1,0:T(8,128)(2,1)S(1)}, u32[]{:S(2)}, u32[]{:S(2)}) collective-permute-start(bf16[528,1024]{1,0:T(8,128)(2,1)S(1)} %collective-permute-done.5.a_down_ref), channel_id=1, source_target_pairs={{1,0},{2,1},{3,2},{4,3},{5,4},{6,5},{7,6},{8,7},{9,8},{10,9},{11,1... | collective-permute-start | bytes 3244040 | tf_op jit(solution)/shard_map/ppermute | solution.py:26
  121.1 21.8 %copy-start.1 = (bf16[1024,1024]{1,0:T(8,128)(2,1)S(1)}, bf16[1024,1024]{1,0:T(8,128)(2,1)}, u32[]{:S(2)}) copy-start(bf16[1024,1024]{1,0:T(8,128)(2,1)} %w_ref.7) | copy-start | bytes 6291460
  121.1 21.8 %copy-start.3 = (bf16[512,1024]{1,0:T(8,128)(2,1)S(1)}, bf16[512,1024]{1,0:T(8,128)(2,1)}, u32[]{:S(2)}) copy-start(bf16[512,1024]{1,0:T(8,128)(2,1)} %get-tuple-element.17.fold_ref) | copy-start | bytes 3145732

commit v4 on v3

--- a/solution.py
+++ b/solution.py
@@ -134,7 +134,7 @@
     down_ref[...] = tn_dot(fold_ref[:, half:], back).astype(jnp.bfloat16).reshape(down_ref.shape)
 
 
-def near_kernel(adj_ref, src_ref, back_ref, after_ref, fold_ref, up_ref, down_ref, acc_ref):
+def near_kernel(adj_ref, src_ref, back_ref, fold_ref, up_ref, down_ref, acc_ref):
     acc_ref[...] = jnp.zeros_like(acc_ref)
     for seed in range(adj_ref.shape[0]):
         rows = pl.ds(seed * TILE, TILE)
@@ -345,6 +345,14 @@
     got_far_up = shifted(far_up, 1)
     got_far_down = shifted(far_down, -1)
 
+    fold_near, near_up, near_down = call(
+        near_kernel,
+        (shape((seeds, near_cols), bf16), quad, quad),
+        [VMEM, SMEM, VMEM],
+        [pltpu.VMEM((seeds, near_cols), f32)],
+        vmem=24,
+    )(blocks, sources, back)
+
     sent = pl.pallas_call(
         gather_kernel,
         grid=(feat_count,),
@@ -358,18 +366,11 @@
         out_shape=shape((feat_count, 2 * width, row_dev), bf16),
         cost_estimate=pl.CostEstimate(flops=100 * GIGA, bytes_accessed=1, transcendentals=0),
         compiler_params=pltpu.CompilerParams(vmem_limit_bytes=56 * MIB),
-    )(src_one.T, features, adj_one, back)
+    )(src_one.T, features, adj_one, near_up)
     taken = lax.all_to_all(sent, "feat", 0, 0)
     swapped = lax.ppermute(halves, "feat", [(i, i ^ 1) for i in range(feat_count)])
     odd = (lax.axis_index("feat") % 2).astype(jnp.int32)[None]
 
-    fold_near, near_up, near_down = call(
-        near_kernel,
-        (shape((seeds, near_cols), bf16), quad, quad),
-        [VMEM, SMEM, VMEM, ANY],
-        [pltpu.VMEM((seeds, near_cols), f32)],
-        vmem=24,
-    )(blocks, sources, back, sent)
     grad_1 = shifted(near_up, 1)
     grad_2 = shifted(near_down, -1)
     grad_0 = shifted(got_far_up, 1)
@@ -383,7 +384,7 @@
         vmem=28,
     )(fold_near, back, upstream, w_self_two, seed_rows[0], got_far_up, got_far_down)
 
-    chunk = hid // 2
+    chunk = hid
     hidden, h_up, h_down = pl.pallas_call(
         hidden_kernel,
         grid=(hid // chunk,),
@@ -407,7 +408,7 @@
             pltpu.VMEM((row_dev, 2 * width * feat_count), bf16),
         ],
         cost_estimate=pl.CostEstimate(flops=GIGA, bytes_accessed=1, transcendentals=0),
-        compiler_params=pltpu.CompilerParams(vmem_limit_bytes=24 * MIB),
+        compiler_params=pltpu.CompilerParams(vmem_limit_bytes=30 * MIB),
     )(taken, halves, swapped, bias_one[None], odd, lists, counts, local)
     got_h_up = shifted(h_up, 1)
     got_h_down = shifted(h_down, -1)

time: 148 us -> 147 us (level)
  starting transfers between devices: 29.6 us -> 31.7 us
  waiting for transfers between devices: 64.3 us -> 62.2 us
    all_to_all x1, waiting for transfers between devices: 5.34 us -> 3.49 us  [shards(): halves = lax.all_to_all(halves, 'feat', 0, 0)]
    ppermute x10, starting transfers between devices: 15 us -> 16.8 us  [shifted(): lax.ppermute(shard, 'dom', [(i, (i + by) % count) for i in range(count)])]
  transfers between devices with their start and end apart: 15 -> 15, of which waited for: 7 -> 7; matrix products, arithmetic and copies ran while one was open for 0% -> 0% of each run, Pallas kernels for 24% -> 23%
where the time goes in v4:
time: 147 us; the launch traced here: 146 us
  waiting for transfers between devices  62.2 us (42%)
  Pallas kernels  44.1 us (30%)
  starting transfers between devices  31.7 us (22%)
  local copies, waits for them, and re-layouts  6.85 us (5%)
    ppermute x10, waiting for transfers between devices, shifted(): lax.ppermute(shard, 'dom', [(i, (i + by) % count) for i in range(count)])  24.7 us
    all_to_all x1, waiting for transfers between devices, shards(): taken = lax.all_to_all(sent, 'feat', 0, 0)  17.3 us
    ppermute x10, starting transfers between devices, shifted(): lax.ppermute(shard, 'dom', [(i, (i + by) % count) for i in range(count)])  16.8 us
    ppermute x2, waiting for transfers between devices, open_shift(): lax.ppermute(shard, 'dom', [(i, i + by) for i in range(count) if 0 <= i +...  16.7 us
    pallas_call x1, Pallas kernels, shards(): pl.pallas_call(gather_kernel, grid=(feat_count,), in_specs=[SMEM, pl.Bloc...  8.39 us
    unnamed x36, local copies, waits for them, and re-layouts  6.85 us
    pallas_call x1, Pallas kernels, shards(): call(far_kernel, (shape((seeds, hid), bf16), shape((seeds, far_cols), bf1...  6.65 us
    ppermute x2, starting transfers between devices, open_shift(): lax.ppermute(shard, 'dom', [(i, i + by) for i in range(count) if 0 <= i +...  6.11 us
  transfers between devices with their start and end apart: 15, of which 7 were waited for; matrix products, arithmetic and copies ran while one was open for 0% of the time, Pallas kernels for 23%

profile of v4, /device:TPU:104, one launch (start us, length us, event | category | flops | bytes accessed | tf_op | source)
XLA Modules:
  0.0 145.8 jit_solution(13171240430642101940)
XLA Ops:
  0.6 6.7 %shard_map.167 = (bf16[512,1024]{1,0:T(8,128)(2,1)}, bf16[512,1024]{1,0:T(8,128)(2,1)}, bf16[4,128,1024]{2,1,0:T(8,128)(2,1)}, bf16[4,128,1024]{2,1,0:T(8,128)(2,1)}) custom-call(bf16[4,16,128,128]{3,2,1,0:T(8,128)(2,1)} %bitcast.14, s32[4,16]{1,0:T(4,128)} %bitcast.21, bf16[512,1024]{1,0:T(8,128)(2,1)} %bitcast.16, bf16[1024,1024]{1,0:T(8,128)(2,1)} %w_ref.7), custom_call_target="tpu_custom_call" | custom-call | flops 1073741824 | bytes 1 | tf_op jit(solution)/shard_map/pallas_call | solution.py:322
  7.3 0.5 collective-permute-start.2
  7.8 3.7 %collective-permute-start.1 = (bf16[4,128,1024]{2,1,0:T(8,128)(2,1)}, bf16[4,128,1024]{2,1,0:T(8,128)(2,1)}, u32[]{:S(2)}, u32[]{:S(2)}) collective-permute-start(bf16[4,128,1024]{2,1,0:T(8,128)(2,1)} %get-tuple-element.20.after_ref), channel_id=1, source_target_pairs={{0,1},{1,2},{2,3},{3,4},{4,5},{5,6},{6,7},{7,8},{8,9},{9,10},{10,1... | collective-permute-start | bytes 3145736 | tf_op jit(solution)/shard_map/ppermute | solution.py:31
  11.5 2.3 %shard_map.170 = bf16[8,96,1024]{2,1,0:T(8,128)(2,1)} custom-call(bf16[96,1024]{1,0:T(8,128)(2,1)} %self_ref.1, bf16[96,1024]{1,0:T(8,128)(2,1)} %neigh_ref.1, bf16[4,128,1024]{2,1,0:T(8,128)(2,1)} %get-tuple-element.20.after_ref), custom_call_target="tpu_custom_call" | custom-call | flops 1073741824 | bytes 1 | tf_op jit(solution)/shard_map/pallas_call | solution.py:335
  13.8 0.0 copy-start.1
  13.8 0.0 copy-start.6
  13.8 4.4 %all-to-all-start.1 = ((bf16[8,96,1024]{2,1,0:T(8,128)(2,1)}), bf16[8,96,1024]{2,1,0:T(8,128)(2,1)}, u32[]{:S(2)}, u32[]{:S(2)}) async-start(bf16[8,96,1024]{2,1,0:T(8,128)(2,1)} %shard_map.170), calls=%async_computation.1 | async-start | bytes 3145728 | tf_op jit(solution)/shard_map/all_to_all | solution.py:343
  18.3 0.0 copy-done.9
  18.3 0.0 copy-done.1
  18.3 0.0 copy-done.6
  18.3 4.4 %shard_map.168 = (bf16[512,1792]{1,0:T(8,128)(2,1)S(1)}, bf16[4,128,1024]{2,1,0:T(8,128)(2,1)}, bf16[4,128,1024]{2,1,0:T(8,128)(2,1)}) custom-call(bf16[4,16,128,128]{3,2,1,0:T(8,128)(2,1)S(1)} %bitcast.15, s32[4,16]{1,0:T(4,128)S(1)} %bitcast.22, bf16[512,1024]{1,0:T(8,128)(2,1)S(1)} %copy-done.9), custom_call_target="tpu_custom_call" | custom-call | flops 1073741824 | bytes 1 | tf_op jit(solution)/shard_map/pallas_call | solution.py:348
  22.7 1.2 copy-done.13
  23.9 0.0 collective-permute-start.9
  23.9 4.1 %collective-permute-start.8 = (bf16[4,128,1024]{2,1,0:T(8,128)(2,1)}, bf16[4,128,1024]{2,1,0:T(8,128)(2,1)}, u32[]{:S(2)}, u32[]{:S(2)}) collective-permute-start(bf16[4,128,1024]{2,1,0:T(8,128)(2,1)} %get-tuple-element.19.after_ref), channel_id=1, source_target_pairs={{0,1},{1,2},{2,3},{3,4},{4,5},{5,6},{6,7},{7,8},{8,9},{9,10},{10,1... | collective-permute-start | bytes 3145736 | tf_op jit(solution)/shard_map/ppermute | solution.py:31
  28.1 8.4 %shard_map.169 = bf16[8,192,768]{2,1,0:T(8,128)(2,1)} custom-call(s32[4,48]{1,0:T(4,128)} %bitcast.28, bf16[96,6144]{1,0:T(8,128)(2,1)} %feat_ref.1, bf16[48,4,128,128]{3,2,1,0:T(8,128)(2,1)} %adj_ref.1, bf16[4,128,1024]{2,1,0:T(8,128)(2,1)} %get-tuple-element.19.after_ref), custom_call_target="tpu_custom_call" | custom-call | flops 107374182400 | bytes 1 | tf_op jit(solution)/shard_map/pallas_call | solution.py:356
  36.5 3.5 %all-to-all-done.1 = bf16[8,96,1024]{2,1,0:T(8,128)(2,1)} async-done(((bf16[8,96,1024]{2,1,0:T(8,128)(2,1)}), bf16[8,96,1024]{2,1,0:T(8,128)(2,1)}, u32[]{:S(2)}, u32[]{:S(2)}) %all-to-all-start.1) | async-done | bytes 1572896 | tf_op jit(solution)/shard_map/all_to_all | solution.py:343
  39.9 4.4 %all-to-all-start = ((bf16[8,192,768]{2,1,0:T(8,128)(2,1)}), bf16[8,192,768]{2,1,0:T(8,128)(2,1)}, u32[]{:S(2)}, u32[]{:S(2)}) async-start(bf16[8,192,768]{2,1,0:T(8,128)(2,1)} %shard_map.169), calls=%async_computation | async-start | bytes 4718592 | tf_op jit(solution)/shard_map/all_to_all | solution.py:370
  44.3 0.0 copy-done.16
  44.3 0.0 copy-done.17
  44.4 0.0 collective-permute-done.2.after_down_ref
  44.4 0.1 collective-permute-start.10
  44.5 0.0 collective-permute-done.1.after_up_ref
  44.5 4.1 %collective-permute-start.7 = (bf16[4,128,1024]{2,1,0:T(8,128)(2,1)}, bf16[4,128,1024]{2,1,0:T(8,128)(2,1)}, u32[]{:S(2)}, u32[]{:S(2)}) collective-permute-start(bf16[4,128,1024]{2,1,0:T(8,128)(2,1)} %collective-permute-done.1.after_up_ref), channel_id=1, source_target_pairs={{0,1},{1,2},{2,3},{3,4},{4,5},{5,6},{6,7},{7,8},{8,9},{9,10},{10,1... | collective-permute-start | bytes 3145736 | tf_op jit(solution)/shard_map/ppermute | solution.py:31
  48.6 0.0 collective-permute-start
  48.6 0.0 copy-done.12
  48.6 1.2 copy-done.2
  49.8 1.6 %copy-done.7 = bf16[1024,1024]{1,0:T(8,128)(2,1)S(1)} copy-done((bf16[1024,1024]{1,0:T(8,128)(2,1)S(1)}, bf16[1024,1024]{1,0:T(8,128)(2,1)}, u32[]{:S(2)}) %copy-start.7) | copy-done | bytes 2097176
  51.4 1.2 copy-done.10
  52.7 1.5 %copy-done.14 = bf16[512,1792]{1,0:T(8,128)(2,1)S(1)} copy-done((bf16[512,1792]{1,0:T(8,128)(2,1)S(1)}, bf16[512,1792]{1,0:T(8,128)(2,1)}, u32[]{:S(2)}) %copy-start.14) | copy-done | bytes 1835032
  54.2 2.9 %shard_map.171.after_ref.local_ref = f32[768,1024]{1,0:T(8,128)S(1)} custom-call(bf16[512,1792]{1,0:T(8,128)(2,1)S(1)} %copy-done.14, bf16[512,1024]{1,0:T(8,128)(2,1)S(1)} %copy-done.10, bf16[512,1024]{1,0:T(8,128)(2,1)S(1)} %bitcast.17, bf16[1024,1024]{1,0:T(8,128)(2,1)S(1)} %copy-done.7, s32[1,512]{1,0:T(1,128)S(1)} %bitcast.24, ...), custom_call_target="tpu_custom_call" | custom-call | flops 21474836480 | bytes 1 | tf_op jit(solution)/shard_map/pallas_call | solution.py:379
  57.1 17.3 %all-to-all-done.in_ref = bf16[8,192,768]{2,1,0:T(8,128)(2,1)} async-done(((bf16[8,192,768]{2,1,0:T(8,128)(2,1)}), bf16[8,192,768]{2,1,0:T(8,128)(2,1)}, u32[]{:S(2)}, u32[]{:S(2)}) %all-to-all-start) | async-done | bytes 2359328 | tf_op jit(solution)/shard_map/all_to_all | solution.py:370
  74.3 0.0 collective-permute-done.other_ref
  74.3 0.0 copy-done.4
  74.3 0.0 copy-done.5
  74.3 5.6 %shard_map.172 = (bf16[6,128,1024]{2,1,0:T(8,128)(2,1)S(1)}, bf16[528,1024]{1,0:T(8,128)(2,1)S(1)}, bf16[528,1024]{1,0:T(8,128)(2,1)S(1)}) custom-call(bf16[8,192,768]{2,1,0:T(8,128)(2,1)} %all-to-all-done.in_ref, bf16[768,1024]{1,0:T(8,128)(2,1)} %bitcast.4.mine_ref, bf16[768,1024]{1,0:T(8,128)(2,1)} %collective-permute-done.other_ref, ...), custom_call_target="tpu_custom_call" | custom-call | flops 1073741824 | bytes 1 | tf_op jit(solution)/shard_map/pallas_call | solution.py:388
  79.9 0.1 collective-permute-start.3
  80.0 0.0 collective-permute-done.9.from_2_ref
  80.0 2.0 %collective-permute-start.5 = (bf16[528,1024]{1,0:T(8,128)(2,1)S(1)}, bf16[528,1024]{1,0:T(8,128)(2,1)S(1)}, u32[]{:S(2)}, u32[]{:S(2)}) collective-permute-start(bf16[528,1024]{1,0:T(8,128)(2,1)S(1)} %get-tuple-element.24), channel_id=1, source_target_pairs={{0,15},{1,0},{2,1},{3,2},{4,3},{5,4},{6,5},{7,6},{8,7},{9,8},{10,9... | collective-permute-start | bytes 3244040 | tf_op jit(solution)/shard_map/ppermute | solution.py:31
  82.0 0.0 collective-permute-done.8.from_1_ref
  82.0 0.0 collective-permute-done.10.from_3_ref
  82.0 0.0 collective-permute-done.7.from_0_ref
  82.1 0.0 copy-start.8
  82.1 0.0 copy-start.11
  82.1 0.0 copy-start.15
  82.1 5.1 %shard_map.173 = (f32[768,1024]{1,0:T(8,128)}, bf16[2,128,1024]{2,1,0:T(8,128)(2,1)S(1)}, bf16[2,128,1024]{2,1,0:T(8,128)(2,1)S(1)}) custom-call(f32[768,1024]{1,0:T(8,128)S(1)} %shard_map.171.after_ref.local_ref, bf16[4,128,1024]{2,1,0:T(8,128)(2,1)} %collective-permute-done.7.from_0_ref, bf16[4,128,1024]{2,1,0:T(8,128)(2,1)} %collective-permute-done.8.from_1_ref, ...), custom_call_target="tpu_custom_call" | custom-call | flops 1073741824 | bytes 1 | tf_op jit(solution)/shard_map/pallas_call | solution.py:417
  87.2 2.1 %collective-permute-start.11 = (bf16[2,128,1024]{2,1,0:T(8,128)(2,1)S(1)}, bf16[2,128,1024]{2,1,0:T(8,128)(2,1)S(1)}, u32[]{:S(2)}, u32[]{:S(2)}) collective-permute-start(bf16[2,128,1024]{2,1,0:T(8,128)(2,1)S(1)} %get-tuple-element.27), channel_id=1, source_target_pairs={{0,1},{1,2},{2,3},{3,4},{4,5},{5,6},{6,7},{7,8},{8,9},{9,10},{10,1... | collective-permute-start | bytes 1572872 | tf_op jit(solution)/shard_map/ppermute | solution.py:31
  89.4 0.0 collective-permute-start.12
  89.4 17.4 %collective-permute-done.3.a_up_ref = bf16[528,1024]{1,0:T(8,128)(2,1)S(1)} collective-permute-done((bf16[528,1024]{1,0:T(8,128)(2,1)S(1)}, bf16[528,1024]{1,0:T(8,128)(2,1)S(1)}, u32[]{:S(2)}, u32[]{:S(2)}) %collective-permute-start.3) | collective-permute-done | bytes 1081376 | tf_op jit(solution)/shard_map/ppermute | solution.py:31
  106.8 4.0 %collective-permute-start.4 = (bf16[528,1024]{1,0:T(8,128)(2,1)S(1)}, bf16[528,1024]{1,0:T(8,128)(2,1)S(1)}, u32[]{:S(2)}, u32[]{:S(2)}) collective-permute-start(bf16[528,1024]{1,0:T(8,128)(2,1)S(1)} %collective-permute-done.3.a_up_ref), channel_id=1, source_target_pairs={{0,1},{1,2},{2,3},{3,4},{4,5},{5,6},{6,7},{7,8},{8,9},{9,10},{10,1... | collective-permute-start | bytes 3244040 | tf_op jit(solution)/shard_map/ppermute | solution.py:26
  110.8 0.0 collective-permute-done.5.a_down_ref
  110.8 2.1 %collective-permute-start.6 = (bf16[528,1024]{1,0:T(8,128)(2,1)S(1)}, bf16[528,1024]{1,0:T(8,128)(2,1)S(1)}, u32[]{:S(2)}, u32[]{:S(2)}) collective-permute-start(bf16[528,1024]{1,0:T(8,128)(2,1)S(1)} %collective-permute-done.5.a_down_ref), channel_id=1, source_target_pairs={{1,0},{2,1},{3,2},{4,3},{5,4},{6,5},{7,6},{8,7},{9,8},{10,9},{11,1... | collective-permute-start | bytes 3244040 | tf_op jit(solution)/shard_map/ppermute | solution.py:26
  112.9 5.1 %collective-permute-done.11.rest_up_ref = bf16[2,128,1024]{2,1,0:T(8,128)(2,1)S(1)} collective-permute-done((bf16[2,128,1024]{2,1,0:T(8,128)(2,1)S(1)}, bf16[2,128,1024]{2,1,0:T(8,128)(2,1)S(1)}, u32[]{:S(2)}, u32[]{:S(2)}) %collective-permute-start.11) | collective-permute-done | bytes 524320 | tf_op jit(solution)/shard_map/ppermute | solution.py:31
  118.0 2.2 %collective-permute-done.12.rest_down_ref = bf16[2,128,1024]{2,1,0:T(8,128)(2,1)S(1)} collective-permute-done((bf16[2,128,1024]{2,1,0:T(8,128)(2,1)S(1)}, bf16[2,128,1024]{2,1,0:T(8,128)(2,1)S(1)}, u32[]{:S(2)}, u32[]{:S(2)}) %collective-permute-start.12) | collective-permute-done | bytes 524320 | tf_op jit(solution)/shard_map/ppermute | solution.py:31
  120.2 0.0 copy-done.8
  120.2 0.0 copy-done.11
  120.2 0.0 copy-done.15
  120.2 0.0 copy-start
  120.3 0.0 copy-start.3
  120.3 5.1 %shard_map.174 = (f32[512,1024]{1,0:T(8,128)S(1)}, f32[512,1024]{1,0:T(8,128)S(1)}) custom-call(bf16[512,1792]{1,0:T(8,128)(2,1)S(1)} %copy-done.15, bf16[6,128,1024]{2,1,0:T(8,128)(2,1)S(1)} %get-tuple-element.25.hid_ref, bf16[528,1024]{1,0:T(8,128)(2,1)S(1)} %collective-permute-done.3.a_up_ref, ...), custom_call_target="tpu_custom_call" | custom-call | flops 107374182400 | bytes 1 | tf_op jit(solution)/shard_map/pallas_call | solution.py:423
  125.3 14.5 %collective-permute-done.4.f_up_ref = bf16[528,1024]{1,0:T(8,128)(2,1)S(1)} collective-permute-done((bf16[528,1024]{1,0:T(8,128)(2,1)S(1)}, bf16[528,1024]{1,0:T(8,128)(2,1)S(1)}, u32[]{:S(2)}, u32[]{:S(2)}) %collective-permute-start.4) | collective-permute-done | bytes 1081376 | tf_op jit(solution)/shard_map/ppermute | solution.py:26
  139.8 2.2 %collective-permute-done.6.f_down_ref = bf16[528,1024]{1,0:T(8,128)(2,1)S(1)} collective-permute-done((bf16[528,1024]{1,0:T(8,128)(2,1)S(1)}, bf16[528,1024]{1,0:T(8,128)(2,1)S(1)}, u32[]{:S(2)}, u32[]{:S(2)}) %collective-permute-start.6) | collective-permute-done | bytes 1081376 | tf_op jit(solution)/shard_map/ppermute | solution.py:26
  142.0 0.0 copy-done
  142.0 0.0 copy-done.3
  142.0 3.7 %shard_map.175 = bf16[512,1024]{1,0:T(8,128)(2,1)} custom-call(bf16[512,1024]{1,0:T(8,128)(2,1)S(1)} %copy-done.3, bf16[528,1024]{1,0:T(8,128)(2,1)S(1)} %collective-permute-done.4.f_up_ref, bf16[528,1024]{1,0:T(8,128)(2,1)S(1)} %collective-permute-done.6.f_down_ref, f32[512,1024]{1,0:T(8,128)S(1)} %get-tuple-element.29.part_ref, ...), custom_call_target="tpu_custom_call" | custom-call | flops 1073741824 | bytes 1 | tf_op jit(solution)/shard_map/pallas_call | solution.py:434
  (12 shorter events, 0.0 us)
Async XLA Ops:
  7.3 37.1 %collective-permute-start.2 = (bf16[4,128,1024]{2,1,0:T(8,128)(2,1)}, bf16[4,128,1024]{2,1,0:T(8,128)(2,1)}, u32[]{:S(2)}, u32[]{:S(2)}) collective-permute-start(bf16[4,128,1024]{2,1,0:T(8,128)(2,1)} %get-tuple-element.22), channel_id=1, source_target_pairs={{0,15},{1,0},{2,1},{3,2},{4,3},{5,4},{6,5},{7,6},{8,7},{9,8},{10,9... | collective-permute-start | bytes 3145736 | tf_op jit(solution)/shard_map/ppermute | solution.py:31
  7.8 36.7 %collective-permute-start.1 = (bf16[4,128,1024]{2,1,0:T(8,128)(2,1)}, bf16[4,128,1024]{2,1,0:T(8,128)(2,1)}, u32[]{:S(2)}, u32[]{:S(2)}) collective-permute-start(bf16[4,128,1024]{2,1,0:T(8,128)(2,1)} %get-tuple-element.20.after_ref), channel_id=1, source_target_pairs={{0,1},{1,2},{2,3},{3,4},{4,5},{5,6},{6,7},{7,8},{8,9},{9,10},{10,1... | collective-permute-start | bytes 3145736 | tf_op jit(solution)/shard_map/ppermute | solution.py:31
  11.5 6.8 %copy-start.9 = (bf16[512,1024]{1,0:T(8,128)(2,1)S(1)}, bf16[512,1024]{1,0:T(8,128)(2,1)}, u32[]{:S(2)}) copy-start(bf16[512,1024]{1,0:T(8,128)(2,1)} %get-tuple-element.18.back_ref) | copy-start | bytes 3145732
  13.8 4.5 %copy-start.1 = (bf16[1,1,4,16,128,128]{5,4,3,2,1,0:T(8,128)(2,1)S(1)}, bf16[1,1,4,16,128,128]{5,4,3,2,1,0:T(8,128)(2,1)}, u32[]{:S(2)}) copy-start(bf16[1,1,4,16,128,128]{5,4,3,2,1,0:T(8,128)(2,1)} %param.26) | copy-start | bytes 6291460
  13.8 4.5 %copy-start.6 = (s32[1,1,4,16]{3,2,1,0:T(4,128)S(1)}, s32[1,1,4,16]{3,2,1,0:T(4,128)}, u32[]{:S(2)}) copy-start(s32[1,1,4,16]{3,2,1,0:T(4,128)} %param.27) | copy-start | bytes 772
  13.8 26.1 %all-to-all-start.1 = ((bf16[8,96,1024]{2,1,0:T(8,128)(2,1)}), bf16[8,96,1024]{2,1,0:T(8,128)(2,1)}, u32[]{:S(2)}, u32[]{:S(2)}) async-start(bf16[8,96,1024]{2,1,0:T(8,128)(2,1)} %shard_map.170), calls=%async_computation.1 | async-start | bytes 3145728 | tf_op jit(solution)/shard_map/all_to_all | solution.py:343
  22.7 1.2 copy-start.13
  23.9 56.1 %collective-permute-start.9 = (bf16[4,128,1024]{2,1,0:T(8,128)(2,1)}, bf16[4,128,1024]{2,1,0:T(8,128)(2,1)}, u32[]{:S(2)}, u32[]{:S(2)}) collective-permute-start(bf16[4,128,1024]{2,1,0:T(8,128)(2,1)} %get-tuple-element.26), channel_id=1, source_target_pairs={{0,15},{1,0},{2,1},{3,2},{4,3},{5,4},{6,5},{7,6},{8,7},{9,8},{10,9... | collective-permute-start | bytes 3145736 | tf_op jit(solution)/shard_map/ppermute | solution.py:31
  23.9 58.1 %collective-permute-start.8 = (bf16[4,128,1024]{2,1,0:T(8,128)(2,1)}, bf16[4,128,1024]{2,1,0:T(8,128)(2,1)}, u32[]{:S(2)}, u32[]{:S(2)}) collective-permute-start(bf16[4,128,1024]{2,1,0:T(8,128)(2,1)} %get-tuple-element.19.after_ref), channel_id=1, source_target_pairs={{0,1},{1,2},{2,3},{3,4},{4,5},{5,6},{6,7},{7,8},{8,9},{9,10},{10,1... | collective-permute-start | bytes 3145736 | tf_op jit(solution)/shard_map/ppermute | solution.py:31
  36.4 7.9 %copy-start.16 = (s32[1,1,4]{2,1,0:T(1,128)S(1)}, s32[1,1,4]{2,1,0:T(1,128)}, u32[]{:S(2)}) copy-start(s32[1,1,4]{2,1,0:T(1,128)} %param.29) | copy-start | bytes 52
  36.5 7.9 %copy-start.17 = (s32[4]{0:T(128)S(1)}, s32[4]{0:T(128)}, u32[]{:S(2)}) copy-start(s32[4]{0:T(128)} %constant.28.clone) | copy-start | bytes 52
  36.5 12.2 %copy-start.12 = (s32[1,1,512]{2,1,0:T(1,128)S(1)}, s32[1,1,512]{2,1,0:T(1,128)}, u32[]{:S(2)}) copy-start(s32[1,1,512]{2,1,0:T(1,128)} %param.25) | copy-start | bytes 6148
  39.9 34.4 %all-to-all-start = ((bf16[8,192,768]{2,1,0:T(8,128)(2,1)}), bf16[8,192,768]{2,1,0:T(8,128)(2,1)}, u32[]{:S(2)}, u32[]{:S(2)}) async-start(bf16[8,192,768]{2,1,0:T(8,128)(2,1)} %shard_map.169), calls=%async_computation | async-start | bytes 4718592 | tf_op jit(solution)/shard_map/all_to_all | solution.py:370
  44.4 37.7 %collective-permute-start.10 = (bf16[4,128,1024]{2,1,0:T(8,128)(2,1)}, bf16[4,128,1024]{2,1,0:T(8,128)(2,1)}, u32[]{:S(2)}, u32[]{:S(2)}) collective-permute-start(bf16[4,128,1024]{2,1,0:T(8,128)(2,1)} %collective-permute-done.2.after_down_ref), channel_id=1, source_target_pairs={{0,15},{1,0},{2,1},{3,2},{4,3},{5,4},{6,5},{7,6},{8,7},{9,8},{10,9... | collective-permute-start | bytes 3145736 | tf_op jit(solution)/shard_map/ppermute | solution.py:31
  44.5 37.6 %collective-permute-start.7 = (bf16[4,128,1024]{2,1,0:T(8,128)(2,1)}, bf16[4,128,1024]{2,1,0:T(8,128)(2,1)}, u32[]{:S(2)}, u32[]{:S(2)}) collective-permute-start(bf16[4,128,1024]{2,1,0:T(8,128)(2,1)} %collective-permute-done.1.after_up_ref), channel_id=1, source_target_pairs={{0,1},{1,2},{2,3},{3,4},{4,5},{5,6},{6,7},{7,8},{8,9},{9,10},{10,1... | collective-permute-start | bytes 3145736 | tf_op jit(solution)/shard_map/ppermute | solution.py:31
  48.6 25.7 %collective-permute-start = (bf16[768,1024]{1,0:T(8,128)(2,1)}, bf16[768,1024]{1,0:T(8,128)(2,1)}, u32[]{:S(2)}, u32[]{:S(2)}) collective-permute-start(bf16[768,1024]{1,0:T(8,128)(2,1)} %bitcast.4.mine_ref), channel_id=1, source_target_pairs={{0,16},{16,0},{32,48},{48,32},{64,80},{80,64},{96,112},{112,96},{1... | collective-permute-start | bytes 4718600 | tf_op jit(solution)/shard_map/ppermute | solution.py:371
  48.6 1.2 copy-start.2
  49.8 1.6 %copy-start.7 = (bf16[1024,1024]{1,0:T(8,128)(2,1)S(1)}, bf16[1024,1024]{1,0:T(8,128)(2,1)}, u32[]{:S(2)}) copy-start(bf16[1024,1024]{1,0:T(8,128)(2,1)} %w_ref.6) | copy-start | bytes 6291460
  51.4 1.2 copy-start.10
  52.7 1.5 %copy-start.14 = (bf16[512,1792]{1,0:T(8,128)(2,1)S(1)}, bf16[512,1792]{1,0:T(8,128)(2,1)}, u32[]{:S(2)}) copy-start(bf16[512,1792]{1,0:T(8,128)(2,1)} %copy-done.13) | copy-start | bytes 5505028
  54.2 20.2 %copy-start.4 = (s32[1,1,4,4]{3,2,1,0:T(4,128)S(1)}, s32[1,1,4,4]{3,2,1,0:T(4,128)}, u32[]{:S(2)}) copy-start(s32[1,1,4,4]{3,2,1,0:T(4,128)} %param.28) | copy-start | bytes 196
  54.2 20.2 %copy-start.5 = (f32[1024]{0:T(1024)S(1)}, f32[1024]{0:T(1024)}, u32[]{:S(2)}) copy-start(f32[1024]{0:T(1024)} %param.21) | copy-start | bytes 12292
  79.9 26.8 %collective-permute-start.3 = (bf16[528,1024]{1,0:T(8,128)(2,1)S(1)}, bf16[528,1024]{1,0:T(8,128)(2,1)S(1)}, u32[]{:S(2)}, u32[]{:S(2)}) collective-permute-start(bf16[528,1024]{1,0:T(8,128)(2,1)S(1)} %get-tuple-element.23), channel_id=1, source_target_pairs={{0,1},{1,2},{2,3},{3,4},{4,5},{5,6},{6,7},{7,8},{8,9},{9,10},{10,1... | collective-permute-start | bytes 3244040 | tf_op jit(solution)/shard_map/ppermute | solution.py:31
  80.0 30.7 %collective-permute-start.5 = (bf16[528,1024]{1,0:T(8,128)(2,1)S(1)}, bf16[528,1024]{1,0:T(8,128)(2,1)S(1)}, u32[]{:S(2)}, u32[]{:S(2)}) collective-permute-start(bf16[528,1024]{1,0:T(8,128)(2,1)S(1)} %get-tuple-element.24), channel_id=1, source_target_pairs={{0,15},{1,0},{2,1},{3,2},{4,3},{5,4},{6,5},{7,6},{8,7},{9,8},{10,9... | collective-permute-start | bytes 3244040 | tf_op jit(solution)/shard_map/ppermute | solution.py:31
  82.1 38.2 %copy-start.8 = (bf16[1024,1024]{1,0:T(8,128)(2,1)S(1)}, bf16[1024,1024]{1,0:T(8,128)(2,1)}, u32[]{:S(2)}) copy-start(bf16[1024,1024]{1,0:T(8,128)(2,1)} %w_ref.6) | copy-start | bytes 6291460
  82.1 38.2 %copy-start.11 = (f32[1024]{0:T(1024)S(1)}, f32[1024]{0:T(1024)}, u32[]{:S(2)}) copy-start(f32[1024]{0:T(1024)} %param.24) | copy-start | bytes 12292
  82.1 38.2 %copy-start.15 = (bf16[512,1792]{1,0:T(8,128)(2,1)S(1)}, bf16[512,1792]{1,0:T(8,128)(2,1)}, u32[]{:S(2)}) copy-start(bf16[512,1792]{1,0:T(8,128)(2,1)} %copy-done.13) | copy-start | bytes 5505028
  87.2 30.8 %collective-permute-start.11 = (bf16[2,128,1024]{2,1,0:T(8,128)(2,1)S(1)}, bf16[2,128,1024]{2,1,0:T(8,128)(2,1)S(1)}, u32[]{:S(2)}, u32[]{:S(2)}) collective-permute-start(bf16[2,128,1024]{2,1,0:T(8,128)(2,1)S(1)} %get-tuple-element.27), channel_id=1, source_target_pairs={{0,1},{1,2},{2,3},{3,4},{4,5},{5,6},{6,7},{7,8},{8,9},{9,10},{10,1... | collective-permute-start | bytes 1572872 | tf_op jit(solution)/shard_map/ppermute | solution.py:31
  89.4 30.9 %collective-permute-start.12 = (bf16[2,128,1024]{2,1,0:T(8,128)(2,1)S(1)}, bf16[2,128,1024]{2,1,0:T(8,128)(2,1)S(1)}, u32[]{:S(2)}, u32[]{:S(2)}) collective-permute-start(bf16[2,128,1024]{2,1,0:T(8,128)(2,1)S(1)} %get-tuple-element.28), channel_id=1, source_target_pairs={{0,15},{1,0},{2,1},{3,2},{4,3},{5,4},{6,5},{7,6},{8,7},{9,8},{10,9... | collective-permute-start | bytes 1572872 | tf_op jit(solution)/shard_map/ppermute | solution.py:31
  106.8 33.0 %collective-permute-start.4 = (bf16[528,1024]{1,0:T(8,128)(2,1)S(1)}, bf16[528,1024]{1,0:T(8,128)(2,1)S(1)}, u32[]{:S(2)}, u32[]{:S(2)}) collective-permute-start(bf16[528,1024]{1,0:T(8,128)(2,1)S(1)} %collective-permute-done.3.a_up_ref), channel_id=1, source_target_pairs={{0,1},{1,2},{2,3},{3,4},{4,5},{5,6},{6,7},{7,8},{8,9},{9,10},{10,1... | collective-permute-start | bytes 3244040 | tf_op jit(solution)/shard_map/ppermute | solution.py:26
  110.8 31.2 %collective-permute-start.6 = (bf16[528,1024]{1,0:T(8,128)(2,1)S(1)}, bf16[528,1024]{1,0:T(8,128)(2,1)S(1)}, u32[]{:S(2)}, u32[]{:S(2)}) collective-permute-start(bf16[528,1024]{1,0:T(8,128)(2,1)S(1)} %collective-permute-done.5.a_down_ref), channel_id=1, source_target_pairs={{1,0},{2,1},{3,2},{4,3},{5,4},{6,5},{7,6},{8,7},{9,8},{10,9},{11,1... | collective-permute-start | bytes 3244040 | tf_op jit(solution)/shard_map/ppermute | solution.py:26
  120.2 21.8 %copy-start = (bf16[1024,1024]{1,0:T(8,128)(2,1)S(1)}, bf16[1024,1024]{1,0:T(8,128)(2,1)}, u32[]{:S(2)}) copy-start(bf16[1024,1024]{1,0:T(8,128)(2,1)} %w_ref.7) | copy-start | bytes 6291460
  120.3 21.8 %copy-start.3 = (bf16[512,1024]{1,0:T(8,128)(2,1)S(1)}, bf16[512,1024]{1,0:T(8,128)(2,1)}, u32[]{:S(2)}) copy-start(bf16[512,1024]{1,0:T(8,128)(2,1)} %get-tuple-element.17.fold_ref) | copy-start | bytes 3145732

commit v5 on v4

--- a/solution.py
+++ b/solution.py
@@ -95,7 +95,7 @@
 
 def far_kernel(
     adj_ref, src_ref, cot_ref, w_ref,
-    back_ref, fold_ref, up_ref, down_ref, adj_buf, cot_buf, w_buf, acc_ref, sems,
+    back_ref, up_ref, down_ref, adj_buf, cot_buf, w_buf, acc_ref, fold_ref, sems,
 ):
     seeds = adj_ref.shape[0]
     loads = [pltpu.make_async_copy(adj_ref.at[s], adj_buf.at[s], sems.at[s]) for s in range(seeds)]
@@ -134,30 +134,26 @@
     down_ref[...] = tn_dot(fold_ref[:, half:], back).astype(jnp.bfloat16).reshape(down_ref.shape)
 
 
-def near_kernel(adj_ref, src_ref, back_ref, fold_ref, up_ref, down_ref, acc_ref):
+def near_kernel(adj_ref, src_ref, back_ref, fold_ref, far_ref, up_ref, down_ref, acc_ref):
     acc_ref[...] = jnp.zeros_like(acc_ref)
     for seed in range(adj_ref.shape[0]):
         rows = pl.ds(seed * TILE, TILE)
 
         def add(k, _):
-            slot = src_ref[seed, k]
-            local = slot < TILE_DEV
-            near = (slot >= TILE_DEV + SLOTS) & (slot < TILE_DEV + 3 * SLOTS)
-
-            @pl.when(local | near)
-            def _():
-                at = jnp.where(local, slot, slot - SLOTS)
-                cols = pl.ds(pl.multiple_of(at * TILE, TILE), TILE)
-                acc_ref[rows, cols] += adj_ref[seed, k].astype(jnp.float32)
-
+            cols = pl.ds(pl.multiple_of(src_ref[seed, k] * TILE, TILE), TILE)
+            acc_ref[rows, cols] += adj_ref[seed, k].astype(jnp.float32)
             return 0
 
         lax.fori_loop(0, adj_ref.shape[1], add, 0, unroll=4)
-    fold_ref[...] = acc_ref[...].astype(jnp.bfloat16)
+    first, half = TILE_DEV * TILE, SLOTS * TILE
+    start = first + half
+    fold_ref[:, :first] = acc_ref[:, :first].astype(jnp.bfloat16)
+    fold_ref[:, first:] = acc_ref[:, start : start + 2 * half].astype(jnp.bfloat16)
+    far_ref[:, :half] = acc_ref[:, first:start].astype(jnp.bfloat16)
+    far_ref[:, half:] = acc_ref[:, start + 2 * half :].astype(jnp.bfloat16)
     back = back_ref[...]
-    start, half = TILE_DEV * TILE, SLOTS * TILE
-    up_ref[...] = tn_dot(fold_ref[:, start : start + half], back).astype(jnp.bfloat16).reshape(up_ref.shape)
-    down_ref[...] = tn_dot(fold_ref[:, start + half :], back).astype(jnp.bfloat16).reshape(down_ref.shape)
+    up_ref[...] = tn_dot(fold_ref[:, first:start], back).astype(jnp.bfloat16).reshape(up_ref.shape)
+    down_ref[...] = tn_dot(fold_ref[:, start:], back).astype(jnp.bfloat16).reshape(down_ref.shape)
 
 
 def local_kernel(fold_ref, back_ref, cot_ref, w_ref, seeds_ref, after_up_ref, after_down_ref, out_ref):
@@ -273,13 +269,21 @@
     self_ref[...] = nn_dot(chosen, w_ref[...]) + bias_ref[...]
 
 
-def last_kernel(fold_ref, f_up_ref, f_down_ref, part_ref, self_ref, w_ref, out_ref, placed_ref):
+def last_kernel(fold_ref, f_up_ref, f_down_ref, part_ref, self_ref, w_ref, out_ref, placed_ref, buf, sems):
     quad = NEAR * TILE
     placed(fold_ref, 0, f_down_ref, SLOTS, NEAR, placed_ref, 0)
     placed(fold_ref, SLOTS, f_up_ref, SLOTS, NEAR, placed_ref, NEAR)
-    gathered = part_ref[...] + nn_dot(placed_ref[:, :quad], f_down_ref[:quad])
-    gathered = (gathered + nn_dot(placed_ref[:, quad:], f_up_ref[:quad])).astype(jnp.bfloat16)
-    out_ref[...] = (self_ref[...] + nn_dot(gathered, w_ref[...])).astype(jnp.bfloat16)
+    half = buf.shape[0] // 2
+    stores = []
+    for part in range(2):
+        rows = slice(part * half, (part + 1) * half)
+        gathered = part_ref[rows] + nn_dot(placed_ref[rows, :quad], f_down_ref[:quad])
+        gathered = (gathered + nn_dot(placed_ref[rows, quad:], f_up_ref[:quad])).astype(jnp.bfloat16)
+        buf[rows] = (self_ref[rows] + nn_dot(gathered, w_ref[...])).astype(jnp.bfloat16)
+        stores.append(pltpu.make_async_copy(buf.at[rows], out_ref.at[rows], sems.at[part]))
+        stores[-1].start()
+    for store in stores:
+        store.wait()
 
 
 def shards(
@@ -319,15 +323,16 @@
     quad_marked = shape((NEAR * TILE + 2 * ROWS, hid), bf16)
     far_cols, near_cols = 2 * SLOTS * TILE, (TILE_DEV + 2 * SLOTS) * TILE
 
-    back, fold_far, far_up, far_down = call(
+    back, far_up, far_down = call(
         far_kernel,
-        (shape((seeds, hid), bf16), shape((seeds, far_cols), bf16), quad, quad),
+        (shape((seeds, hid), bf16), quad, quad),
         [ANY, SMEM, ANY, ANY],
         [
             pltpu.VMEM(blocks.shape, bf16),
             pltpu.VMEM((seeds, hid), bf16),
             pltpu.VMEM((hid, hid), bf16),
             pltpu.VMEM((seeds, far_cols), f32),
+            pltpu.VMEM((seeds, far_cols), bf16),
             pltpu.SemaphoreType.DMA((blocks.shape[0] + 2,)),
         ],
         vmem=56,
@@ -345,12 +350,12 @@
     got_far_up = shifted(far_up, 1)
     got_far_down = shifted(far_down, -1)
 
-    fold_near, near_up, near_down = call(
+    fold_near, fold_far, near_up, near_down = call(
         near_kernel,
-        (shape((seeds, near_cols), bf16), quad, quad),
+        (shape((seeds, near_cols), bf16), shape((seeds, far_cols), bf16), quad, quad),
         [VMEM, SMEM, VMEM],
-        [pltpu.VMEM((seeds, near_cols), f32)],
-        vmem=24,
+        [pltpu.VMEM((seeds, near_cols + far_cols), f32)],
+        vmem=28,
     )(blocks, sources, back)
 
     sent = pl.pallas_call(
@@ -435,7 +440,8 @@
         last_kernel,
         shape((seeds, hid), bf16),
         [VMEM] * 6,
-        [pltpu.VMEM((seeds, far_cols), bf16)],
+        [pltpu.VMEM((seeds, far_cols), bf16), pltpu.VMEM((seeds, hid), bf16), pltpu.SemaphoreType.DMA((2,))],
+        out_specs=ANY,
         vmem=20,
     )(fold_far, next_up, next_down, part, self_term, w_neigh_two)
     return (layer_out[None], grads[None])

time: 147 us -> 147 us (level)
    unnamed x36 -> x38, local copies, waits for them, and re-layouts: 6.85 us -> 7.94 us
where the time goes in v5:
time: 147 us; the launch traced here: 146 us
  waiting for transfers between devices  61.6 us (42%)
  Pallas kernels  43.3 us (29%)
  starting transfers between devices  31.9 us (22%)
  local copies, waits for them, and re-layouts  7.94 us (5%)
    ppermute x10, waiting for transfers between devices, shifted(): lax.ppermute(shard, 'dom', [(i, (i + by) % count) for i in range(count)])  24.9 us
    all_to_all x1, waiting for transfers between devices, shards(): taken = lax.all_to_all(sent, 'feat', 0, 0)  17.3 us
    ppermute x10, starting transfers between devices, shifted(): lax.ppermute(shard, 'dom', [(i, (i + by) % count) for i in range(count)])  16.9 us
    ppermute x2, waiting for transfers between devices, open_shift(): lax.ppermute(shard, 'dom', [(i, i + by) for i in range(count) if 0 <= i +...  16.7 us
    pallas_call x1, Pallas kernels, shards(): pl.pallas_call(gather_kernel, grid=(feat_count,), in_specs=[SMEM, pl.Bloc...  8.38 us
    unnamed x38, local copies, waits for them, and re-layouts  7.94 us
    pallas_call x1, Pallas kernels, shards(): call(far_kernel, (shape((seeds, hid), bf16), quad, quad), [ANY, SMEM, ANY...  6.66 us
    ppermute x2, starting transfers between devices, open_shift(): lax.ppermute(shard, 'dom', [(i, i + by) for i in range(count) if 0 <= i +...  6.12 us
  transfers between devices with their start and end apart: 15, of which 7 were waited for; matrix products, arithmetic and copies ran while one was open for 0% of the time, Pallas kernels for 23%

profile of v5, /device:TPU:104, one launch (start us, length us, event | category | flops | bytes accessed | tf_op | source)
XLA Modules:
  0.0 145.8 jit_solution(348548223777430172)
XLA Ops:
  0.6 6.7 %shard_map.167 = (bf16[512,1024]{1,0:T(8,128)(2,1)}, bf16[4,128,1024]{2,1,0:T(8,128)(2,1)}, bf16[4,128,1024]{2,1,0:T(8,128)(2,1)}) custom-call(bf16[4,16,128,128]{3,2,1,0:T(8,128)(2,1)} %bitcast.14, s32[4,16]{1,0:T(4,128)} %bitcast.21, bf16[512,1024]{1,0:T(8,128)(2,1)} %bitcast.16, bf16[1024,1024]{1,0:T(8,128)(2,1)} %w_ref.7), custom_call_target="tpu_custom_call" | custom-call | flops 1073741824 | bytes 1 | tf_op jit(solution)/shard_map/pallas_call | solution.py:326
  7.3 0.5 collective-permute-start.2
  7.8 3.7 %collective-permute-start.1 = (bf16[4,128,1024]{2,1,0:T(8,128)(2,1)}, bf16[4,128,1024]{2,1,0:T(8,128)(2,1)}, u32[]{:S(2)}, u32[]{:S(2)}) collective-permute-start(bf16[4,128,1024]{2,1,0:T(8,128)(2,1)} %get-tuple-element.20.after_ref), channel_id=1, source_target_pairs={{0,1},{1,2},{2,3},{3,4},{4,5},{5,6},{6,7},{7,8},{8,9},{9,10},{10,1... | collective-permute-start | bytes 3145736 | tf_op jit(solution)/shard_map/ppermute | solution.py:31
  11.5 2.3 %shard_map.170 = bf16[8,96,1024]{2,1,0:T(8,128)(2,1)} custom-call(bf16[96,1024]{1,0:T(8,128)(2,1)} %self_ref.1, bf16[96,1024]{1,0:T(8,128)(2,1)} %neigh_ref.1, bf16[4,128,1024]{2,1,0:T(8,128)(2,1)} %get-tuple-element.20.after_ref), custom_call_target="tpu_custom_call" | custom-call | flops 1073741824 | bytes 1 | tf_op jit(solution)/shard_map/pallas_call | solution.py:340
  13.8 0.0 copy-start.1
  13.8 0.0 copy-start.7
  13.8 4.5 %all-to-all-start.1 = ((bf16[8,96,1024]{2,1,0:T(8,128)(2,1)}), bf16[8,96,1024]{2,1,0:T(8,128)(2,1)}, u32[]{:S(2)}, u32[]{:S(2)}) async-start(bf16[8,96,1024]{2,1,0:T(8,128)(2,1)} %shard_map.170), calls=%async_computation.1 | async-start | bytes 3145728 | tf_op jit(solution)/shard_map/all_to_all | solution.py:348
  18.3 0.0 copy-done.10
  18.3 0.0 copy-done.1
  18.3 0.0 copy-done.7
  18.3 3.9 %shard_map.168 = (bf16[512,1792]{1,0:T(8,128)(2,1)S(1)}, bf16[512,1024]{1,0:T(8,128)(2,1)S(1)}, bf16[4,128,1024]{2,1,0:T(8,128)(2,1)}, bf16[4,128,1024]{2,1,0:T(8,128)(2,1)}) custom-call(bf16[4,16,128,128]{3,2,1,0:T(8,128)(2,1)S(1)} %bitcast.15, s32[4,16]{1,0:T(4,128)S(1)} %bitcast.22, bf16[512,1024]{1,0:T(8,128)(2,1)S(1)} %copy-done.10), custom_call_target="tpu_custom_call" | custom-call | flops 1073741824 | bytes 1 | tf_op jit(solution)/shard_map/pallas_call | solution.py:353
  22.3 1.1 copy-done.3
  23.4 1.3 copy-done.14
  24.6 0.0 collective-permute-start.9
  24.6 4.1 %collective-permute-start.8 = (bf16[4,128,1024]{2,1,0:T(8,128)(2,1)}, bf16[4,128,1024]{2,1,0:T(8,128)(2,1)}, u32[]{:S(2)}, u32[]{:S(2)}) collective-permute-start(bf16[4,128,1024]{2,1,0:T(8,128)(2,1)} %get-tuple-element.19.after_ref), channel_id=1, source_target_pairs={{0,1},{1,2},{2,3},{3,4},{4,5},{5,6},{6,7},{7,8},{8,9},{9,10},{10,1... | collective-permute-start | bytes 3145736 | tf_op jit(solution)/shard_map/ppermute | solution.py:31
  28.7 8.4 %shard_map.169 = bf16[8,192,768]{2,1,0:T(8,128)(2,1)} custom-call(s32[4,48]{1,0:T(4,128)} %bitcast.28, bf16[96,6144]{1,0:T(8,128)(2,1)} %feat_ref.1, bf16[48,4,128,128]{3,2,1,0:T(8,128)(2,1)} %adj_ref.1, bf16[4,128,1024]{2,1,0:T(8,128)(2,1)} %get-tuple-element.19.after_ref), custom_call_target="tpu_custom_call" | custom-call | flops 107374182400 | bytes 1 | tf_op jit(solution)/shard_map/pallas_call | solution.py:361
  37.1 2.8 %all-to-all-done.1 = bf16[8,96,1024]{2,1,0:T(8,128)(2,1)} async-done(((bf16[8,96,1024]{2,1,0:T(8,128)(2,1)}), bf16[8,96,1024]{2,1,0:T(8,128)(2,1)}, u32[]{:S(2)}, u32[]{:S(2)}) %all-to-all-start.1) | async-done | bytes 1572896 | tf_op jit(solution)/shard_map/all_to_all | solution.py:348
  40.0 4.4 %all-to-all-start = ((bf16[8,192,768]{2,1,0:T(8,128)(2,1)}), bf16[8,192,768]{2,1,0:T(8,128)(2,1)}, u32[]{:S(2)}, u32[]{:S(2)}) async-start(bf16[8,192,768]{2,1,0:T(8,128)(2,1)} %shard_map.169), calls=%async_computation | async-start | bytes 4718592 | tf_op jit(solution)/shard_map/all_to_all | solution.py:375
  44.3 0.0 copy-done.17
  44.3 0.0 copy-done.18
  44.4 0.0 collective-permute-done.2.after_down_ref
  44.4 0.1 collective-permute-start.10
  44.5 0.0 collective-permute-done.1.after_up_ref
  44.5 4.1 %collective-permute-start.7 = (bf16[4,128,1024]{2,1,0:T(8,128)(2,1)}, bf16[4,128,1024]{2,1,0:T(8,128)(2,1)}, u32[]{:S(2)}, u32[]{:S(2)}) collective-permute-start(bf16[4,128,1024]{2,1,0:T(8,128)(2,1)} %collective-permute-done.1.after_up_ref), channel_id=1, source_target_pairs={{0,1},{1,2},{2,3},{3,4},{4,5},{5,6},{6,7},{7,8},{8,9},{9,10},{10,1... | collective-permute-start | bytes 3145736 | tf_op jit(solution)/shard_map/ppermute | solution.py:31
  48.6 0.0 collective-permute-start
  48.6 0.0 copy-done.13
  48.6 1.2 copy-done.2
  49.8 1.6 %copy-done.8 = bf16[1024,1024]{1,0:T(8,128)(2,1)S(1)} copy-done((bf16[1024,1024]{1,0:T(8,128)(2,1)S(1)}, bf16[1024,1024]{1,0:T(8,128)(2,1)}, u32[]{:S(2)}) %copy-start.8) | copy-done | bytes 2097176
  51.4 1.2 copy-done.11
  52.7 1.5 %copy-done.15 = bf16[512,1792]{1,0:T(8,128)(2,1)S(1)} copy-done((bf16[512,1792]{1,0:T(8,128)(2,1)S(1)}, bf16[512,1792]{1,0:T(8,128)(2,1)}, u32[]{:S(2)}) %copy-start.15) | copy-done | bytes 1835032
  54.2 2.9 %shard_map.171.after_ref.local_ref = f32[768,1024]{1,0:T(8,128)S(1)} custom-call(bf16[512,1792]{1,0:T(8,128)(2,1)S(1)} %copy-done.15, bf16[512,1024]{1,0:T(8,128)(2,1)S(1)} %copy-done.11, bf16[512,1024]{1,0:T(8,128)(2,1)S(1)} %bitcast.17, bf16[1024,1024]{1,0:T(8,128)(2,1)S(1)} %copy-done.8, s32[1,512]{1,0:T(1,128)S(1)} %bitcast.24, ...), custom_call_target="tpu_custom_call" | custom-call | flops 21474836480 | bytes 1 | tf_op jit(solution)/shard_map/pallas_call | solution.py:384
  57.1 17.3 %all-to-all-done.in_ref = bf16[8,192,768]{2,1,0:T(8,128)(2,1)} async-done(((bf16[8,192,768]{2,1,0:T(8,128)(2,1)}), bf16[8,192,768]{2,1,0:T(8,128)(2,1)}, u32[]{:S(2)}, u32[]{:S(2)}) %all-to-all-start) | async-done | bytes 2359328 | tf_op jit(solution)/shard_map/all_to_all | solution.py:375
  74.3 0.0 collective-permute-done.other_ref
  74.3 0.0 copy-done.5
  74.3 0.0 copy-done.6
  74.3 5.6 %shard_map.172 = (bf16[6,128,1024]{2,1,0:T(8,128)(2,1)S(1)}, bf16[528,1024]{1,0:T(8,128)(2,1)S(1)}, bf16[528,1024]{1,0:T(8,128)(2,1)S(1)}) custom-call(bf16[8,192,768]{2,1,0:T(8,128)(2,1)} %all-to-all-done.in_ref, bf16[768,1024]{1,0:T(8,128)(2,1)} %bitcast.4.mine_ref, bf16[768,1024]{1,0:T(8,128)(2,1)} %collective-permute-done.other_ref, ...), custom_call_target="tpu_custom_call" | custom-call | flops 1073741824 | bytes 1 | tf_op jit(solution)/shard_map/pallas_call | solution.py:393
  80.0 0.1 collective-permute-start.3
  80.0 0.0 collective-permute-done.9.from_2_ref
  80.0 2.0 %collective-permute-start.5 = (bf16[528,1024]{1,0:T(8,128)(2,1)S(1)}, bf16[528,1024]{1,0:T(8,128)(2,1)S(1)}, u32[]{:S(2)}, u32[]{:S(2)}) collective-permute-start(bf16[528,1024]{1,0:T(8,128)(2,1)S(1)} %get-tuple-element.24), channel_id=1, source_target_pairs={{0,15},{1,0},{2,1},{3,2},{4,3},{5,4},{6,5},{7,6},{8,7},{9,8},{10,9... | collective-permute-start | bytes 3244040 | tf_op jit(solution)/shard_map/ppermute | solution.py:31
  82.1 0.0 collective-permute-done.8.from_1_ref
  82.1 0.0 collective-permute-done.10.from_3_ref
  82.1 0.0 collective-permute-done.7.from_0_ref
  82.1 0.0 copy-start.9
  82.1 0.0 copy-start.12
  82.1 0.0 copy-start.16
  82.1 4.9 %shard_map.173 = (f32[768,1024]{1,0:T(8,128)}, bf16[2,128,1024]{2,1,0:T(8,128)(2,1)S(1)}, bf16[2,128,1024]{2,1,0:T(8,128)(2,1)S(1)}) custom-call(f32[768,1024]{1,0:T(8,128)S(1)} %shard_map.171.after_ref.local_ref, bf16[4,128,1024]{2,1,0:T(8,128)(2,1)} %collective-permute-done.7.from_0_ref, bf16[4,128,1024]{2,1,0:T(8,128)(2,1)} %collective-permute-done.8.from_1_ref, ...), custom_call_target="tpu_custom_call" | custom-call | flops 1073741824 | bytes 1 | tf_op jit(solution)/shard_map/pallas_call | solution.py:422
  87.0 2.3 %collective-permute-start.11 = (bf16[2,128,1024]{2,1,0:T(8,128)(2,1)S(1)}, bf16[2,128,1024]{2,1,0:T(8,128)(2,1)S(1)}, u32[]{:S(2)}, u32[]{:S(2)}) collective-permute-start(bf16[2,128,1024]{2,1,0:T(8,128)(2,1)S(1)} %get-tuple-element.27), channel_id=1, source_target_pairs={{0,1},{1,2},{2,3},{3,4},{4,5},{5,6},{6,7},{7,8},{8,9},{9,10},{10,1... | collective-permute-start | bytes 1572872 | tf_op jit(solution)/shard_map/ppermute | solution.py:31
  89.2 0.0 collective-permute-start.12
  89.2 17.5 %collective-permute-done.3.a_up_ref = bf16[528,1024]{1,0:T(8,128)(2,1)S(1)} collective-permute-done((bf16[528,1024]{1,0:T(8,128)(2,1)S(1)}, bf16[528,1024]{1,0:T(8,128)(2,1)S(1)}, u32[]{:S(2)}, u32[]{:S(2)}) %collective-permute-start.3) | collective-permute-done | bytes 1081376 | tf_op jit(solution)/shard_map/ppermute | solution.py:31
  106.8 4.0 %collective-permute-start.4 = (bf16[528,1024]{1,0:T(8,128)(2,1)S(1)}, bf16[528,1024]{1,0:T(8,128)(2,1)S(1)}, u32[]{:S(2)}, u32[]{:S(2)}) collective-permute-start(bf16[528,1024]{1,0:T(8,128)(2,1)S(1)} %collective-permute-done.3.a_up_ref), channel_id=1, source_target_pairs={{0,1},{1,2},{2,3},{3,4},{4,5},{5,6},{6,7},{7,8},{8,9},{9,10},{10,1... | collective-permute-start | bytes 3244040 | tf_op jit(solution)/shard_map/ppermute | solution.py:26
  110.8 0.0 collective-permute-done.5.a_down_ref
  110.8 2.1 %collective-permute-start.6 = (bf16[528,1024]{1,0:T(8,128)(2,1)S(1)}, bf16[528,1024]{1,0:T(8,128)(2,1)S(1)}, u32[]{:S(2)}, u32[]{:S(2)}) collective-permute-start(bf16[528,1024]{1,0:T(8,128)(2,1)S(1)} %collective-permute-done.5.a_down_ref), channel_id=1, source_target_pairs={{1,0},{2,1},{3,2},{4,3},{5,4},{6,5},{7,6},{8,7},{9,8},{10,9},{11,1... | collective-permute-start | bytes 3244040 | tf_op jit(solution)/shard_map/ppermute | solution.py:26
  112.9 5.1 %collective-permute-done.11.rest_up_ref = bf16[2,128,1024]{2,1,0:T(8,128)(2,1)S(1)} collective-permute-done((bf16[2,128,1024]{2,1,0:T(8,128)(2,1)S(1)}, bf16[2,128,1024]{2,1,0:T(8,128)(2,1)S(1)}, u32[]{:S(2)}, u32[]{:S(2)}) %collective-permute-start.11) | collective-permute-done | bytes 524320 | tf_op jit(solution)/shard_map/ppermute | solution.py:31
  118.0 2.2 %collective-permute-done.12.rest_down_ref = bf16[2,128,1024]{2,1,0:T(8,128)(2,1)S(1)} collective-permute-done((bf16[2,128,1024]{2,1,0:T(8,128)(2,1)S(1)}, bf16[2,128,1024]{2,1,0:T(8,128)(2,1)S(1)}, u32[]{:S(2)}, u32[]{:S(2)}) %collective-permute-start.12) | collective-permute-done | bytes 524320 | tf_op jit(solution)/shard_map/ppermute | solution.py:31
  120.2 0.0 copy-done.9
  120.2 0.0 copy-done.12
  120.2 0.0 copy-done.16
  120.2 0.0 copy-start
  120.3 0.0 copy-start.4
  120.3 5.1 %shard_map.174 = (f32[512,1024]{1,0:T(8,128)S(1)}, f32[512,1024]{1,0:T(8,128)S(1)}) custom-call(bf16[512,1792]{1,0:T(8,128)(2,1)S(1)} %copy-done.16, bf16[6,128,1024]{2,1,0:T(8,128)(2,1)S(1)} %get-tuple-element.25.hid_ref, bf16[528,1024]{1,0:T(8,128)(2,1)S(1)} %collective-permute-done.3.a_up_ref, ...), custom_call_target="tpu_custom_call" | custom-call | flops 107374182400 | bytes 1 | tf_op jit(solution)/shard_map/pallas_call | solution.py:428
  125.3 14.5 %collective-permute-done.4.f_up_ref = bf16[528,1024]{1,0:T(8,128)(2,1)S(1)} collective-permute-done((bf16[528,1024]{1,0:T(8,128)(2,1)S(1)}, bf16[528,1024]{1,0:T(8,128)(2,1)S(1)}, u32[]{:S(2)}, u32[]{:S(2)}) %collective-permute-start.4) | collective-permute-done | bytes 1081376 | tf_op jit(solution)/shard_map/ppermute | solution.py:26
  139.8 2.2 %collective-permute-done.6.f_down_ref = bf16[528,1024]{1,0:T(8,128)(2,1)S(1)} collective-permute-done((bf16[528,1024]{1,0:T(8,128)(2,1)S(1)}, bf16[528,1024]{1,0:T(8,128)(2,1)S(1)}, u32[]{:S(2)}, u32[]{:S(2)}) %collective-permute-start.6) | collective-permute-done | bytes 1081376 | tf_op jit(solution)/shard_map/ppermute | solution.py:26
  142.0 0.0 copy-done
  142.0 3.6 %shard_map.175 = bf16[512,1024]{1,0:T(8,128)(2,1)} custom-call(bf16[512,1024]{1,0:T(8,128)(2,1)S(1)} %copy-done.4, bf16[528,1024]{1,0:T(8,128)(2,1)S(1)} %collective-permute-done.4.f_up_ref, bf16[528,1024]{1,0:T(8,128)(2,1)S(1)} %collective-permute-done.6.f_down_ref, f32[512,1024]{1,0:T(8,128)S(1)} %get-tuple-element.29.part_ref, ...), custom_call_target="tpu_custom_call" | custom-call | flops 1073741824 | bytes 1 | tf_op jit(solution)/shard_map/pallas_call | solution.py:439
  (14 shorter events, 0.0 us)
Async XLA Ops:
  7.3 37.1 %collective-permute-start.2 = (bf16[4,128,1024]{2,1,0:T(8,128)(2,1)}, bf16[4,128,1024]{2,1,0:T(8,128)(2,1)}, u32[]{:S(2)}, u32[]{:S(2)}) collective-permute-start(bf16[4,128,1024]{2,1,0:T(8,128)(2,1)} %get-tuple-element.22), channel_id=1, source_target_pairs={{0,15},{1,0},{2,1},{3,2},{4,3},{5,4},{6,5},{7,6},{8,7},{9,8},{10,9... | collective-permute-start | bytes 3145736 | tf_op jit(solution)/shard_map/ppermute | solution.py:31
  7.8 36.7 %collective-permute-start.1 = (bf16[4,128,1024]{2,1,0:T(8,128)(2,1)}, bf16[4,128,1024]{2,1,0:T(8,128)(2,1)}, u32[]{:S(2)}, u32[]{:S(2)}) collective-permute-start(bf16[4,128,1024]{2,1,0:T(8,128)(2,1)} %get-tuple-element.20.after_ref), channel_id=1, source_target_pairs={{0,1},{1,2},{2,3},{3,4},{4,5},{5,6},{6,7},{7,8},{8,9},{9,10},{10,1... | collective-permute-start | bytes 3145736 | tf_op jit(solution)/shard_map/ppermute | solution.py:31
  11.5 6.8 %copy-start.10 = (bf16[512,1024]{1,0:T(8,128)(2,1)S(1)}, bf16[512,1024]{1,0:T(8,128)(2,1)}, u32[]{:S(2)}) copy-start(bf16[512,1024]{1,0:T(8,128)(2,1)} %get-tuple-element.17.back_ref) | copy-start | bytes 3145732
  13.8 4.5 %copy-start.1 = (bf16[1,1,4,16,128,128]{5,4,3,2,1,0:T(8,128)(2,1)S(1)}, bf16[1,1,4,16,128,128]{5,4,3,2,1,0:T(8,128)(2,1)}, u32[]{:S(2)}) copy-start(bf16[1,1,4,16,128,128]{5,4,3,2,1,0:T(8,128)(2,1)} %param.26) | copy-start | bytes 6291460
  13.8 4.5 %copy-start.7 = (s32[1,1,4,16]{3,2,1,0:T(4,128)S(1)}, s32[1,1,4,16]{3,2,1,0:T(4,128)}, u32[]{:S(2)}) copy-start(s32[1,1,4,16]{3,2,1,0:T(4,128)} %param.27) | copy-start | bytes 772
  13.8 26.1 %all-to-all-start.1 = ((bf16[8,96,1024]{2,1,0:T(8,128)(2,1)}), bf16[8,96,1024]{2,1,0:T(8,128)(2,1)}, u32[]{:S(2)}, u32[]{:S(2)}) async-start(bf16[8,96,1024]{2,1,0:T(8,128)(2,1)} %shard_map.170), calls=%async_computation.1 | async-start | bytes 3145728 | tf_op jit(solution)/shard_map/all_to_all | solution.py:348
  22.3 1.1 copy-start.3
  23.3 1.3 copy-start.14
  24.6 55.4 %collective-permute-start.9 = (bf16[4,128,1024]{2,1,0:T(8,128)(2,1)}, bf16[4,128,1024]{2,1,0:T(8,128)(2,1)}, u32[]{:S(2)}, u32[]{:S(2)}) collective-permute-start(bf16[4,128,1024]{2,1,0:T(8,128)(2,1)} %get-tuple-element.26), channel_id=1, source_target_pairs={{0,15},{1,0},{2,1},{3,2},{4,3},{5,4},{6,5},{7,6},{8,7},{9,8},{10,9... | collective-permute-start | bytes 3145736 | tf_op jit(solution)/shard_map/ppermute | solution.py:31
  24.6 57.4 %collective-permute-start.8 = (bf16[4,128,1024]{2,1,0:T(8,128)(2,1)}, bf16[4,128,1024]{2,1,0:T(8,128)(2,1)}, u32[]{:S(2)}, u32[]{:S(2)}) collective-permute-start(bf16[4,128,1024]{2,1,0:T(8,128)(2,1)} %get-tuple-element.19.after_ref), channel_id=1, source_target_pairs={{0,1},{1,2},{2,3},{3,4},{4,5},{5,6},{6,7},{7,8},{8,9},{9,10},{10,1... | collective-permute-start | bytes 3145736 | tf_op jit(solution)/shard_map/ppermute | solution.py:31
  37.1 7.2 %copy-start.17 = (s32[1,1,4]{2,1,0:T(1,128)S(1)}, s32[1,1,4]{2,1,0:T(1,128)}, u32[]{:S(2)}) copy-start(s32[1,1,4]{2,1,0:T(1,128)} %param.29) | copy-start | bytes 52
  37.1 7.2 %copy-start.18 = (s32[4]{0:T(128)S(1)}, s32[4]{0:T(128)}, u32[]{:S(2)}) copy-start(s32[4]{0:T(128)} %constant.28.clone) | copy-start | bytes 52
  37.1 11.5 %copy-start.13 = (s32[1,1,512]{2,1,0:T(1,128)S(1)}, s32[1,1,512]{2,1,0:T(1,128)}, u32[]{:S(2)}) copy-start(s32[1,1,512]{2,1,0:T(1,128)} %param.25) | copy-start | bytes 6148
  40.0 34.4 %all-to-all-start = ((bf16[8,192,768]{2,1,0:T(8,128)(2,1)}), bf16[8,192,768]{2,1,0:T(8,128)(2,1)}, u32[]{:S(2)}, u32[]{:S(2)}) async-start(bf16[8,192,768]{2,1,0:T(8,128)(2,1)} %shard_map.169), calls=%async_computation | async-start | bytes 4718592 | tf_op jit(solution)/shard_map/all_to_all | solution.py:375
  44.4 37.7 %collective-permute-start.10 = (bf16[4,128,1024]{2,1,0:T(8,128)(2,1)}, bf16[4,128,1024]{2,1,0:T(8,128)(2,1)}, u32[]{:S(2)}, u32[]{:S(2)}) collective-permute-start(bf16[4,128,1024]{2,1,0:T(8,128)(2,1)} %collective-permute-done.2.after_down_ref), channel_id=1, source_target_pairs={{0,15},{1,0},{2,1},{3,2},{4,3},{5,4},{6,5},{7,6},{8,7},{9,8},{10,9... | collective-permute-start | bytes 3145736 | tf_op jit(solution)/shard_map/ppermute | solution.py:31
  44.5 37.6 %collective-permute-start.7 = (bf16[4,128,1024]{2,1,0:T(8,128)(2,1)}, bf16[4,128,1024]{2,1,0:T(8,128)(2,1)}, u32[]{:S(2)}, u32[]{:S(2)}) collective-permute-start(bf16[4,128,1024]{2,1,0:T(8,128)(2,1)} %collective-permute-done.1.after_up_ref), channel_id=1, source_target_pairs={{0,1},{1,2},{2,3},{3,4},{4,5},{5,6},{6,7},{7,8},{8,9},{9,10},{10,1... | collective-permute-start | bytes 3145736 | tf_op jit(solution)/shard_map/ppermute | solution.py:31
  48.6 25.7 %collective-permute-start = (bf16[768,1024]{1,0:T(8,128)(2,1)}, bf16[768,1024]{1,0:T(8,128)(2,1)}, u32[]{:S(2)}, u32[]{:S(2)}) collective-permute-start(bf16[768,1024]{1,0:T(8,128)(2,1)} %bitcast.4.mine_ref), channel_id=1, source_target_pairs={{0,16},{16,0},{32,48},{48,32},{64,80},{80,64},{96,112},{112,96},{1... | collective-permute-start | bytes 4718600 | tf_op jit(solution)/shard_map/ppermute | solution.py:376
  48.6 1.2 copy-start.2
  49.8 1.6 %copy-start.8 = (bf16[1024,1024]{1,0:T(8,128)(2,1)S(1)}, bf16[1024,1024]{1,0:T(8,128)(2,1)}, u32[]{:S(2)}) copy-start(bf16[1024,1024]{1,0:T(8,128)(2,1)} %w_ref.6) | copy-start | bytes 6291460
  51.4 1.2 copy-start.11
  52.7 1.5 %copy-start.15 = (bf16[512,1792]{1,0:T(8,128)(2,1)S(1)}, bf16[512,1792]{1,0:T(8,128)(2,1)}, u32[]{:S(2)}) copy-start(bf16[512,1792]{1,0:T(8,128)(2,1)} %copy-done.14) | copy-start | bytes 5505028
  54.2 20.2 %copy-start.5 = (s32[1,1,4,4]{3,2,1,0:T(4,128)S(1)}, s32[1,1,4,4]{3,2,1,0:T(4,128)}, u32[]{:S(2)}) copy-start(s32[1,1,4,4]{3,2,1,0:T(4,128)} %param.28) | copy-start | bytes 196
  54.2 20.2 %copy-start.6 = (f32[1024]{0:T(1024)S(1)}, f32[1024]{0:T(1024)}, u32[]{:S(2)}) copy-start(f32[1024]{0:T(1024)} %param.21) | copy-start | bytes 12292
  80.0 26.8 %collective-permute-start.3 = (bf16[528,1024]{1,0:T(8,128)(2,1)S(1)}, bf16[528,1024]{1,0:T(8,128)(2,1)S(1)}, u32[]{:S(2)}, u32[]{:S(2)}) collective-permute-start(bf16[528,1024]{1,0:T(8,128)(2,1)S(1)} %get-tuple-element.23), channel_id=1, source_target_pairs={{0,1},{1,2},{2,3},{3,4},{4,5},{5,6},{6,7},{7,8},{8,9},{9,10},{10,1... | collective-permute-start | bytes 3244040 | tf_op jit(solution)/shard_map/ppermute | solution.py:31
  80.0 30.7 %collective-permute-start.5 = (bf16[528,1024]{1,0:T(8,128)(2,1)S(1)}, bf16[528,1024]{1,0:T(8,128)(2,1)S(1)}, u32[]{:S(2)}, u32[]{:S(2)}) collective-permute-start(bf16[528,1024]{1,0:T(8,128)(2,1)S(1)} %get-tuple-element.24), channel_id=1, source_target_pairs={{0,15},{1,0},{2,1},{3,2},{4,3},{5,4},{6,5},{7,6},{8,7},{9,8},{10,9... | collective-permute-start | bytes 3244040 | tf_op jit(solution)/shard_map/ppermute | solution.py:31
  82.1 38.2 %copy-start.9 = (bf16[1024,1024]{1,0:T(8,128)(2,1)S(1)}, bf16[1024,1024]{1,0:T(8,128)(2,1)}, u32[]{:S(2)}) copy-start(bf16[1024,1024]{1,0:T(8,128)(2,1)} %w_ref.6) | copy-start | bytes 6291460
  82.1 38.2 %copy-start.12 = (f32[1024]{0:T(1024)S(1)}, f32[1024]{0:T(1024)}, u32[]{:S(2)}) copy-start(f32[1024]{0:T(1024)} %param.24) | copy-start | bytes 12292
  82.1 38.2 %copy-start.16 = (bf16[512,1792]{1,0:T(8,128)(2,1)S(1)}, bf16[512,1792]{1,0:T(8,128)(2,1)}, u32[]{:S(2)}) copy-start(bf16[512,1792]{1,0:T(8,128)(2,1)} %copy-done.14) | copy-start | bytes 5505028
  87.0 31.1 %collective-permute-start.11 = (bf16[2,128,1024]{2,1,0:T(8,128)(2,1)S(1)}, bf16[2,128,1024]{2,1,0:T(8,128)(2,1)S(1)}, u32[]{:S(2)}, u32[]{:S(2)}) collective-permute-start(bf16[2,128,1024]{2,1,0:T(8,128)(2,1)S(1)} %get-tuple-element.27), channel_id=1, source_target_pairs={{0,1},{1,2},{2,3},{3,4},{4,5},{5,6},{6,7},{7,8},{8,9},{9,10},{10,1... | collective-permute-start | bytes 1572872 | tf_op jit(solution)/shard_map/ppermute | solution.py:31
  89.2 31.0 %collective-permute-start.12 = (bf16[2,128,1024]{2,1,0:T(8,128)(2,1)S(1)}, bf16[2,128,1024]{2,1,0:T(8,128)(2,1)S(1)}, u32[]{:S(2)}, u32[]{:S(2)}) collective-permute-start(bf16[2,128,1024]{2,1,0:T(8,128)(2,1)S(1)} %get-tuple-element.28), channel_id=1, source_target_pairs={{0,15},{1,0},{2,1},{3,2},{4,3},{5,4},{6,5},{7,6},{8,7},{9,8},{10,9... | collective-permute-start | bytes 1572872 | tf_op jit(solution)/shard_map/ppermute | solution.py:31
  106.8 33.0 %collective-permute-start.4 = (bf16[528,1024]{1,0:T(8,128)(2,1)S(1)}, bf16[528,1024]{1,0:T(8,128)(2,1)S(1)}, u32[]{:S(2)}, u32[]{:S(2)}) collective-permute-start(bf16[528,1024]{1,0:T(8,128)(2,1)S(1)} %collective-permute-done.3.a_up_ref), channel_id=1, source_target_pairs={{0,1},{1,2},{2,3},{3,4},{4,5},{5,6},{6,7},{7,8},{8,9},{9,10},{10,1... | collective-permute-start | bytes 3244040 | tf_op jit(solution)/shard_map/ppermute | solution.py:26
  110.8 31.2 %collective-permute-start.6 = (bf16[528,1024]{1,0:T(8,128)(2,1)S(1)}, bf16[528,1024]{1,0:T(8,128)(2,1)S(1)}, u32[]{:S(2)}, u32[]{:S(2)}) collective-permute-start(bf16[528,1024]{1,0:T(8,128)(2,1)S(1)} %collective-permute-done.5.a_down_ref), channel_id=1, source_target_pairs={{1,0},{2,1},{3,2},{4,3},{5,4},{6,5},{7,6},{8,7},{9,8},{10,9},{11,1... | collective-permute-start | bytes 3244040 | tf_op jit(solution)/shard_map/ppermute | solution.py:26
  120.2 21.8 %copy-start = (bf16[1024,1024]{1,0:T(8,128)(2,1)S(1)}, bf16[1024,1024]{1,0:T(8,128)(2,1)}, u32[]{:S(2)}) copy-start(bf16[1024,1024]{1,0:T(8,128)(2,1)} %w_ref.7) | copy-start | bytes 6291460
  120.3 21.8 %copy-start.4 = (bf16[512,1024]{1,0:T(8,128)(2,1)S(1)}, bf16[512,1024]{1,0:T(8,128)(2,1)}, u32[]{:S(2)}) copy-start(bf16[512,1024]{1,0:T(8,128)(2,1)} %copy-done.3) | copy-start | bytes 3145732

commit v6 on v4

--- a/solution.py
+++ b/solution.py
@@ -365,7 +365,7 @@
         out_specs=pl.BlockSpec((1, 2 * width, row_dev), lambda i: (i, 0, 0)),
         out_shape=shape((feat_count, 2 * width, row_dev), bf16),
         cost_estimate=pl.CostEstimate(flops=100 * GIGA, bytes_accessed=1, transcendentals=0),
-        compiler_params=pltpu.CompilerParams(vmem_limit_bytes=56 * MIB),
+        compiler_params=pltpu.CompilerParams(vmem_limit_bytes=40 * MIB),
     )(src_one.T, features, adj_one, near_up)
     taken = lax.all_to_all(sent, "feat", 0, 0)
     swapped = lax.ppermute(halves, "feat", [(i, i ^ 1) for i in range(feat_count)])

time: 147 us -> 147 us (level)
  Pallas kernels: 44.1 us -> 41.1 us
  local copies, waits for them, and re-layouts: 6.85 us -> 9.65 us
    pallas_call x1, Pallas kernels: 8.39 us -> 5.47 us  [shards(): pl.pallas_call(gather_kernel, grid=(feat_count,), in_specs=[SMEM, pl.Bloc...]
    unnamed x36 -> x42, local copies, waits for them, and re-layouts: 6.85 us -> 9.65 us
  transfers between devices with their start and end apart: 15 -> 15, of which waited for: 7 -> 7; matrix products, arithmetic and copies ran while one was open for 0% -> 0% of each run, Pallas kernels for 23% -> 21%
where the time goes in v6:
time: 147 us; the launch traced here: 146 us
  waiting for transfers between devices  62.2 us (42%)
  Pallas kernels  41.1 us (28%)
  starting transfers between devices  32 us (22%)
  local copies, waits for them, and re-layouts  9.65 us (7%)
    ppermute x10, waiting for transfers between devices, shifted(): lax.ppermute(shard, 'dom', [(i, (i + by) % count) for i in range(count)])  24.7 us
    all_to_all x1, waiting for transfers between devices, shards(): taken = lax.all_to_all(sent, 'feat', 0, 0)  17.2 us
    ppermute x10, starting transfers between devices, shifted(): lax.ppermute(shard, 'dom', [(i, (i + by) % count) for i in range(count)])  17.1 us
    ppermute x2, waiting for transfers between devices, open_shift(): lax.ppermute(shard, 'dom', [(i, i + by) for i in range(count) if 0 <= i +...  16.7 us
    unnamed x42, local copies, waits for them, and re-layouts  9.65 us
    pallas_call x1, Pallas kernels, shards(): call(far_kernel, (shape((seeds, hid), bf16), shape((seeds, far_cols), bf1...  6.68 us
    ppermute x2, starting transfers between devices, open_shift(): lax.ppermute(shard, 'dom', [(i, i + by) for i in range(count) if 0 <= i +...  6.11 us
    pallas_call x1, Pallas kernels, shards(): pl.pallas_call(hidden_kernel, grid=(hid // chunk,), in_specs=[pl.BlockSpe...  5.6 us
  transfers between devices with their start and end apart: 15, of which 7 were waited for; matrix products, arithmetic and copies ran while one was open for 0% of the time, Pallas kernels for 21%

profile of v6, /device:TPU:104, one launch (start us, length us, event | category | flops | bytes accessed | tf_op | source)
XLA Modules:
  0.0 145.8 jit_solution(4857564781668107581)
XLA Ops:
  0.6 6.7 %shard_map.167 = (bf16[512,1024]{1,0:T(8,128)(2,1)}, bf16[512,1024]{1,0:T(8,128)(2,1)}, bf16[4,128,1024]{2,1,0:T(8,128)(2,1)}, bf16[4,128,1024]{2,1,0:T(8,128)(2,1)}) custom-call(bf16[4,16,128,128]{3,2,1,0:T(8,128)(2,1)} %bitcast.14, s32[4,16]{1,0:T(4,128)} %bitcast.21, bf16[512,1024]{1,0:T(8,128)(2,1)} %bitcast.16, bf16[1024,1024]{1,0:T(8,128)(2,1)} %w_ref.7), custom_call_target="tpu_custom_call" | custom-call | flops 1073741824 | bytes 1 | tf_op jit(solution)/shard_map/pallas_call | solution.py:322
  7.3 0.5 collective-permute-start.2
  7.8 3.7 %collective-permute-start.1 = (bf16[4,128,1024]{2,1,0:T(8,128)(2,1)}, bf16[4,128,1024]{2,1,0:T(8,128)(2,1)}, u32[]{:S(2)}, u32[]{:S(2)}) collective-permute-start(bf16[4,128,1024]{2,1,0:T(8,128)(2,1)} %get-tuple-element.20.after_ref), channel_id=1, source_target_pairs={{0,1},{1,2},{2,3},{3,4},{4,5},{5,6},{6,7},{7,8},{8,9},{9,10},{10,1... | collective-permute-start | bytes 3145736 | tf_op jit(solution)/shard_map/ppermute | solution.py:31
  11.5 2.3 %shard_map.170 = bf16[8,96,1024]{2,1,0:T(8,128)(2,1)} custom-call(bf16[96,1024]{1,0:T(8,128)(2,1)} %self_ref.1, bf16[96,1024]{1,0:T(8,128)(2,1)} %neigh_ref.1, bf16[4,128,1024]{2,1,0:T(8,128)(2,1)} %get-tuple-element.20.after_ref), custom_call_target="tpu_custom_call" | custom-call | flops 1073741824 | bytes 1 | tf_op jit(solution)/shard_map/pallas_call | solution.py:335
  13.8 0.0 copy-start.1
  13.8 0.0 copy-start.6
  13.8 4.5 %all-to-all-start.1 = ((bf16[8,96,1024]{2,1,0:T(8,128)(2,1)}), bf16[8,96,1024]{2,1,0:T(8,128)(2,1)}, u32[]{:S(2)}, u32[]{:S(2)}) async-start(bf16[8,96,1024]{2,1,0:T(8,128)(2,1)} %shard_map.170), calls=%async_computation.1 | async-start | bytes 3145728 | tf_op jit(solution)/shard_map/all_to_all | solution.py:343
  18.3 0.0 copy-done.11
  18.3 0.0 copy-done.1
  18.3 0.0 copy-done.6
  18.3 0.0 copy-start.10
  18.4 0.0 copy-start.14
  18.4 4.5 %shard_map.168 = (bf16[512,1792]{1,0:T(8,128)(2,1)S(1)}, bf16[4,128,1024]{2,1,0:T(8,128)(2,1)}, bf16[4,128,1024]{2,1,0:T(8,128)(2,1)}) custom-call(bf16[4,16,128,128]{3,2,1,0:T(8,128)(2,1)S(1)} %bitcast.15, s32[4,16]{1,0:T(4,128)S(1)} %bitcast.22, bf16[512,1024]{1,0:T(8,128)(2,1)S(1)} %copy-done.11), custom_call_target="tpu_custom_call" | custom-call | flops 1073741824 | bytes 1 | tf_op jit(solution)/shard_map/pallas_call | solution.py:348
  22.8 1.2 copy-done.16
  24.1 0.0 collective-permute-start.9
  24.1 4.1 %collective-permute-start.8 = (bf16[4,128,1024]{2,1,0:T(8,128)(2,1)}, bf16[4,128,1024]{2,1,0:T(8,128)(2,1)}, u32[]{:S(2)}, u32[]{:S(2)}) collective-permute-start(bf16[4,128,1024]{2,1,0:T(8,128)(2,1)} %get-tuple-element.19.after_ref), channel_id=1, source_target_pairs={{0,1},{1,2},{2,3},{3,4},{4,5},{5,6},{6,7},{7,8},{8,9},{9,10},{10,1... | collective-permute-start | bytes 3145736 | tf_op jit(solution)/shard_map/ppermute | solution.py:31
  28.2 0.0 copy-done.10
  28.2 0.0 copy-done.14
  28.2 2.8 %copy-done.7 = bf16[48,4,128,128]{3,2,1,0:T(8,128)(2,1)S(1)} copy-done((bf16[48,4,128,128]{3,2,1,0:T(8,128)(2,1)S(1)}, bf16[48,4,128,128]{3,2,1,0:T(8,128)(2,1)}, u32[]{:S(2)}) %copy-start.7) | copy-done | bytes 6291480
  31.0 5.5 %shard_map.169 = bf16[8,192,768]{2,1,0:T(8,128)(2,1)} custom-call(s32[4,48]{1,0:T(4,128)S(1)} %bitcast.24, bf16[96,6144]{1,0:T(8,128)(2,1)S(1)} %copy-done.10, bf16[48,4,128,128]{3,2,1,0:T(8,128)(2,1)S(1)} %copy-done.7, bf16[4,128,1024]{2,1,0:T(8,128)(2,1)} %get-tuple-element.19.after_ref), custom_call_target="tpu_custom_call" | custom-call | flops 107374182400 | bytes 1 | tf_op jit(solution)/shard_map/pallas_call | solution.py:356
  36.5 3.5 %all-to-all-done.1 = bf16[8,96,1024]{2,1,0:T(8,128)(2,1)} async-done(((bf16[8,96,1024]{2,1,0:T(8,128)(2,1)}), bf16[8,96,1024]{2,1,0:T(8,128)(2,1)}, u32[]{:S(2)}, u32[]{:S(2)}) %all-to-all-start.1) | async-done | bytes 1572896 | tf_op jit(solution)/shard_map/all_to_all | solution.py:343
  40.0 4.4 %all-to-all-start = ((bf16[8,192,768]{2,1,0:T(8,128)(2,1)}), bf16[8,192,768]{2,1,0:T(8,128)(2,1)}, u32[]{:S(2)}, u32[]{:S(2)}) async-start(bf16[8,192,768]{2,1,0:T(8,128)(2,1)} %shard_map.169), calls=%async_computation | async-start | bytes 4718592 | tf_op jit(solution)/shard_map/all_to_all | solution.py:370
  44.4 0.0 copy-done.19
  44.4 0.0 copy-done.20
  44.4 0.0 collective-permute-done.2.after_down_ref
  44.4 0.1 collective-permute-start.10
  44.5 0.0 collective-permute-done.1.after_up_ref
  44.5 4.1 %collective-permute-start.7 = (bf16[4,128,1024]{2,1,0:T(8,128)(2,1)}, bf16[4,128,1024]{2,1,0:T(8,128)(2,1)}, u32[]{:S(2)}, u32[]{:S(2)}) collective-permute-start(bf16[4,128,1024]{2,1,0:T(8,128)(2,1)} %collective-permute-done.1.after_up_ref), channel_id=1, source_target_pairs={{0,1},{1,2},{2,3},{3,4},{4,5},{5,6},{6,7},{7,8},{8,9},{9,10},{10,1... | collective-permute-start | bytes 3145736 | tf_op jit(solution)/shard_map/ppermute | solution.py:31
  48.6 0.0 collective-permute-start
  48.6 0.0 copy-done.15
  48.6 1.2 copy-done.2
  49.9 1.6 %copy-done.8 = bf16[1024,1024]{1,0:T(8,128)(2,1)S(1)} copy-done((bf16[1024,1024]{1,0:T(8,128)(2,1)S(1)}, bf16[1024,1024]{1,0:T(8,128)(2,1)}, u32[]{:S(2)}) %copy-start.8) | copy-done | bytes 2097176
  51.5 1.2 copy-done.12
  52.7 1.5 %copy-done.17 = bf16[512,1792]{1,0:T(8,128)(2,1)S(1)} copy-done((bf16[512,1792]{1,0:T(8,128)(2,1)S(1)}, bf16[512,1792]{1,0:T(8,128)(2,1)}, u32[]{:S(2)}) %copy-start.17) | copy-done | bytes 1835032
  54.2 2.9 %shard_map.171.after_ref.local_ref = f32[768,1024]{1,0:T(8,128)S(1)} custom-call(bf16[512,1792]{1,0:T(8,128)(2,1)S(1)} %copy-done.17, bf16[512,1024]{1,0:T(8,128)(2,1)S(1)} %copy-done.12, bf16[512,1024]{1,0:T(8,128)(2,1)S(1)} %bitcast.17, bf16[1024,1024]{1,0:T(8,128)(2,1)S(1)} %copy-done.8, s32[1,512]{1,0:T(1,128)S(1)} %bitcast.25, ...), custom_call_target="tpu_custom_call" | custom-call | flops 21474836480 | bytes 1 | tf_op jit(solution)/shard_map/pallas_call | solution.py:379
  57.1 17.2 %all-to-all-done.in_ref = bf16[8,192,768]{2,1,0:T(8,128)(2,1)} async-done(((bf16[8,192,768]{2,1,0:T(8,128)(2,1)}), bf16[8,192,768]{2,1,0:T(8,128)(2,1)}, u32[]{:S(2)}, u32[]{:S(2)}) %all-to-all-start) | async-done | bytes 2359328 | tf_op jit(solution)/shard_map/all_to_all | solution.py:370
  74.4 0.0 collective-permute-done.other_ref
  74.4 0.0 copy-done.4
  74.4 0.0 copy-done.5
  74.4 5.6 %shard_map.172 = (bf16[6,128,1024]{2,1,0:T(8,128)(2,1)S(1)}, bf16[528,1024]{1,0:T(8,128)(2,1)S(1)}, bf16[528,1024]{1,0:T(8,128)(2,1)S(1)}) custom-call(bf16[8,192,768]{2,1,0:T(8,128)(2,1)} %all-to-all-done.in_ref, bf16[768,1024]{1,0:T(8,128)(2,1)} %bitcast.4.mine_ref, bf16[768,1024]{1,0:T(8,128)(2,1)} %collective-permute-done.other_ref, ...), custom_call_target="tpu_custom_call" | custom-call | flops 1073741824 | bytes 1 | tf_op jit(solution)/shard_map/pallas_call | solution.py:388
  80.0 0.1 collective-permute-start.3
  80.1 0.0 collective-permute-done.9.from_2_ref
  80.1 2.0 %collective-permute-start.5 = (bf16[528,1024]{1,0:T(8,128)(2,1)S(1)}, bf16[528,1024]{1,0:T(8,128)(2,1)S(1)}, u32[]{:S(2)}, u32[]{:S(2)}) collective-permute-start(bf16[528,1024]{1,0:T(8,128)(2,1)S(1)} %get-tuple-element.24), channel_id=1, source_target_pairs={{0,15},{1,0},{2,1},{3,2},{4,3},{5,4},{6,5},{7,6},{8,7},{9,8},{10,9... | collective-permute-start | bytes 3244040 | tf_op jit(solution)/shard_map/ppermute | solution.py:31
  82.1 0.0 collective-permute-done.8.from_1_ref
  82.1 0.0 collective-permute-done.10.from_3_ref
  82.1 0.0 collective-permute-done.7.from_0_ref
  82.1 0.0 copy-start.9
  82.1 0.0 copy-start.13
  82.1 0.0 copy-start.18
  82.1 4.9 %shard_map.173 = (f32[768,1024]{1,0:T(8,128)}, bf16[2,128,1024]{2,1,0:T(8,128)(2,1)S(1)}, bf16[2,128,1024]{2,1,0:T(8,128)(2,1)S(1)}) custom-call(f32[768,1024]{1,0:T(8,128)S(1)} %shard_map.171.after_ref.local_ref, bf16[4,128,1024]{2,1,0:T(8,128)(2,1)} %collective-permute-done.7.from_0_ref, bf16[4,128,1024]{2,1,0:T(8,128)(2,1)} %collective-permute-done.8.from_1_ref, ...), custom_call_target="tpu_custom_call" | custom-call | flops 1073741824 | bytes 1 | tf_op jit(solution)/shard_map/pallas_call | solution.py:417
  87.0 2.4 %collective-permute-start.11 = (bf16[2,128,1024]{2,1,0:T(8,128)(2,1)S(1)}, bf16[2,128,1024]{2,1,0:T(8,128)(2,1)S(1)}, u32[]{:S(2)}, u32[]{:S(2)}) collective-permute-start(bf16[2,128,1024]{2,1,0:T(8,128)(2,1)S(1)} %get-tuple-element.27), channel_id=1, source_target_pairs={{0,1},{1,2},{2,3},{3,4},{4,5},{5,6},{6,7},{7,8},{8,9},{9,10},{10,1... | collective-permute-start | bytes 1572872 | tf_op jit(solution)/shard_map/ppermute | solution.py:31
  89.4 0.0 collective-permute-start.12
  89.4 17.4 %collective-permute-done.3.a_up_ref = bf16[528,1024]{1,0:T(8,128)(2,1)S(1)} collective-permute-done((bf16[528,1024]{1,0:T(8,128)(2,1)S(1)}, bf16[528,1024]{1,0:T(8,128)(2,1)S(1)}, u32[]{:S(2)}, u32[]{:S(2)}) %collective-permute-start.3) | collective-permute-done | bytes 1081376 | tf_op jit(solution)/shard_map/ppermute | solution.py:31
  106.8 4.0 %collective-permute-start.4 = (bf16[528,1024]{1,0:T(8,128)(2,1)S(1)}, bf16[528,1024]{1,0:T(8,128)(2,1)S(1)}, u32[]{:S(2)}, u32[]{:S(2)}) collective-permute-start(bf16[528,1024]{1,0:T(8,128)(2,1)S(1)} %collective-permute-done.3.a_up_ref), channel_id=1, source_target_pairs={{0,1},{1,2},{2,3},{3,4},{4,5},{5,6},{6,7},{7,8},{8,9},{9,10},{10,1... | collective-permute-start | bytes 3244040 | tf_op jit(solution)/shard_map/ppermute | solution.py:26
  110.8 0.0 collective-permute-done.5.a_down_ref
  110.8 2.1 %collective-permute-start.6 = (bf16[528,1024]{1,0:T(8,128)(2,1)S(1)}, bf16[528,1024]{1,0:T(8,128)(2,1)S(1)}, u32[]{:S(2)}, u32[]{:S(2)}) collective-permute-start(bf16[528,1024]{1,0:T(8,128)(2,1)S(1)} %collective-permute-done.5.a_down_ref), channel_id=1, source_target_pairs={{1,0},{2,1},{3,2},{4,3},{5,4},{6,5},{7,6},{8,7},{9,8},{10,9},{11,1... | collective-permute-start | bytes 3244040 | tf_op jit(solution)/shard_map/ppermute | solution.py:26
  113.0 5.1 %collective-permute-done.11.rest_up_ref = bf16[2,128,1024]{2,1,0:T(8,128)(2,1)S(1)} collective-permute-done((bf16[2,128,1024]{2,1,0:T(8,128)(2,1)S(1)}, bf16[2,128,1024]{2,1,0:T(8,128)(2,1)S(1)}, u32[]{:S(2)}, u32[]{:S(2)}) %collective-permute-start.11) | collective-permute-done | bytes 524320 | tf_op jit(solution)/shard_map/ppermute | solution.py:31
  118.1 2.2 %collective-permute-done.12.rest_down_ref = bf16[2,128,1024]{2,1,0:T(8,128)(2,1)S(1)} collective-permute-done((bf16[2,128,1024]{2,1,0:T(8,128)(2,1)S(1)}, bf16[2,128,1024]{2,1,0:T(8,128)(2,1)S(1)}, u32[]{:S(2)}, u32[]{:S(2)}) %collective-permute-start.12) | collective-permute-done | bytes 524320 | tf_op jit(solution)/shard_map/ppermute | solution.py:31
  120.3 0.0 copy-done.9
  120.3 0.0 copy-start
  120.3 5.1 %shard_map.174 = (f32[512,1024]{1,0:T(8,128)S(1)}, f32[512,1024]{1,0:T(8,128)S(1)}) custom-call(bf16[512,1792]{1,0:T(8,128)(2,1)S(1)} %copy-done.18, bf16[6,128,1024]{2,1,0:T(8,128)(2,1)S(1)} %get-tuple-element.25.hid_ref, bf16[528,1024]{1,0:T(8,128)(2,1)S(1)} %collective-permute-done.3.a_up_ref, ...), custom_call_target="tpu_custom_call" | custom-call | flops 107374182400 | bytes 1 | tf_op jit(solution)/shard_map/pallas_call | solution.py:423
  125.4 14.5 %collective-permute-done.4.f_up_ref = bf16[528,1024]{1,0:T(8,128)(2,1)S(1)} collective-permute-done((bf16[528,1024]{1,0:T(8,128)(2,1)S(1)}, bf16[528,1024]{1,0:T(8,128)(2,1)S(1)}, u32[]{:S(2)}, u32[]{:S(2)}) %collective-permute-start.4) | collective-permute-done | bytes 1081376 | tf_op jit(solution)/shard_map/ppermute | solution.py:26
  139.9 2.2 %collective-permute-done.6.f_down_ref = bf16[528,1024]{1,0:T(8,128)(2,1)S(1)} collective-permute-done((bf16[528,1024]{1,0:T(8,128)(2,1)S(1)}, bf16[528,1024]{1,0:T(8,128)(2,1)S(1)}, u32[]{:S(2)}, u32[]{:S(2)}) %collective-permute-start.6) | collective-permute-done | bytes 1081376 | tf_op jit(solution)/shard_map/ppermute | solution.py:26
  142.1 3.7 %shard_map.175 = bf16[512,1024]{1,0:T(8,128)(2,1)} custom-call(bf16[512,1024]{1,0:T(8,128)(2,1)S(1)} %copy-done.3, bf16[528,1024]{1,0:T(8,128)(2,1)S(1)} %collective-permute-done.4.f_up_ref, bf16[528,1024]{1,0:T(8,128)(2,1)S(1)} %collective-permute-done.6.f_down_ref, f32[512,1024]{1,0:T(8,128)S(1)} %get-tuple-element.29.part_ref, ...), custom_call_target="tpu_custom_call" | custom-call | flops 1073741824 | bytes 1 | tf_op jit(solution)/shard_map/pallas_call | solution.py:434
  (18 shorter events, 0.0 us)
Async XLA Ops:
  7.3 37.1 %collective-permute-start.2 = (bf16[4,128,1024]{2,1,0:T(8,128)(2,1)}, bf16[4,128,1024]{2,1,0:T(8,128)(2,1)}, u32[]{:S(2)}, u32[]{:S(2)}) collective-permute-start(bf16[4,128,1024]{2,1,0:T(8,128)(2,1)} %get-tuple-element.22), channel_id=1, source_target_pairs={{0,15},{1,0},{2,1},{3,2},{4,3},{5,4},{6,5},{7,6},{8,7},{9,8},{10,9... | collective-permute-start | bytes 3145736 | tf_op jit(solution)/shard_map/ppermute | solution.py:31
  7.8 36.7 %collective-permute-start.1 = (bf16[4,128,1024]{2,1,0:T(8,128)(2,1)}, bf16[4,128,1024]{2,1,0:T(8,128)(2,1)}, u32[]{:S(2)}, u32[]{:S(2)}) collective-permute-start(bf16[4,128,1024]{2,1,0:T(8,128)(2,1)} %get-tuple-element.20.after_ref), channel_id=1, source_target_pairs={{0,1},{1,2},{2,3},{3,4},{4,5},{5,6},{6,7},{7,8},{8,9},{9,10},{10,1... | collective-permute-start | bytes 3145736 | tf_op jit(solution)/shard_map/ppermute | solution.py:31
  11.5 6.8 %copy-start.11 = (bf16[512,1024]{1,0:T(8,128)(2,1)S(1)}, bf16[512,1024]{1,0:T(8,128)(2,1)}, u32[]{:S(2)}) copy-start(bf16[512,1024]{1,0:T(8,128)(2,1)} %get-tuple-element.18.back_ref) | copy-start | bytes 3145732
  13.8 4.5 %copy-start.1 = (bf16[1,1,4,16,128,128]{5,4,3,2,1,0:T(8,128)(2,1)S(1)}, bf16[1,1,4,16,128,128]{5,4,3,2,1,0:T(8,128)(2,1)}, u32[]{:S(2)}) copy-start(bf16[1,1,4,16,128,128]{5,4,3,2,1,0:T(8,128)(2,1)} %param.26) | copy-start | bytes 6291460
  13.8 4.5 %copy-start.6 = (s32[1,1,4,16]{3,2,1,0:T(4,128)S(1)}, s32[1,1,4,16]{3,2,1,0:T(4,128)}, u32[]{:S(2)}) copy-start(s32[1,1,4,16]{3,2,1,0:T(4,128)} %param.27) | copy-start | bytes 772
  13.8 26.1 %all-to-all-start.1 = ((bf16[8,96,1024]{2,1,0:T(8,128)(2,1)}), bf16[8,96,1024]{2,1,0:T(8,128)(2,1)}, u32[]{:S(2)}, u32[]{:S(2)}) async-start(bf16[8,96,1024]{2,1,0:T(8,128)(2,1)} %shard_map.170), calls=%async_computation.1 | async-start | bytes 3145728 | tf_op jit(solution)/shard_map/all_to_all | solution.py:343
  18.3 9.9 %copy-start.10 = (bf16[96,6144]{1,0:T(8,128)(2,1)S(1)}, bf16[96,6144]{1,0:T(8,128)(2,1)}, u32[]{:S(2)}) copy-start(bf16[96,6144]{1,0:T(8,128)(2,1)} %feat_ref.1) | copy-start | bytes 3538948
  18.4 9.9 %copy-start.14 = (s32[48,4]{0,1:T(4,128)S(1)}, s32[48,4]{0,1:T(4,128)}, u32[]{:S(2)}) copy-start(s32[48,4]{0,1:T(4,128)} %param.18) | copy-start | bytes 2308
  22.8 1.3 copy-start.16
  24.1 56.0 %collective-permute-start.9 = (bf16[4,128,1024]{2,1,0:T(8,128)(2,1)}, bf16[4,128,1024]{2,1,0:T(8,128)(2,1)}, u32[]{:S(2)}, u32[]{:S(2)}) collective-permute-start(bf16[4,128,1024]{2,1,0:T(8,128)(2,1)} %get-tuple-element.26), channel_id=1, source_target_pairs={{0,15},{1,0},{2,1},{3,2},{4,3},{5,4},{6,5},{7,6},{8,7},{9,8},{10,9... | collective-permute-start | bytes 3145736 | tf_op jit(solution)/shard_map/ppermute | solution.py:31
  24.1 58.0 %collective-permute-start.8 = (bf16[4,128,1024]{2,1,0:T(8,128)(2,1)}, bf16[4,128,1024]{2,1,0:T(8,128)(2,1)}, u32[]{:S(2)}, u32[]{:S(2)}) collective-permute-start(bf16[4,128,1024]{2,1,0:T(8,128)(2,1)} %get-tuple-element.19.after_ref), channel_id=1, source_target_pairs={{0,1},{1,2},{2,3},{3,4},{4,5},{5,6},{6,7},{7,8},{8,9},{9,10},{10,1... | collective-permute-start | bytes 3145736 | tf_op jit(solution)/shard_map/ppermute | solution.py:31
  28.2 2.8 %copy-start.7 = (bf16[48,4,128,128]{3,2,1,0:T(8,128)(2,1)S(1)}, bf16[48,4,128,128]{3,2,1,0:T(8,128)(2,1)}, u32[]{:S(2)}) copy-start(bf16[48,4,128,128]{3,2,1,0:T(8,128)(2,1)} %adj_ref.1) | copy-start | bytes 18874372
  36.5 7.9 %copy-start.19 = (s32[1,1,4]{2,1,0:T(1,128)S(1)}, s32[1,1,4]{2,1,0:T(1,128)}, u32[]{:S(2)}) copy-start(s32[1,1,4]{2,1,0:T(1,128)} %param.29) | copy-start | bytes 52
  36.5 7.9 %copy-start.20 = (s32[4]{0:T(128)S(1)}, s32[4]{0:T(128)}, u32[]{:S(2)}) copy-start(s32[4]{0:T(128)} %constant.28.clone) | copy-start | bytes 52
  36.5 12.2 %copy-start.15 = (s32[1,1,512]{2,1,0:T(1,128)S(1)}, s32[1,1,512]{2,1,0:T(1,128)}, u32[]{:S(2)}) copy-start(s32[1,1,512]{2,1,0:T(1,128)} %param.25) | copy-start | bytes 6148
  40.0 34.4 %all-to-all-start = ((bf16[8,192,768]{2,1,0:T(8,128)(2,1)}), bf16[8,192,768]{2,1,0:T(8,128)(2,1)}, u32[]{:S(2)}, u32[]{:S(2)}) async-start(bf16[8,192,768]{2,1,0:T(8,128)(2,1)} %shard_map.169), calls=%async_computation | async-start | bytes 4718592 | tf_op jit(solution)/shard_map/all_to_all | solution.py:370
  44.4 37.7 %collective-permute-start.10 = (bf16[4,128,1024]{2,1,0:T(8,128)(2,1)}, bf16[4,128,1024]{2,1,0:T(8,128)(2,1)}, u32[]{:S(2)}, u32[]{:S(2)}) collective-permute-start(bf16[4,128,1024]{2,1,0:T(8,128)(2,1)} %collective-permute-done.2.after_down_ref), channel_id=1, source_target_pairs={{0,15},{1,0},{2,1},{3,2},{4,3},{5,4},{6,5},{7,6},{8,7},{9,8},{10,9... | collective-permute-start | bytes 3145736 | tf_op jit(solution)/shard_map/ppermute | solution.py:31
  44.5 37.6 %collective-permute-start.7 = (bf16[4,128,1024]{2,1,0:T(8,128)(2,1)}, bf16[4,128,1024]{2,1,0:T(8,128)(2,1)}, u32[]{:S(2)}, u32[]{:S(2)}) collective-permute-start(bf16[4,128,1024]{2,1,0:T(8,128)(2,1)} %collective-permute-done.1.after_up_ref), channel_id=1, source_target_pairs={{0,1},{1,2},{2,3},{3,4},{4,5},{5,6},{6,7},{7,8},{8,9},{9,10},{10,1... | collective-permute-start | bytes 3145736 | tf_op jit(solution)/shard_map/ppermute | solution.py:31
  48.6 25.7 %collective-permute-start = (bf16[768,1024]{1,0:T(8,128)(2,1)}, bf16[768,1024]{1,0:T(8,128)(2,1)}, u32[]{:S(2)}, u32[]{:S(2)}) collective-permute-start(bf16[768,1024]{1,0:T(8,128)(2,1)} %bitcast.4.mine_ref), channel_id=1, source_target_pairs={{0,16},{16,0},{32,48},{48,32},{64,80},{80,64},{96,112},{112,96},{1... | collective-permute-start | bytes 4718600 | tf_op jit(solution)/shard_map/ppermute | solution.py:371
  48.6 1.2 copy-start.2
  49.9 1.6 %copy-start.8 = (bf16[1024,1024]{1,0:T(8,128)(2,1)S(1)}, bf16[1024,1024]{1,0:T(8,128)(2,1)}, u32[]{:S(2)}) copy-start(bf16[1024,1024]{1,0:T(8,128)(2,1)} %w_ref.6) | copy-start | bytes 6291460
  51.5 1.2 copy-start.12
  52.7 1.5 %copy-start.17 = (bf16[512,1792]{1,0:T(8,128)(2,1)S(1)}, bf16[512,1792]{1,0:T(8,128)(2,1)}, u32[]{:S(2)}) copy-start(bf16[512,1792]{1,0:T(8,128)(2,1)} %copy-done.16) | copy-start | bytes 5505028
  54.2 20.2 %copy-start.4 = (s32[1,1,4,4]{3,2,1,0:T(4,128)S(1)}, s32[1,1,4,4]{3,2,1,0:T(4,128)}, u32[]{:S(2)}) copy-start(s32[1,1,4,4]{3,2,1,0:T(4,128)} %param.28) | copy-start | bytes 196
  54.2 20.2 %copy-start.5 = (f32[1024]{0:T(1024)S(1)}, f32[1024]{0:T(1024)}, u32[]{:S(2)}) copy-start(f32[1024]{0:T(1024)} %param.21) | copy-start | bytes 12292
  80.0 26.8 %collective-permute-start.3 = (bf16[528,1024]{1,0:T(8,128)(2,1)S(1)}, bf16[528,1024]{1,0:T(8,128)(2,1)S(1)}, u32[]{:S(2)}, u32[]{:S(2)}) collective-permute-start(bf16[528,1024]{1,0:T(8,128)(2,1)S(1)} %get-tuple-element.23), channel_id=1, source_target_pairs={{0,1},{1,2},{2,3},{3,4},{4,5},{5,6},{6,7},{7,8},{8,9},{9,10},{10,1... | collective-permute-start | bytes 3244040 | tf_op jit(solution)/shard_map/ppermute | solution.py:31
  80.1 30.7 %collective-permute-start.5 = (bf16[528,1024]{1,0:T(8,128)(2,1)S(1)}, bf16[528,1024]{1,0:T(8,128)(2,1)S(1)}, u32[]{:S(2)}, u32[]{:S(2)}) collective-permute-start(bf16[528,1024]{1,0:T(8,128)(2,1)S(1)} %get-tuple-element.24), channel_id=1, source_target_pairs={{0,15},{1,0},{2,1},{3,2},{4,3},{5,4},{6,5},{7,6},{8,7},{9,8},{10,9... | collective-permute-start | bytes 3244040 | tf_op jit(solution)/shard_map/ppermute | solution.py:31
  82.1 38.2 %copy-start.9 = (bf16[1024,1024]{1,0:T(8,128)(2,1)S(1)}, bf16[1024,1024]{1,0:T(8,128)(2,1)}, u32[]{:S(2)}) copy-start(bf16[1024,1024]{1,0:T(8,128)(2,1)} %w_ref.6) | copy-start | bytes 6291460
  82.1 38.2 %copy-start.13 = (f32[1024]{0:T(1024)S(1)}, f32[1024]{0:T(1024)}, u32[]{:S(2)}) copy-start(f32[1024]{0:T(1024)} %param.24) | copy-start | bytes 12292
  82.1 38.2 %copy-start.18 = (bf16[512,1792]{1,0:T(8,128)(2,1)S(1)}, bf16[512,1792]{1,0:T(8,128)(2,1)}, u32[]{:S(2)}) copy-start(bf16[512,1792]{1,0:T(8,128)(2,1)} %copy-done.16) | copy-start | bytes 5505028
  87.0 31.1 %collective-permute-start.11 = (bf16[2,128,1024]{2,1,0:T(8,128)(2,1)S(1)}, bf16[2,128,1024]{2,1,0:T(8,128)(2,1)S(1)}, u32[]{:S(2)}, u32[]{:S(2)}) collective-permute-start(bf16[2,128,1024]{2,1,0:T(8,128)(2,1)S(1)} %get-tuple-element.27), channel_id=1, source_target_pairs={{0,1},{1,2},{2,3},{3,4},{4,5},{5,6},{6,7},{7,8},{8,9},{9,10},{10,1... | collective-permute-start | bytes 1572872 | tf_op jit(solution)/shard_map/ppermute | solution.py:31
  89.4 30.8 %collective-permute-start.12 = (bf16[2,128,1024]{2,1,0:T(8,128)(2,1)S(1)}, bf16[2,128,1024]{2,1,0:T(8,128)(2,1)S(1)}, u32[]{:S(2)}, u32[]{:S(2)}) collective-permute-start(bf16[2,128,1024]{2,1,0:T(8,128)(2,1)S(1)} %get-tuple-element.28), channel_id=1, source_target_pairs={{0,15},{1,0},{2,1},{3,2},{4,3},{5,4},{6,5},{7,6},{8,7},{9,8},{10,9... | collective-permute-start | bytes 1572872 | tf_op jit(solution)/shard_map/ppermute | solution.py:31
  106.8 33.0 %collective-permute-start.4 = (bf16[528,1024]{1,0:T(8,128)(2,1)S(1)}, bf16[528,1024]{1,0:T(8,128)(2,1)S(1)}, u32[]{:S(2)}, u32[]{:S(2)}) collective-permute-start(bf16[528,1024]{1,0:T(8,128)(2,1)S(1)} %collective-permute-done.3.a_up_ref), channel_id=1, source_target_pairs={{0,1},{1,2},{2,3},{3,4},{4,5},{5,6},{6,7},{7,8},{8,9},{9,10},{10,1... | collective-permute-start | bytes 3244040 | tf_op jit(solution)/shard_map/ppermute | solution.py:26
  110.8 31.2 %collective-permute-start.6 = (bf16[528,1024]{1,0:T(8,128)(2,1)S(1)}, bf16[528,1024]{1,0:T(8,128)(2,1)S(1)}, u32[]{:S(2)}, u32[]{:S(2)}) collective-permute-start(bf16[528,1024]{1,0:T(8,128)(2,1)S(1)} %collective-permute-done.5.a_down_ref), channel_id=1, source_target_pairs={{1,0},{2,1},{3,2},{4,3},{5,4},{6,5},{7,6},{8,7},{9,8},{10,9},{11,1... | collective-permute-start | bytes 3244040 | tf_op jit(solution)/shard_map/ppermute | solution.py:26
  120.3 21.8 %copy-start = (bf16[1024,1024]{1,0:T(8,128)(2,1)S(1)}, bf16[1024,1024]{1,0:T(8,128)(2,1)}, u32[]{:S(2)}) copy-start(bf16[1024,1024]{1,0:T(8,128)(2,1)} %w_ref.7) | copy-start | bytes 6291460
  120.3 21.8 %copy-start.3 = (bf16[512,1024]{1,0:T(8,128)(2,1)S(1)}, bf16[512,1024]{1,0:T(8,128)(2,1)}, u32[]{:S(2)}) copy-start(bf16[512,1024]{1,0:T(8,128)(2,1)} %get-tuple-element.17.fold_ref) | copy-start | bytes 3145732
